TPU v7x, 256 devices: a whole 4x4x8 slice. The times are simulated.
256 devices in a mesh: member: 16 (over y, z_lo), space: 16 (over x, z_hi, core).
Axes of the slice: x: 4, y: 4, z: 8 (z_hi: 2, z_lo: 4; z = z_hi * 4 + z_lo), core: 2. Of those that a mesh axis runs over, the one named last changes fastest.
Arguments:
- background: bfloat16 [64, 4, 6, 16, 8192], P('member', None, None, 'space'), may hold values from -6 to 6
- obs_values: float32 [16, 8, 128], P('space'), may hold values from -6 to 6
- obs_precision: float32 [16, 8, 128], P('space'), may hold values from 0.25 to 4
- obs_cell: int32 [16, 8, 128], P('space'), may hold values from 0 to 24575
- obs_count: int32 [16, 8], P('space'), may hold values from 32 to 128, as said below
- radius: int32 [16, 8], P('space'), may hold values from 32 to 64
Outputs:
- analysis: bfloat16 [64, 4, 6, 16, 8192], P('member', None, None, 'space')
Inputs may be any that keep to these rules, and one draw needn't show every extreme that they name: `obs_count`: slots at or past a tile's count are unused; in every draw some tile uses all 128 slots.
All inputs are finite; a program needn't handle non-finite values.
Results may differ from a plain program's by a relative error of at most 0.0049.
Values may be sent and summed in bfloat16 or wider, within the bound.
No kernel may reach another device: no remote copies, remote signals or barrier semaphores. Data moves between devices by JAX's collectives and lax.ppermute only.
A program may use at most 192 MiB of HBM per device.

v0:
```python
import jax
import jax.numpy as jnp
from jax import lax
from jax.sharding import PartitionSpec as P

TILE_SIDE = 32
TILE_CELLS = 1024
SWEEPS = 6


exact_mode = lax.Precision.HIGHEST


def with_halo(array, sides, width):
    for axis, dim in sides:
        devices, length = (lax.axis_size(axis), array.shape[dim])
        up = [(i, (i + 1) % devices) for i in range(devices - 1)]
        down = [(j, i) for i, j in up]
        last = lax.slice_in_dim(array, length - width, length, axis=dim)
        initial = lax.slice_in_dim(array, 0, width, axis=dim)
        before = lax.ppermute(last, axis, up)
        after = lax.ppermute(initial, axis, down)
        array = jnp.concatenate([before, array, after], axis=dim)
    return array


def observe(fields, obs_cell, cell_count):
    members = fields.shape[0]
    row_count = fields.shape[3]
    row_width = fields.shape[4]
    level_field = obs_cell // cell_count
    in_tile = obs_cell % cell_count
    row_index = jnp.arange(row_count, dtype=jnp.int32)[:, None, None]
    col_index = jnp.arange(row_width // cell_count, dtype=jnp.int32)[None, :, None]
    flat_index = (
        (level_field * row_count + row_index) * row_width + col_index * cell_count + in_tile
    )
    gathered = jnp.take(fields.reshape(members, -1), flat_index.reshape(-1), axis=1)
    return gathered.reshape(members, row_count, row_width // cell_count, -1)


def observation_rows(obs_values, obs_precision, obs_cell, obs_count, cell_count, tile_side):
    slot_count = obs_cell.shape[-1]
    slot_index = jnp.arange(slot_count, dtype=jnp.int32)
    active = jnp.where(
        slot_index[None, None, :] < obs_count[:, :, None],
        obs_precision,
        jnp.zeros_like(obs_precision),
    )
    in_tile = obs_cell % cell_count
    row_place = (in_tile // tile_side).astype(obs_values.dtype)
    col_place = (in_tile % tile_side).astype(obs_values.dtype)
    return jnp.stack([obs_values, active, row_place, col_place])


def neighbourhood(obs_rows, tile_side):
    row_count = obs_rows.shape[1] - 2
    col_count = obs_rows.shape[2]
    slot_count = obs_rows.shape[3]
    padded = jnp.pad(obs_rows, ((0, 0), (0, 0), (1, 1), (0, 0)))
    pieces = []
    shift_rows = []
    shift_cols = []
    for row_step in range(3):
        for col_step in range(3):
            pieces.append(
                padded[:, row_step : row_step + row_count, col_step : col_step + col_count, :]
            )
            shift_rows.append(jnp.full((slot_count,), (row_step - 1) * tile_side, obs_rows.dtype))
            shift_cols.append(jnp.full((slot_count,), (col_step - 1) * tile_side, obs_rows.dtype))
    stacked = jnp.concatenate(pieces, axis=3)
    offset_row = jnp.concatenate(shift_rows)
    offset_col = jnp.concatenate(shift_cols)
    return (stacked, offset_row, offset_col)


def solve_tiles(stacked, offset_row, offset_col, radius, members, tile_side, sweeps):
    ensemble = stacked[:members]
    values = stacked[members]
    active = stacked[members + 1]
    centre = 0.5 * tile_side - 0.5
    dist_row = offset_row + stacked[members + 2] - centre
    dist_col = offset_col + stacked[members + 3] - centre
    reach_cells = radius.astype(stacked.dtype)[:, :, None]
    tapered = (
        jnp.maximum(
            1.0 - (dist_row * dist_row + dist_col * dist_col) / (reach_cells * reach_cells), 0.0
        )
        ** 2
    )
    weight = active * tapered
    mean_obs = jnp.mean(ensemble, axis=0)
    anomaly = ensemble - mean_obs
    scaled = anomaly * weight
    innovation = values - mean_obs
    identity = jnp.eye(members, dtype=stacked.dtype)
    system = (members - 1.0) * identity + jnp.einsum(
        "krtm,jrtm->rtkj", scaled, anomaly, precision=exact_mode
    )
    forcing = jnp.einsum("krtm,rtm->rtk", scaled, innovation, precision=exact_mode)
    scale = jnp.trace(system, axis1=2, axis2=3)[:, :, None, None]
    root_part = system / scale
    inverse = jnp.broadcast_to(identity, system.shape)
    for sweep_index in range(sweeps):
        factor = 0.5 * (
            3.0 * identity - jnp.einsum("rtij,rtjk->rtik", inverse, root_part, precision=exact_mode)
        )
        root_part = jnp.einsum("rtij,rtjk->rtik", root_part, factor, precision=exact_mode)
        inverse = jnp.einsum("rtij,rtjk->rtik", factor, inverse, precision=exact_mode)
    inv_sqrt = inverse / jnp.sqrt(scale)
    covariance = jnp.einsum("rtij,rtjk->rtik", inv_sqrt, inv_sqrt, precision=exact_mode)
    mean_weight = jnp.einsum("rtkj,rtj->rtk", covariance, forcing, precision=exact_mode)
    total = jnp.sqrt(members - 1.0) * inv_sqrt + mean_weight[:, :, :, None]
    mixing = total - jnp.mean(total, axis=2, keepdims=True) + 1.0 / members
    return mixing.astype(jnp.bfloat16)


def make_accumulate(own_mixing, col_count, running, piece):
    piece_count = piece.shape[0]
    chosen = lax.slice_in_dim(own_mixing, 0, piece_count, axis=2)
    shaped = piece.reshape(piece.shape[:4] + (col_count, TILE_CELLS))
    return running + jnp.einsum(
        "jlfrtc,rtjk->klfrtc", shaped, chosen, preferred_element_type=jnp.float32
    )


def on_device(background, obs_values, obs_precision, obs_cell, obs_count, radius):
    own_members = background.shape[0]
    predicted = observe(background, obs_cell, TILE_CELLS)
    extra = observation_rows(obs_values, obs_precision, obs_cell, obs_count, TILE_CELLS, TILE_SIDE)
    collected = lax.all_gather(predicted, "member", axis=0, tiled=True)
    obs_rows = with_halo(
        jnp.concatenate([collected.astype(jnp.float32), extra], axis=0), (("space", 1),), 1
    )
    members = obs_rows.shape[0] - 4
    stacked, offset_row, offset_col = neighbourhood(obs_rows, TILE_SIDE)
    row_width = background.shape[4]
    col_count = row_width // TILE_CELLS
    first_member = lax.axis_index("member") * own_members
    shape_out = (own_members,) + background.shape[1:4] + (col_count, TILE_CELLS)
    mixing = solve_tiles(stacked, offset_row, offset_col, radius, members, TILE_SIDE, SWEEPS)
    own_mixing = lax.dynamic_slice_in_dim(mixing, first_member, own_members, 3)
    initial = jnp.zeros(shape_out, jnp.float32)
    summed = make_accumulate(
        own_mixing, col_count, initial, lax.all_gather(background, "member", axis=0, tiled=True)
    )
    analysis = summed.astype(jnp.bfloat16).reshape(background.shape)
    return analysis


def solution(mesh):
    return jax.shard_map(
        on_device,
        mesh=mesh,
        in_specs=(
            P("member", None, None, "space", None),
            P("space", None, None),
            P("space", None, None),
            P("space", None, None),
            P("space", None),
            P("space", None),
        ),
        out_specs=P("member", None, None, "space", None),
        check_vma=False,
    )
```

profile of v0, /device:TPU:2, one launch (start us, length us, event | category | flops | bytes accessed | tf_op | source)
XLA Modules:
  0.0 641.0 jit_solution(9184902969550619182)
XLA Ops:
  6.5 0.7 all-gather.2.cloned.1.call-update
  7.3 0.7 copy-done
  8.0 30.6 %copy.25 = bf16[4,4,6,1,8192]{0,4,2,1,3:T(8,128)(2,1)} copy(bf16[4,4,6,1,8192]{4,1,3,2,0:T(4,128)(2,1)S(1)} %copy-done) | data formatting | bytes 3145728 | tf_op args[0]
  38.6 11.2 %gather_fusion = bf16[1024,4]{1,0:T(8,128)(2,1)S(1)} fusion(bf16[4,196608]{0,1:T(8,128)(2,1)} %bitcast.103, s32[1024]{0:T(1024)S(1)} %broadcast_clamp_fusion), kind=kCustom, calls=%fused_computation | custom fusion | bytes 20480 | tf_op jit(solution)/shard_map/jit(_take)/gather | solution.py:38
  50.0 46.9 %all_gather.6 = bf16[64,1,8,128]{3,2,1,0:T(8,128)(2,1)S(1)} all-gather(bf16[4,1,8,128]{3,2,1,0:T(8,128)(2,1)S(1)} %broadcast_select_fusion), channel_id=1, replica_groups=mesh['member'=16,'space'=16] {'member'}, dimensions={0}, use_global_device_ids=true | all-gather | bytes 139264 | tf_op jit(solution)/shard_map/all_gather | solution.py:131
  97.1 1.9 collective-permute-start
  99.0 8.4 %collective-permute-start.1 = (f32[68,1,8,128]{3,2,1,0:T(8,128)S(1)}, f32[68,1,8,128]{3,2,1,0:T(8,128)S(1)}, u32[]{:S(2)}, u32[]{:S(2)}) collective-permute-start(f32[68,1,8,128]{3,2,1,0:T(8,128)S(1)} %constant_dynamic-update-slice_fusion), channel_id=1, source_target_pairs={{1,0},{2,1},{3,2},{4,3},{5,4},{6,5},{7,6},{8,7},{9,8},{10,9},{11,1... | collective-permute-start | bytes 835592 | tf_op jit(solution)/shard_map/ppermute | solution.py:22
  107.5 11.7 %collective-permute-done = f32[68,1,8,128]{3,2,1,0:T(8,128)S(1)} collective-permute-done((f32[68,1,8,128]{3,2,1,0:T(8,128)S(1)}, f32[68,1,8,128]{3,2,1,0:T(8,128)S(1)}, u32[]{:S(2)}, u32[]{:S(2)}) %collective-permute-start) | collective-permute-done | bytes 278560 | tf_op jit(solution)/shard_map/ppermute | solution.py:21
  119.3 2.6 collective-permute-done.1
  123.4 3.1 select_reduce_fusion
  126.5 0.4 fusion.25
  127.4 0.4 fusion.32
  127.8 0.4 fusion.24
  128.2 0.4 fusion.73
  128.6 0.4 fusion.72
  129.0 0.4 fusion.23
  129.4 0.4 fusion.75
  129.8 0.4 fusion.74
  130.2 0.4 fusion.22
  131.4 0.4 fusion.21
  131.8 0.4 fusion.79
  132.2 0.4 fusion.78
  132.6 0.4 fusion.20
  133.0 0.6 convolution_divide_fusion
  133.6 0.6 fusion.80
  134.2 2.5 fusion.26
  136.7 0.5 fusion.81
  137.5 411.6 %all-gather.2.cloned.1.call-done = bf16[64,4,6,1,8192]{4,1,3,2,0:T(4,128)(2,1)} async-done(((bf16[4,4,6,1,8192]{4,1,3,2,0:T(4,128)(2,1)}), bf16[64,4,6,1,8192]{4,1,3,2,0:T(4,128)(2,1)}) %all-gather.2.cloned.1.call-update) | async-done | bytes 25165840 | tf_op jit(solution)/shard_map/all_gather | solution.py:145
  549.1 40.8 %reshape.387 = bf16[64,4,6,8,1024]{4,3,1,2,0:T(8,128)(2,1)} reshape(bf16[64,4,6,1,8192]{4,1,3,2,0:T(4,128)(2,1)} %all-gather.2.cloned.1.call-done) | data formatting | bytes 50331648 | tf_op jit(solution)/shard_map/reshape.89
  589.9 40.9 %fusion.12 = bf16[4,4,6,1,8,1024]{5,0,2,1,4,3:T(4,128)(2,1)S(1)} fusion(bf16[64,4,6,8,1024]{4,3,1,2,0:T(8,128)(2,1)} %reshape.387, f32[8,64,64]{1,2,0:T(8,128)S(1)} %get-tuple-element.6, s32[]{:T(128)S(6)} %select_n.71, f32[8,4]{1,0:T(8,128)S(1)} %constant_dynamic-slice_fusion), kind=kOutput, calls=%fused_computation.18 | convolution fusion | flops 101455872 | bytes 26759172 | tf_op jit(solution)/shard_map/jlfrtc,rtjk->klfrtc/dot_general | solution.py:122
  630.8 0.9 copy.34
  631.6 2.4 reshape.373
  (57 shorter events, 3.2 us)
Async XLA Ops:
  6.5 1.4 copy-start
  6.5 542.5 %all-gather.2.cloned.1.call-start = ((), (), s32[]{:S(2)}) async-start(), calls=%async_computation | async-start | bytes 26738688 | tf_op jit(solution)/shard_map/all_gather | solution.py:145
  7.9 30.6 %copy-start.1 = (s32[1,8,128]{2,1,0:T(8,128)S(1)}, s32[1,8,128]{2,1,0:T(8,128)}, u32[]{:S(2)}) copy-start(s32[1,8,128]{2,1,0:T(8,128)} %param.9) | copy-start | bytes 12292
  7.9 89.0 %copy-start.2 = (f32[1,8,128]{2,1,0:T(8,128)S(1)}, f32[1,8,128]{2,1,0:T(8,128)}, u32[]{:S(2)}) copy-start(f32[1,8,128]{2,1,0:T(8,128)} %param.7) | copy-start | bytes 12292
  7.9 89.0 %copy-start.3 = (f32[1,8,128]{2,1,0:T(8,128)S(1)}, f32[1,8,128]{2,1,0:T(8,128)}, u32[]{:S(2)}) copy-start(f32[1,8,128]{2,1,0:T(8,128)} %param.8) | copy-start | bytes 12292
  7.9 89.0 %copy-start.6 = (s32[1,8]{1,0:T(1,128)S(1)}, s32[1,8]{1,0:T(1,128)}, u32[]{:S(2)}) copy-start(s32[1,8]{1,0:T(1,128)} %param.10) | copy-start | bytes 100
  8.0 99.6 %copy-start.7 = (s32[1,8]{1,0:T(1,128)S(1)}, s32[1,8]{1,0:T(1,128)}, u32[]{:S(2)}) copy-start(s32[1,8]{1,0:T(1,128)} %param.11) | copy-start | bytes 100
  97.1 22.2 %collective-permute-start = (f32[68,1,8,128]{3,2,1,0:T(8,128)S(1)}, f32[68,1,8,128]{3,2,1,0:T(8,128)S(1)}, u32[]{:S(2)}, u32[]{:S(2)}) collective-permute-start(f32[68,1,8,128]{3,2,1,0:T(8,128)S(1)} %constant_dynamic-update-slice_fusion), channel_id=1, source_target_pairs={{0,1},{1,2},{2,3},{3,4},{4,5},{5,6},{6,7},{7,8},{8,9},{9,10},{10,1... | collective-permute-start | bytes 835592 | tf_op jit(solution)/shard_map/ppermute | solution.py:21
  99.0 22.9 %collective-permute-start.1 = (f32[68,1,8,128]{3,2,1,0:T(8,128)S(1)}, f32[68,1,8,128]{3,2,1,0:T(8,128)S(1)}, u32[]{:S(2)}, u32[]{:S(2)}) collective-permute-start(f32[68,1,8,128]{3,2,1,0:T(8,128)S(1)} %constant_dynamic-update-slice_fusion), channel_id=1, source_target_pairs={{1,0},{2,1},{3,2},{4,3},{5,4},{6,5},{7,6},{8,7},{9,8},{10,9},{11,1... | collective-permute-start | bytes 835592 | tf_op jit(solution)/shard_map/ppermute | solution.py:22
  122.3 0.7 copy-start.4
  122.3 0.7 copy-start.5
Sparse Core Ops, SparseCore 0:
  9.1 539.8 all-gather.1
where the time goes:
time: 653 us; the launch traced here: 641 us
  waiting for transfers between devices  427 us (65%)
  local copies, waits for them, and re-layouts  87.2 us (13%)
  matrix products  54.5 us (8%)
  blocking collectives  46.9 us (7%)
  between operations  14 us (2%)
  starting transfers between devices  10.4 us (2%)
    all_gather x1, waiting for transfers between devices, on_device(): lax.all_gather(background, 'member', axis=0, tiled=True)  412 us
    all_gather x1, blocking collectives, on_device(): collected = lax.all_gather(predicted, 'member', axis=0, tiled=True)  46.9 us
    another operation x2, local copies, waits for them, and re-layouts  40.9 us
    dot_general x1, matrix products, make_accumulate(): jnp.einsum('jlfrtc,rtjk->klfrtc', shaped, chosen, preferred_element_type=...  40.9 us
    unnamed x26, local copies, waits for them, and re-layouts  31.7 us
  transfers between devices with their start and end apart: 3, of which 3 were waited for; matrix products, arithmetic and copies ran while one was open for 9% of the time, Pallas kernels for 0%

commit v1 on v0

v1 whole, which is shorter than its diff:
```python
import functools

import jax
import jax.numpy as jnp
from jax import lax
from jax.experimental import pallas as pl
from jax.experimental.pallas import tpu as pltpu
from jax.sharding import PartitionSpec as P

TILE_SIDE = 32
TILE_CELLS = 1024
SWEEPS = 6
EXACT = lax.Precision.HIGHEST


def split_kernel(parts, width, x_ref, out_ref, sems):
    copies = [
        pltpu.make_async_copy(
            x_ref.at[:, :, :, pl.ds(d * width, width)], out_ref.at[d], sems.at[d]
        )
        for d in range(parts)
    ]
    for copy in copies:
        copy.start()
    for copy in copies:
        copy.wait()


def join_kernel(parts, width, x_ref, out_ref, sems):
    copies = [
        pltpu.make_async_copy(
            x_ref.at[d], out_ref.at[:, :, :, pl.ds(d * width, width)], sems.at[d]
        )
        for d in range(parts)
    ]
    for copy in copies:
        copy.start()
    for copy in copies:
        copy.wait()


def observe_kernel(x_ref, cell_ref, out_ref):
    own, fields, levels, cells = x_ref.shape
    slots = out_ref.shape[-1]
    tile = pl.program_id(0)
    cell = cell_ref[pl.ds(tile, 1), :]
    in_tile = cell % cells
    level_field = cell // cells
    wanted = (level_field % fields) * levels + level_field // fields
    onehot = lax.broadcasted_iota(jnp.int32, (cells, slots), 0) == in_tile
    rows = x_ref[...].reshape(own * fields * levels, cells)
    found = jnp.dot(rows, onehot.astype(rows.dtype), preferred_element_type=jnp.float32)
    found = found.reshape(own, fields * levels, slots)
    match = lax.broadcasted_iota(jnp.int32, (fields * levels, slots), 0) == wanted
    picked = jnp.sum(jnp.where(match[None], found, 0.0), axis=1)
    out_ref[...] = picked.astype(out_ref.dtype)[None]


def solve_kernel(levels, where_ref, radius_ref, pred_ref, above_ref, own_ref, below_ref, out_ref):
    tile = where_ref[0]
    tiles = own_ref.shape[1]
    sources, _, own, slots = pred_ref.shape
    members = sources * own
    reach = radius_ref[0, tile].astype(jnp.float32)
    centre = 0.5 * TILE_SIDE - 0.5
    ensemble, values, weights = [], [], []
    for a, rows_ref in enumerate((above_ref, own_ref, below_ref)):
        for b in range(3):
            place = tile + b - 1
            inside = jnp.logical_and(place >= 0, place < tiles)
            held = jnp.clip(place, 0, tiles - 1)
            value, active, row, col = (rows_ref[i, pl.ds(held, 1), :] for i in range(4))
            dist_row = row + ((a - 1) * TILE_SIDE - centre)
            dist_col = col + ((b - 1) * TILE_SIDE - centre)
            taper = jnp.maximum(
                1.0 - (dist_row * dist_row + dist_col * dist_col) / (reach * reach), 0.0
            )
            weights.append(jnp.where(inside, active, 0.0) * (taper * taper))
            values.append(value)
            ensemble.append(
                pred_ref[:, a * 3 + b].astype(jnp.float32).reshape(members, slots)
            )
    ensemble = jnp.concatenate(ensemble, axis=1)
    values = jnp.concatenate(values, axis=1)
    weight = jnp.concatenate(weights, axis=1)
    mean_obs = jnp.mean(ensemble, axis=0, keepdims=True)
    anomaly = ensemble - mean_obs
    innovation = values - mean_obs
    scaled = anomaly * weight
    extended = jnp.concatenate(
        [anomaly, jnp.broadcast_to(innovation, (8, innovation.shape[1]))], axis=0
    )
    product = lax.dot_general(
        extended, scaled, (((1,), (1,)), ((), ())), precision=EXACT,
        preferred_element_type=jnp.float32,
    )
    forcing = product[members : members + 1]
    row_id = lax.broadcasted_iota(jnp.int32, (members, members), 0)
    col_id = lax.broadcasted_iota(jnp.int32, (members, members), 1)
    identity = (row_id == col_id).astype(jnp.float32)
    system = (members - 1.0) * identity + product[:members]
    scale = jnp.sum(
        jnp.sum(system * identity, axis=1, keepdims=True), axis=0, keepdims=True
    )
    root_part = system / scale
    inverse = identity
    mul = functools.partial(jnp.dot, precision=EXACT, preferred_element_type=jnp.float32)
    for sweep in range(SWEEPS):
        factor = 1.5 * identity - 0.5 * (root_part if sweep == 0 else mul(inverse, root_part))
        if sweep < SWEEPS - 1:
            root_part = mul(root_part, factor)
        inverse = factor if sweep == 0 else mul(factor, inverse)
    inv_sqrt = inverse / jnp.sqrt(scale)
    half = jnp.sum(inv_sqrt * forcing, axis=1, keepdims=True)
    mean_weight = jnp.sum(inv_sqrt * half, axis=0, keepdims=True)
    total = jnp.sqrt(jnp.float32(members - 1)) * inv_sqrt + mean_weight
    mixing = total - jnp.mean(total, axis=1, keepdims=True) + 1.0 / members
    mixing = mixing.astype(jnp.bfloat16)
    wide = members * levels
    spread = (
        lax.broadcasted_iota(jnp.int32, (wide, members), 0) // levels
        == lax.broadcasted_iota(jnp.int32, (wide, members), 1)
    ).astype(jnp.bfloat16)
    tall = jnp.dot(spread, mixing, preferred_element_type=jnp.float32).astype(jnp.bfloat16)
    full = lax.dot_general(
        tall, spread, (((1,), (1,)), ((), ())), preferred_element_type=jnp.float32
    )
    same = (
        lax.broadcasted_iota(jnp.int32, (wide, wide), 0) % levels
        == lax.broadcasted_iota(jnp.int32, (wide, wide), 1) % levels
    )
    out_ref[...] = jnp.where(same, full, 0.0).astype(out_ref.dtype)


def apply_kernel(mix_ref, x_ref, out_ref):
    sources, own, _, levels, width = x_ref.shape
    rows = x_ref[...].reshape(sources * own * levels, width)
    mixed = jnp.dot(mix_ref[...], rows, preferred_element_type=jnp.float32)
    out_ref[...] = mixed.astype(out_ref.dtype).reshape(out_ref.shape)


def observe(fields, cells):
    own, count, levels, width = fields.shape
    tiles, slots = cells.shape
    return pl.pallas_call(
        observe_kernel,
        grid=(tiles,),
        in_specs=[
            pl.BlockSpec((own, count, levels, TILE_CELLS), lambda t: (0, 0, 0, t)),
            pl.BlockSpec((tiles, slots), lambda t: (0, 0)),
        ],
        out_specs=pl.BlockSpec((1, own, slots), lambda t: (t, 0, 0)),
        out_shape=jax.ShapeDtypeStruct((tiles, own, slots), fields.dtype),
        name="observe",
    )(fields, cells)


def split(fields, parts):
    own, count, levels, width = fields.shape
    part = width // parts
    return pl.pallas_call(
        functools.partial(split_kernel, parts, part),
        in_specs=[pl.BlockSpec(memory_space=pl.ANY)],
        out_specs=pl.BlockSpec(memory_space=pl.ANY),
        out_shape=jax.ShapeDtypeStruct((parts, own, count, levels, part), fields.dtype),
        scratch_shapes=[pltpu.SemaphoreType.DMA((parts,))],
        name="split",
    )(fields)


def join(pieces):
    parts, own, count, levels, part = pieces.shape
    return pl.pallas_call(
        functools.partial(join_kernel, parts, part),
        in_specs=[pl.BlockSpec(memory_space=pl.ANY)],
        out_specs=pl.BlockSpec(memory_space=pl.ANY),
        out_shape=jax.ShapeDtypeStruct((own, count, levels, parts * part), pieces.dtype),
        scratch_shapes=[pltpu.SemaphoreType.DMA((parts,))],
        name="join",
    )(pieces)


def solve(tile, radius, pred, above, own, below, levels):
    members = pred.shape[0] * pred.shape[2]
    wide = members * levels
    vmem = pl.BlockSpec(memory_space=pltpu.VMEM)
    smem = pl.BlockSpec(memory_space=pltpu.SMEM)
    return pl.pallas_call(
        functools.partial(solve_kernel, levels),
        in_specs=[smem, smem, vmem, vmem, vmem, vmem],
        out_specs=vmem,
        out_shape=jax.ShapeDtypeStruct((wide, wide), jnp.bfloat16),
        name="solve",
    )(tile, radius, pred, above, own, below)


def apply_mixing(mix, pieces):
    parts, own, count, levels, part = pieces.shape
    block = pl.BlockSpec((parts, own, 1, levels, part), lambda f: (0, 0, f, 0, 0))
    return pl.pallas_call(
        apply_kernel,
        grid=(count,),
        in_specs=[pl.BlockSpec(mix.shape, lambda f: (0, 0)), block],
        out_specs=block,
        out_shape=jax.ShapeDtypeStruct(pieces.shape, pieces.dtype),
        name="apply",
    )(mix, pieces)


def observation_rows(obs_values, obs_precision, obs_cell, obs_count):
    slot_index = jnp.arange(obs_cell.shape[-1], dtype=jnp.int32)
    active = jnp.where(slot_index[None, :] < obs_count[:, None], obs_precision, 0.0)
    in_tile = obs_cell % TILE_CELLS
    row_place = (in_tile // TILE_SIDE).astype(jnp.float32)
    col_place = (in_tile % TILE_SIDE).astype(jnp.float32)
    return jnp.stack([obs_values, active, row_place, col_place])


def on_device(background, obs_values, obs_precision, obs_cell, obs_count, radius):
    own, levels, count, _, width = background.shape
    parts = lax.axis_size("member")
    rows = lax.axis_size("space")
    tiles = width // TILE_CELLS
    down = [(i, i + 1) for i in range(rows - 1)]
    up = [(i + 1, i) for i in range(rows - 1)]
    fields = background.transpose(0, 2, 3, 1, 4).reshape(own, count, levels, width)
    sent = lax.all_to_all(split(fields, parts), "member", 0, 0)

    extra = observation_rows(obs_values[0], obs_precision[0], obs_cell[0], obs_count[0])
    extra_above = lax.ppermute(extra, "space", down)
    extra_below = lax.ppermute(extra, "space", up)
    pred = observe(fields, obs_cell[0])
    around = jnp.stack(
        [lax.ppermute(pred, "space", down), pred, lax.ppermute(pred, "space", up)]
    )
    padded = jnp.pad(around, ((0, 0), (1, 1), (0, 0), (0, 0)))
    near = jnp.stack([padded[:, b : b + tiles] for b in range(3)], axis=1)
    near = near.reshape((9,) + pred.shape).transpose(1, 0, 2, 3)
    share = parts // tiles
    near = jnp.repeat(near, share, axis=0)
    near = lax.all_to_all(near, "member", 0, 0)
    tile = (lax.axis_index("member") // share).astype(jnp.int32).reshape(1)
    mix = solve(tile, radius, near, extra_above, extra, extra_below, levels)

    mixed = apply_mixing(mix, sent)
    back = lax.all_to_all(mixed, "member", 0, 0)
    out = join(back)
    return out.reshape(own, count, 1, levels, width).transpose(0, 3, 1, 2, 4)


def solution(mesh):
    return jax.shard_map(
        on_device,
        mesh=mesh,
        in_specs=(
            P("member", None, None, "space", None),
            P("space", None, None),
            P("space", None, None),
            P("space", None, None),
            P("space", None),
            P("space", None),
        ),
        out_specs=P("member", None, None, "space", None),
        check_vma=False,
    )
```

time: 653 us -> 224 us (0.34); the launches traced: 641 us -> 223 us
  waiting for transfers between devices: 427 us -> 31.9 us
  Pallas kernels: 0 us -> 114 us
  local copies, waits for them, and re-layouts: 87.2 us -> 3.21 us
  matrix products: 54.5 us -> 0 us
  starting transfers between devices: 10.4 us -> 28.2 us
  between operations: 14 us -> 0.21 us
    all_gather x1 -> x0, waiting for transfers between devices: 412 us -> none  [on_device(): lax.all_gather(background, 'member', axis=0, tiled=True)]
    pallas_call x0 -> x5, Pallas kernels: none -> 114 us  [the longest x1 48.9 us: split(): pl.pallas_call(functools.partial(split_kernel, parts, part), in_specs=[pl...]
    dot_general x22 -> x0, matrix products: 54.5 us -> none  [the longest x1 40.9 us: make_accumulate(): jnp.einsum('jlfrtc,rtjk->klfrtc', shaped, chosen, preferred_element_type=...]
    all_gather x1 -> x0, blocking collectives: 46.9 us -> none  [on_device(): collected = lax.all_gather(predicted, 'member', axis=0, tiled=True)]
    all_to_all x0 -> x1, blocking collectives: none -> 44.5 us  [on_device(): back = lax.all_to_all(mixed, 'member', 0, 0)]
    another operation x2, local copies, waits for them, and re-layouts: 40.9 us -> 0.03 us  [on_device(): near = jnp.stack([padded[:, b:b + tiles] for b in range(3)], axis=1)]
    unnamed x26 -> x18, local copies, waits for them, and re-layouts: 31.7 us -> 2.43 us
    all_to_all x0 -> x2, starting transfers between devices: none -> 13.4 us  [the longest x1 7.51 us: on_device(): sent = lax.all_to_all(split(fields, parts), 'member', 0, 0)]
  transfers between devices with their start and end apart: 3 -> 6, of which waited for: 3 -> 4; matrix products, arithmetic and copies ran while one was open for 9% -> 0% of each run, Pallas kernels for 0% -> 24%
where the time goes in v1:
time: 224 us; the launch traced here: 223 us
  Pallas kernels  114 us (51%)
  blocking collectives  44.5 us (20%)
  waiting for transfers between devices  31.9 us (14%)
  starting transfers between devices  28.2 us (13%)
  local copies, waits for them, and re-layouts  3.21 us (1%)
    pallas_call x1, Pallas kernels, split(): pl.pallas_call(functools.partial(split_kernel, parts, part), in_specs=[pl...  48.9 us
    pallas_call x1, Pallas kernels, join(): pl.pallas_call(functools.partial(join_kernel, parts, part), in_specs=[pl....  48.9 us
    all_to_all x1, blocking collectives, on_device(): back = lax.all_to_all(mixed, 'member', 0, 0)  44.5 us
    ppermute x1, waiting for transfers between devices, on_device(): extra_below = lax.ppermute(extra, 'space', up)  15.8 us
    ppermute x1, starting transfers between devices, on_device(): lax.ppermute(pred, 'space', up)  8.5 us
    ppermute x1, waiting for transfers between devices, on_device(): lax.ppermute(pred, 'space', down)  8.05 us
    all_to_all x1, starting transfers between devices, on_device(): sent = lax.all_to_all(split(fields, parts), 'member', 0, 0)  7.51 us
    all_to_all x1, starting transfers between devices, on_device(): near = lax.all_to_all(near, 'member', 0, 0)  5.94 us
  transfers between devices with their start and end apart: 6, of which 4 were waited for; matrix products, arithmetic and copies ran while one was open for 0% of the time, Pallas kernels for 24%

profile of v1, /device:TPU:2, one launch (start us, length us, event | category | flops | bytes accessed | tf_op | source)
XLA Modules:
  0.0 223.3 jit_solution(3753915169075024258)
XLA Ops:
  0.0 5.8 %observe.1 = bf16[8,4,128]{2,1,0:T(4,128)(2,1)} custom-call(bf16[4,6,4,8192]{3,2,1,0:T(4,128)(2,1)} %bitcast.26, s32[8,128]{1,0:T(8,128)} %bitcast.35), custom_call_target="tpu_custom_call" | custom-call | tf_op jit(solution)/shard_map/observe/pallas_call | solution.py:145
  5.8 8.5 %collective-permute-start.1 = (bf16[8,4,128]{2,1,0:T(4,128)(2,1)}, bf16[8,4,128]{2,1,0:T(4,128)(2,1)S(1)}, u32[]{:S(2)}, u32[]{:S(2)}) collective-permute-start(bf16[8,4,128]{2,1,0:T(4,128)(2,1)} %observe.1), channel_id=1, source_target_pairs={{1,0},{2,1},{3,2},{4,3},{5,4},{6,5},{7,6},{8,7},{9,8},{10,9},{11,1... | collective-permute-start | bytes 24584 | tf_op jit(solution)/shard_map/ppermute | solution.py:234
  14.3 1.9 collective-permute-start
  16.3 0.0 collective-permute-done.1
  16.3 8.0 %collective-permute-done = bf16[8,4,128]{2,1,0:T(4,128)(2,1)S(1)} collective-permute-done((bf16[8,4,128]{2,1,0:T(4,128)(2,1)}, bf16[8,4,128]{2,1,0:T(4,128)(2,1)S(1)}, u32[]{:S(2)}, u32[]{:S(2)}) %collective-permute-start) | collective-permute-done | bytes 8224 | tf_op jit(solution)/shard_map/ppermute | solution.py:234
  24.3 0.7 fusion.8
  25.1 0.7 pad_maximum_fusion.1
  25.8 0.1 pad_maximum_fusion
  25.9 0.7 broadcast_in_dim.8
  26.6 5.9 %all-to-all-start = ((bf16[16,9,4,128]{3,2,1,0:T(4,128)(2,1)}), bf16[16,9,4,128]{3,2,1,0:T(4,128)(2,1)S(1)}, u32[]{:S(2)}, u32[]{:S(2)}) async-start(bf16[16,9,4,128]{3,2,1,0:T(4,128)(2,1)} %bitcast.13), calls=%async_computation | async-start | bytes 294912 | tf_op jit(solution)/shard_map/all_to_all | solution.py:241
  32.6 48.9 %split.1 = bf16[16,4,6,4,512]{4,3,2,1,0:T(4,128)(2,1)} custom-call(bf16[4,6,4,8192]{3,2,1,0:T(4,128)(2,1)} %bitcast.27), custom_call_target="tpu_custom_call" | custom-call | tf_op jit(solution)/shard_map/split/pallas_call | solution.py:161
  81.5 0.0 copy-start.6
  81.5 0.0 copy-start.8
  81.5 0.0 copy-start.3
  81.5 0.0 copy-start.7
  81.5 0.0 all-to-all-done.pred_ref
  81.6 0.7 copy-done.1
  82.2 7.5 %all-to-all-start.1 = ((bf16[16,4,6,4,512]{4,3,2,1,0:T(4,128)(2,1)}), bf16[16,4,6,4,512]{4,3,2,1,0:T(4,128)(2,1)S(1)}, u32[]{:S(2)}, u32[]{:S(2)}) async-start(bf16[16,4,6,4,512]{4,3,2,1,0:T(4,128)(2,1)} %split.1), calls=%async_computation.1 | async-start | bytes 3145728 | tf_op jit(solution)/shard_map/all_to_all | solution.py:227
  89.8 0.1 fusion.5
  89.8 0.0 copy-done.3
  89.8 0.0 copy-done.7
  89.9 1.9 collective-permute-start.3
  91.8 2.4 %collective-permute-start.2 = (f32[4,8,128]{2,1,0:T(8,128)S(1)}, f32[4,8,128]{2,1,0:T(8,128)S(1)}, u32[]{:S(2)}, u32[]{:S(2)}) collective-permute-start(f32[4,8,128]{2,1,0:T(8,128)S(1)} %pad_maximum_fusion.2.own_ref), channel_id=1, source_target_pairs={{0,1},{1,2},{2,3},{3,4},{4,5},{5,6},{6,7},{7,8},{8,9},{9,10},{10,1... | collective-permute-start | bytes 49160 | tf_op jit(solution)/shard_map/ppermute | solution.py:230
  94.2 15.8 %collective-permute-done.3.below_ref = f32[4,8,128]{2,1,0:T(8,128)S(1)} collective-permute-done((f32[4,8,128]{2,1,0:T(8,128)S(1)}, f32[4,8,128]{2,1,0:T(8,128)S(1)}, u32[]{:S(2)}, u32[]{:S(2)}) %collective-permute-start.3) | collective-permute-done | bytes 16416 | tf_op jit(solution)/shard_map/ppermute | solution.py:231
  110.1 3.4 %collective-permute-done.2.above_ref = f32[4,8,128]{2,1,0:T(8,128)S(1)} collective-permute-done((f32[4,8,128]{2,1,0:T(8,128)S(1)}, f32[4,8,128]{2,1,0:T(8,128)S(1)}, u32[]{:S(2)}, u32[]{:S(2)}) %collective-permute-start.2) | collective-permute-done | bytes 16416 | tf_op jit(solution)/shard_map/ppermute | solution.py:230
  113.5 0.6 copy-done.5
  114.1 4.9 %solve.1.mix_ref = bf16[256,256]{1,0:T(8,128)(2,1)} custom-call(s32[1]{0:T(128)} %bitcast.where_ref, s32[1,8]{1,0:T(1,128)} %radius_ref.1, bf16[16,9,4,128]{3,2,1,0:T(4,128)(2,1)} %copy-done.1, f32[4,8,128]{2,1,0:T(8,128)} %copy-done.5, f32[4,8,128]{2,1,0:T(8,128)} %copy-done.2, f32[4,8,128]{2,1,0:T(8,128)} %copy-done.4), custom_call_target="tpu_custom_call" | custom-call | tf_op jit(solution)/shard_map/solve/pallas_call | solution.py:188
  119.0 4.6 %all-to-all-done.1.x_ref = bf16[16,4,6,4,512]{4,3,2,1,0:T(4,128)(2,1)S(1)} async-done(((bf16[16,4,6,4,512]{4,3,2,1,0:T(4,128)(2,1)}), bf16[16,4,6,4,512]{4,3,2,1,0:T(4,128)(2,1)S(1)}, u32[]{:S(2)}, u32[]{:S(2)}) %all-to-all-start.1) | async-done | bytes 1572896 | tf_op jit(solution)/shard_map/all_to_all | solution.py:227
  123.6 1.1 copy-done
  124.7 5.2 %apply.1 = bf16[16,4,6,4,512]{4,3,2,1,0:T(4,128)(2,1)} custom-call(bf16[256,256]{1,0:T(8,128)(2,1)} %solve.1.mix_ref, bf16[16,4,6,4,512]{4,3,2,1,0:T(4,128)(2,1)} %copy-done), custom_call_target="tpu_custom_call" | custom-call | tf_op jit(solution)/shard_map/apply/pallas_call | solution.py:200
  129.9 44.5 %all_to_all.15.x_ref = bf16[16,4,6,4,512]{4,3,2,1,0:T(4,128)(2,1)} all-to-all(bf16[16,4,6,4,512]{4,3,2,1,0:T(4,128)(2,1)} %apply.1), channel_id=1, replica_groups=mesh['member'=16,'space'=16] {'member'}, dimensions={0} | all-to-all | bytes 3145728 | tf_op jit(solution)/shard_map/all_to_all | solution.py:246
  174.4 48.9 %join.1 = bf16[4,6,4,8192]{3,2,1,0:T(4,128)(2,1)} custom-call(bf16[16,4,6,4,512]{4,3,2,1,0:T(4,128)(2,1)} %all_to_all.15.x_ref), custom_call_target="tpu_custom_call" | custom-call | tf_op jit(solution)/shard_map/join/pallas_call | solution.py:173
  (14 shorter events, 0.1 us)
Async XLA Ops:
  5.8 10.4 %collective-permute-start.1 = (bf16[8,4,128]{2,1,0:T(4,128)(2,1)}, bf16[8,4,128]{2,1,0:T(4,128)(2,1)S(1)}, u32[]{:S(2)}, u32[]{:S(2)}) collective-permute-start(bf16[8,4,128]{2,1,0:T(4,128)(2,1)} %observe.1), channel_id=1, source_target_pairs={{1,0},{2,1},{3,2},{4,3},{5,4},{6,5},{7,6},{8,7},{9,8},{10,9},{11,1... | collective-permute-start | bytes 24584 | tf_op jit(solution)/shard_map/ppermute | solution.py:234
  14.3 10.0 %collective-permute-start = (bf16[8,4,128]{2,1,0:T(4,128)(2,1)}, bf16[8,4,128]{2,1,0:T(4,128)(2,1)S(1)}, u32[]{:S(2)}, u32[]{:S(2)}) collective-permute-start(bf16[8,4,128]{2,1,0:T(4,128)(2,1)} %observe.1), channel_id=1, source_target_pairs={{0,1},{1,2},{2,3},{3,4},{4,5},{5,6},{6,7},{7,8},{8,9},{9,10},{10,1... | collective-permute-start | bytes 24584 | tf_op jit(solution)/shard_map/ppermute | solution.py:234
  26.6 54.9 %all-to-all-start = ((bf16[16,9,4,128]{3,2,1,0:T(4,128)(2,1)}), bf16[16,9,4,128]{3,2,1,0:T(4,128)(2,1)S(1)}, u32[]{:S(2)}, u32[]{:S(2)}) async-start(bf16[16,9,4,128]{3,2,1,0:T(4,128)(2,1)} %bitcast.13), calls=%async_computation | async-start | bytes 294912 | tf_op jit(solution)/shard_map/all_to_all | solution.py:241
  81.5 8.2 %copy-start.6 = (f32[1,8,128]{2,1,0:T(8,128)S(1)}, f32[1,8,128]{2,1,0:T(8,128)}, u32[]{:S(2)}) copy-start(f32[1,8,128]{2,1,0:T(8,128)} %param.8) | copy-start | bytes 12292
  81.5 8.2 %copy-start.8 = (s32[1,8]{1,0:T(1,128)S(1)}, s32[1,8]{1,0:T(1,128)}, u32[]{:S(2)}) copy-start(s32[1,8]{1,0:T(1,128)} %param.10) | copy-start | bytes 100
  81.5 8.3 %copy-start.3 = (s32[1,8,128]{2,1,0:T(8,128)S(1)}, s32[1,8,128]{2,1,0:T(8,128)}, u32[]{:S(2)}) copy-start(s32[1,8,128]{2,1,0:T(8,128)} %param.9) | copy-start | bytes 12292
  81.5 8.3 %copy-start.7 = (f32[1,8,128]{2,1,0:T(8,128)S(1)}, f32[1,8,128]{2,1,0:T(8,128)}, u32[]{:S(2)}) copy-start(f32[1,8,128]{2,1,0:T(8,128)} %param.7) | copy-start | bytes 12292
  81.5 0.7 copy-start.1
  82.2 41.4 %all-to-all-start.1 = ((bf16[16,4,6,4,512]{4,3,2,1,0:T(4,128)(2,1)}), bf16[16,4,6,4,512]{4,3,2,1,0:T(4,128)(2,1)S(1)}, u32[]{:S(2)}, u32[]{:S(2)}) async-start(bf16[16,4,6,4,512]{4,3,2,1,0:T(4,128)(2,1)} %split.1), calls=%async_computation.1 | async-start | bytes 3145728 | tf_op jit(solution)/shard_map/all_to_all | solution.py:227
  89.9 23.6 %copy-start.2 = (f32[4,8,128]{2,1,0:T(8,128)}, f32[4,8,128]{2,1,0:T(8,128)S(1)}, u32[]{:S(2)}) copy-start(f32[4,8,128]{2,1,0:T(8,128)S(1)} %pad_maximum_fusion.2.own_ref) | copy-start | bytes 49156
  89.9 20.2 %collective-permute-start.3 = (f32[4,8,128]{2,1,0:T(8,128)S(1)}, f32[4,8,128]{2,1,0:T(8,128)S(1)}, u32[]{:S(2)}, u32[]{:S(2)}) collective-permute-start(f32[4,8,128]{2,1,0:T(8,128)S(1)} %pad_maximum_fusion.2.own_ref), channel_id=1, source_target_pairs={{1,0},{2,1},{3,2},{4,3},{5,4},{6,5},{7,6},{8,7},{9,8},{10,9},{11,1... | collective-permute-start | bytes 49160 | tf_op jit(solution)/shard_map/ppermute | solution.py:231
  91.8 21.7 %collective-permute-start.2 = (f32[4,8,128]{2,1,0:T(8,128)S(1)}, f32[4,8,128]{2,1,0:T(8,128)S(1)}, u32[]{:S(2)}, u32[]{:S(2)}) collective-permute-start(f32[4,8,128]{2,1,0:T(8,128)S(1)} %pad_maximum_fusion.2.own_ref), channel_id=1, source_target_pairs={{0,1},{1,2},{2,3},{3,4},{4,5},{5,6},{6,7},{7,8},{8,9},{9,10},{10,1... | collective-permute-start | bytes 49160 | tf_op jit(solution)/shard_map/ppermute | solution.py:230
  110.1 3.4 %copy-start.4 = (f32[4,8,128]{2,1,0:T(8,128)}, f32[4,8,128]{2,1,0:T(8,128)S(1)}, u32[]{:S(2)}) copy-start(f32[4,8,128]{2,1,0:T(8,128)S(1)} %collective-permute-done.3.below_ref) | copy-start | bytes 49156
  113.5 0.6 copy-start.5
  123.6 1.1 copy-start

commit v2 on v1

--- a/solution.py
+++ b/solution.py
@@ -13,33 +13,19 @@
 EXACT = lax.Precision.HIGHEST
 
 
-def split_kernel(parts, width, x_ref, out_ref, sems):
-    copies = [
-        pltpu.make_async_copy(
-            x_ref.at[:, :, :, pl.ds(d * width, width)], out_ref.at[d], sems.at[d]
-        )
-        for d in range(parts)
-    ]
-    for copy in copies:
-        copy.start()
-    for copy in copies:
-        copy.wait()
-
-
-def join_kernel(parts, width, x_ref, out_ref, sems):
-    copies = [
-        pltpu.make_async_copy(
-            x_ref.at[d], out_ref.at[:, :, :, pl.ds(d * width, width)], sems.at[d]
-        )
-        for d in range(parts)
-    ]
-    for copy in copies:
-        copy.start()
-    for copy in copies:
-        copy.wait()
-
-
-def observe_kernel(x_ref, cell_ref, out_ref):
+def split_kernel(x_ref, out_ref):
+    share, _, _, _, width = out_ref.shape
+    for h in range(share):
+        out_ref[h] = x_ref[:, :, :, h * width : (h + 1) * width]
+
+
+def join_kernel(x_ref, out_ref):
+    share, _, _, _, width = x_ref.shape
+    for h in range(share):
+        out_ref[:, :, :, h * width : (h + 1) * width] = x_ref[h]
+
+
+def observe_kernel(x_ref, value_ref, precision_ref, cell_ref, count_ref, out_ref):
     own, fields, levels, cells = x_ref.shape
     slots = out_ref.shape[-1]
     tile = pl.program_id(0)
@@ -53,12 +39,39 @@
     found = found.reshape(own, fields * levels, slots)
     match = lax.broadcasted_iota(jnp.int32, (fields * levels, slots), 0) == wanted
     picked = jnp.sum(jnp.where(match[None], found, 0.0), axis=1)
-    out_ref[...] = picked.astype(out_ref.dtype)[None]
+    used = lax.broadcasted_iota(jnp.int32, (1, slots), 1) < count_ref[0, tile]
+    active = jnp.where(used, precision_ref[pl.ds(tile, 1), :], 0.0)
+    row_place = (in_tile // TILE_SIDE).astype(jnp.float32)
+    col_place = (in_tile % TILE_SIDE).astype(jnp.float32)
+    out_ref[0, 0:own, :] = picked
+    out_ref[0, own : own + 1, :] = value_ref[pl.ds(tile, 1), :]
+    out_ref[0, own + 1 : own + 2, :] = active
+    out_ref[0, own + 2 : own + 3, :] = row_place
+    out_ref[0, own + 3 : own + 4, :] = col_place
+
+
+def near_kernel(above_ref, own_ref, below_ref, out_ref):
+    parts, _, own, _ = out_ref.shape
+    tiles = own_ref.shape[0]
+    share = parts // tiles
+    for a, rows_ref in enumerate((above_ref, own_ref, below_ref)):
+        for t in range(tiles):
+            rows = rows_ref[t, 0:own, :].astype(out_ref.dtype)
+            for b in range(3):
+                for h in range(share):
+                    place = t + 1 - b
+                    if 0 <= place < tiles:
+                        out_ref[place * share + h, a * 3 + b] = rows
+    for h in range(share):
+        for a in range(3):
+            blank = jnp.zeros((own, out_ref.shape[-1]), out_ref.dtype)
+            out_ref[h, a * 3] = blank
+            out_ref[(tiles - 1) * share + h, a * 3 + 2] = blank
 
 
 def solve_kernel(levels, where_ref, radius_ref, pred_ref, above_ref, own_ref, below_ref, out_ref):
     tile = where_ref[0]
-    tiles = own_ref.shape[1]
+    tiles = own_ref.shape[0]
     sources, _, own, slots = pred_ref.shape
     members = sources * own
     reach = radius_ref[0, tile].astype(jnp.float32)
@@ -69,7 +82,9 @@
             place = tile + b - 1
             inside = jnp.logical_and(place >= 0, place < tiles)
             held = jnp.clip(place, 0, tiles - 1)
-            value, active, row, col = (rows_ref[i, pl.ds(held, 1), :] for i in range(4))
+            value, active, row, col = (
+                rows_ref[held, own + i : own + i + 1, :] for i in range(4)
+            )
             dist_row = row + ((a - 1) * TILE_SIDE - centre)
             dist_col = col + ((b - 1) * TILE_SIDE - centre)
             taper = jnp.maximum(
@@ -139,45 +154,63 @@
     out_ref[...] = mixed.astype(out_ref.dtype).reshape(out_ref.shape)
 
 
-def observe(fields, cells):
-    own, count, levels, width = fields.shape
+def observe(fields, values, precision, cells, count):
+    own, kinds, levels, width = fields.shape
     tiles, slots = cells.shape
+    whole = pl.BlockSpec((tiles, slots), lambda t: (0, 0))
     return pl.pallas_call(
         observe_kernel,
         grid=(tiles,),
         in_specs=[
-            pl.BlockSpec((own, count, levels, TILE_CELLS), lambda t: (0, 0, 0, t)),
-            pl.BlockSpec((tiles, slots), lambda t: (0, 0)),
+            pl.BlockSpec((own, kinds, levels, TILE_CELLS), lambda t: (0, 0, 0, t)),
+            whole,
+            whole,
+            whole,
+            pl.BlockSpec(memory_space=pltpu.SMEM),
         ],
-        out_specs=pl.BlockSpec((1, own, slots), lambda t: (t, 0, 0)),
-        out_shape=jax.ShapeDtypeStruct((tiles, own, slots), fields.dtype),
+        out_specs=pl.BlockSpec((1, own + 4, slots), lambda t: (t, 0, 0)),
+        out_shape=jax.ShapeDtypeStruct((tiles, own + 4, slots), jnp.float32),
         name="observe",
-    )(fields, cells)
+    )(fields, values, precision, cells, count)
 
 
 def split(fields, parts):
-    own, count, levels, width = fields.shape
+    own, kinds, levels, width = fields.shape
     part = width // parts
-    return pl.pallas_call(
-        functools.partial(split_kernel, parts, part),
-        in_specs=[pl.BlockSpec(memory_space=pl.ANY)],
-        out_specs=pl.BlockSpec(memory_space=pl.ANY),
-        out_shape=jax.ShapeDtypeStruct((parts, own, count, levels, part), fields.dtype),
-        scratch_shapes=[pltpu.SemaphoreType.DMA((parts,))],
+    share = TILE_CELLS // part
+    return pl.pallas_call(
+        split_kernel,
+        grid=(parts // share,),
+        in_specs=[pl.BlockSpec((own, kinds, levels, TILE_CELLS), lambda t: (0, 0, 0, t))],
+        out_specs=pl.BlockSpec((share, own, kinds, levels, part), lambda t: (t, 0, 0, 0, 0)),
+        out_shape=jax.ShapeDtypeStruct((parts, own, kinds, levels, part), fields.dtype),
         name="split",
     )(fields)
 
 
 def join(pieces):
-    parts, own, count, levels, part = pieces.shape
-    return pl.pallas_call(
-        functools.partial(join_kernel, parts, part),
-        in_specs=[pl.BlockSpec(memory_space=pl.ANY)],
-        out_specs=pl.BlockSpec(memory_space=pl.ANY),
-        out_shape=jax.ShapeDtypeStruct((own, count, levels, parts * part), pieces.dtype),
-        scratch_shapes=[pltpu.SemaphoreType.DMA((parts,))],
+    parts, own, kinds, levels, part = pieces.shape
+    share = TILE_CELLS // part
+    return pl.pallas_call(
+        join_kernel,
+        grid=(parts // share,),
+        in_specs=[pl.BlockSpec((share, own, kinds, levels, part), lambda t: (t, 0, 0, 0, 0))],
+        out_specs=pl.BlockSpec((own, kinds, levels, TILE_CELLS), lambda t: (0, 0, 0, t)),
+        out_shape=jax.ShapeDtypeStruct((own, kinds, levels, parts * part), pieces.dtype),
         name="join",
     )(pieces)
+
+
+def surround(above, own, below, parts, members):
+    tiles, _, slots = own.shape
+    vmem = pl.BlockSpec(memory_space=pltpu.VMEM)
+    return pl.pallas_call(
+        near_kernel,
+        in_specs=[vmem, vmem, vmem],
+        out_specs=vmem,
+        out_shape=jax.ShapeDtypeStruct((parts, 9, members, slots), jnp.bfloat16),
+        name="surround",
+    )(above, own, below)
 
 
 def solve(tile, radius, pred, above, own, below, levels):
@@ -207,45 +240,29 @@
     )(mix, pieces)
 
 
-def observation_rows(obs_values, obs_precision, obs_cell, obs_count):
-    slot_index = jnp.arange(obs_cell.shape[-1], dtype=jnp.int32)
-    active = jnp.where(slot_index[None, :] < obs_count[:, None], obs_precision, 0.0)
-    in_tile = obs_cell % TILE_CELLS
-    row_place = (in_tile // TILE_SIDE).astype(jnp.float32)
-    col_place = (in_tile % TILE_SIDE).astype(jnp.float32)
-    return jnp.stack([obs_values, active, row_place, col_place])
-
-
 def on_device(background, obs_values, obs_precision, obs_cell, obs_count, radius):
-    own, levels, count, _, width = background.shape
+    own, levels, kinds, _, width = background.shape
     parts = lax.axis_size("member")
     rows = lax.axis_size("space")
-    tiles = width // TILE_CELLS
+    share = parts * TILE_CELLS // width
     down = [(i, i + 1) for i in range(rows - 1)]
     up = [(i + 1, i) for i in range(rows - 1)]
-    fields = background.transpose(0, 2, 3, 1, 4).reshape(own, count, levels, width)
-    sent = lax.all_to_all(split(fields, parts), "member", 0, 0)
-
-    extra = observation_rows(obs_values[0], obs_precision[0], obs_cell[0], obs_count[0])
-    extra_above = lax.ppermute(extra, "space", down)
-    extra_below = lax.ppermute(extra, "space", up)
-    pred = observe(fields, obs_cell[0])
-    around = jnp.stack(
-        [lax.ppermute(pred, "space", down), pred, lax.ppermute(pred, "space", up)]
-    )
-    padded = jnp.pad(around, ((0, 0), (1, 1), (0, 0), (0, 0)))
-    near = jnp.stack([padded[:, b : b + tiles] for b in range(3)], axis=1)
-    near = near.reshape((9,) + pred.shape).transpose(1, 0, 2, 3)
-    share = parts // tiles
-    near = jnp.repeat(near, share, axis=0)
-    near = lax.all_to_all(near, "member", 0, 0)
+    fields = background.transpose(0, 2, 3, 1, 4).reshape(own, kinds, levels, width)
+    pieces = split(fields, parts)
+    pieces, fields = lax.optimization_barrier((pieces, fields))
+    sent = lax.all_to_all(pieces, "member", 0, 0)
+
+    here = observe(fields, obs_values[0], obs_precision[0], obs_cell[0], obs_count)
+    above = lax.ppermute(here, "space", down)
+    below = lax.ppermute(here, "space", up)
+    near = lax.all_to_all(surround(above, here, below, parts, own), "member", 0, 0)
     tile = (lax.axis_index("member") // share).astype(jnp.int32).reshape(1)
-    mix = solve(tile, radius, near, extra_above, extra, extra_below, levels)
+    mix = solve(tile, radius, near, above, here, below, levels)
 
     mixed = apply_mixing(mix, sent)
     back = lax.all_to_all(mixed, "member", 0, 0)
     out = join(back)
-    return out.reshape(own, count, 1, levels, width).transpose(0, 3, 1, 2, 4)
+    return out.reshape(own, kinds, 1, levels, width).transpose(0, 3, 1, 2, 4)
 
 
 def solution(mesh):

time: 224 us -> 137 us (0.61)
  Pallas kernels: 114 us -> 28.3 us
  starting transfers between devices: 28.2 us -> 14.1 us
  blocking collectives: 44.5 us -> 55.6 us
  waiting for transfers between devices: 31.9 us -> 35.9 us
    pallas_call x2 -> x3, Pallas kernels: 97.8 us -> 12.3 us  [the longest x1 5.41 us: split(): pl.pallas_call(split_kernel, grid=(parts // share,), in_specs=[pl.BlockSp...]
    all_to_all x2 -> x1, waiting for transfers between devices: 4.63 us -> 27.6 us  [on_device(): sent = lax.all_to_all(pieces, 'member', 0, 0)]
    ppermute x4 -> x2, waiting for transfers between devices: 27.3 us -> 8.3 us  [the longest x1 8.3 us: on_device(): above = lax.ppermute(here, 'space', down)]
    all_to_all x0 -> x1, blocking collectives: none -> 14.5 us  [on_device(): lax.all_to_all(surround(above, here, below, parts, own), 'member', 0, 0)]
    all_to_all x2 -> x1, starting transfers between devices: 13.4 us -> 3.71 us  [on_device(): sent = lax.all_to_all(pieces, 'member', 0, 0)]
    ppermute x4 -> x2, starting transfers between devices: 14.7 us -> 10.4 us  [the longest x1 8.5 us: on_device(): below = lax.ppermute(here, 'space', up)]
    all_to_all x1, blocking collectives: 44.5 us -> 41.1 us  [on_device(): back = lax.all_to_all(mixed, 'member', 0, 0)]
  transfers between devices with their start and end apart: 6 -> 3, of which waited for: 4 -> 2; matrix products, arithmetic and copies ran while one was open for 0% -> 0% of each run, Pallas kernels for 24% -> 4%
where the time goes in v2:
time: 137 us; the launch traced here: 136 us
  blocking collectives  55.6 us (41%)
  waiting for transfers between devices  35.9 us (26%)
  Pallas kernels  28.3 us (21%)
  starting transfers between devices  14.1 us (10%)
  local copies, waits for them, and re-layouts  1.76 us (1%)
    all_to_all x1, blocking collectives, on_device(): back = lax.all_to_all(mixed, 'member', 0, 0)  41.1 us
    all_to_all x1, waiting for transfers between devices, on_device(): sent = lax.all_to_all(pieces, 'member', 0, 0)  27.6 us
    all_to_all x1, blocking collectives, on_device(): lax.all_to_all(surround(above, here, below, parts, own), 'member', 0, 0)  14.5 us
    ppermute x1, starting transfers between devices, on_device(): below = lax.ppermute(here, 'space', up)  8.5 us
    ppermute x1, waiting for transfers between devices, on_device(): above = lax.ppermute(here, 'space', down)  8.3 us
    pallas_call x1, Pallas kernels, observe(): pl.pallas_call(observe_kernel, grid=(tiles,), in_specs=[pl.BlockSpec((own...  5.91 us
    pallas_call x1, Pallas kernels, split(): pl.pallas_call(split_kernel, grid=(parts // share,), in_specs=[pl.BlockSp...  5.41 us
    pallas_call x1, Pallas kernels, join(): pl.pallas_call(join_kernel, grid=(parts // share,), in_specs=[pl.BlockSpe...  5.41 us
  transfers between devices with their start and end apart: 3, of which 2 were waited for; matrix products, arithmetic and copies ran while one was open for 0% of the time, Pallas kernels for 4%

profile of v2, /device:TPU:2, one launch (start us, length us, event | category | flops | bytes accessed | tf_op | source)
XLA Modules:
  0.0 135.8 jit_solution(11553528871980612724)
XLA Ops:
  0.0 5.4 %split.1 = bf16[16,4,6,4,512]{4,3,2,1,0:T(4,128)(2,1)} custom-call(bf16[4,6,4,8192]{3,2,1,0:T(4,128)(2,1)} %bitcast.14), custom_call_target="tpu_custom_call" | custom-call | tf_op jit(solution)/shard_map/split/pallas_call | solution.py:181
  5.4 5.9 %observe.1.own_ref = f32[8,8,128]{2,1,0:T(8,128)} custom-call(bf16[4,6,4,8192]{3,2,1,0:T(4,128)(2,1)} %bitcast.15, f32[8,128]{1,0:T(8,128)} %bitcast.16, f32[8,128]{1,0:T(8,128)} %bitcast.17, s32[8,128]{1,0:T(8,128)} %bitcast.18, s32[1,8]{1,0:T(1,128)} %count_ref.1), custom_call_target="tpu_custom_call" | custom-call | tf_op jit(solution)/shard_map/observe/pallas_call | solution.py:161
  11.3 8.5 %collective-permute-start.1 = (f32[8,8,128]{2,1,0:T(8,128)}, f32[8,8,128]{2,1,0:T(8,128)S(1)}, u32[]{:S(2)}, u32[]{:S(2)}) collective-permute-start(f32[8,8,128]{2,1,0:T(8,128)} %observe.1.own_ref), channel_id=1, source_target_pairs={{1,0},{2,1},{3,2},{4,3},{5,4},{6,5},{7,6},{8,7},{9,8},{10,9},{11,1... | collective-permute-start | bytes 98312 | tf_op jit(solution)/shard_map/ppermute | solution.py:257
  19.8 1.9 %collective-permute-start = (f32[8,8,128]{2,1,0:T(8,128)}, f32[8,8,128]{2,1,0:T(8,128)S(1)}, u32[]{:S(2)}, u32[]{:S(2)}) collective-permute-start(f32[8,8,128]{2,1,0:T(8,128)} %observe.1.own_ref), channel_id=1, source_target_pairs={{0,1},{1,2},{2,3},{3,4},{4,5},{5,6},{6,7},{7,8},{8,9},{9,10},{10,1... | collective-permute-start | bytes 98312 | tf_op jit(solution)/shard_map/ppermute | solution.py:256
  21.8 0.0 collective-permute-done.1.below_ref
  21.8 0.0 copy-start.1
  21.8 8.3 %collective-permute-done.above_ref = f32[8,8,128]{2,1,0:T(8,128)S(1)} collective-permute-done((f32[8,8,128]{2,1,0:T(8,128)}, f32[8,8,128]{2,1,0:T(8,128)S(1)}, u32[]{:S(2)}, u32[]{:S(2)}) %collective-permute-start) | collective-permute-done | bytes 32800 | tf_op jit(solution)/shard_map/ppermute | solution.py:256
  30.1 0.0 copy-done.1
  30.1 0.0 copy-start.2
  30.1 0.6 copy-done.2
  30.7 1.5 %surround.1 = bf16[16,9,4,128]{3,2,1,0:T(4,128)(2,1)} custom-call(f32[8,8,128]{2,1,0:T(8,128)} %copy-done.2, f32[8,8,128]{2,1,0:T(8,128)} %observe.1.own_ref, f32[8,8,128]{2,1,0:T(8,128)} %copy-done.1), custom_call_target="tpu_custom_call" | custom-call | tf_op jit(solution)/shard_map/surround/pallas_call | solution.py:207
  32.2 14.5 %all_to_all.15.pred_ref = bf16[16,9,4,128]{3,2,1,0:T(4,128)(2,1)} all-to-all(bf16[16,9,4,128]{3,2,1,0:T(4,128)(2,1)} %surround.1), channel_id=1, replica_groups=mesh['member'=16,'space'=16] {'member'}, dimensions={0} | all-to-all | bytes 294912 | tf_op jit(solution)/shard_map/all_to_all | solution.py:258
  46.7 3.7 %all-to-all-start.1 = ((bf16[16,4,6,4,512]{4,3,2,1,0:T(4,128)(2,1)}), bf16[16,4,6,4,512]{4,3,2,1,0:T(4,128)(2,1)S(1)}, u32[]{:S(2)}, u32[]{:S(2)}) async-start(bf16[16,4,6,4,512]{4,3,2,1,0:T(4,128)(2,1)} %split.1), calls=%async_computation.1 | async-start | bytes 3145728 | tf_op jit(solution)/shard_map/all_to_all | solution.py:253
  50.4 4.9 %solve.1.mix_ref = bf16[256,256]{1,0:T(8,128)(2,1)} custom-call(s32[1]{0:T(128)} %bitcast.where_ref, s32[1,8]{1,0:T(1,128)} %radius_ref.1, bf16[16,9,4,128]{3,2,1,0:T(4,128)(2,1)} %all_to_all.15.pred_ref, f32[8,8,128]{2,1,0:T(8,128)} %copy-done.2, f32[8,8,128]{2,1,0:T(8,128)} %observe.1.own_ref, f32[8,8,128]{2,1,0:T(8,128)} %copy-done.1), custom_call_target="tpu_custom_call" | custom-call | tf_op jit(solution)/shard_map/solve/pallas_call | solution.py:221
  55.3 27.6 %all-to-all-done.1.x_ref = bf16[16,4,6,4,512]{4,3,2,1,0:T(4,128)(2,1)S(1)} async-done(((bf16[16,4,6,4,512]{4,3,2,1,0:T(4,128)(2,1)}), bf16[16,4,6,4,512]{4,3,2,1,0:T(4,128)(2,1)S(1)}, u32[]{:S(2)}, u32[]{:S(2)}) %all-to-all-start.1) | async-done | bytes 1572896 | tf_op jit(solution)/shard_map/all_to_all | solution.py:253
  83.0 0.0 copy-start
  83.0 1.1 copy-done
  84.1 5.2 %apply.1 = bf16[16,4,6,4,512]{4,3,2,1,0:T(4,128)(2,1)} custom-call(bf16[256,256]{1,0:T(8,128)(2,1)} %solve.1.mix_ref, bf16[16,4,6,4,512]{4,3,2,1,0:T(4,128)(2,1)} %copy-done), custom_call_target="tpu_custom_call" | custom-call | tf_op jit(solution)/shard_map/apply/pallas_call | solution.py:233
  89.3 41.1 %all_to_all.16.x_ref = bf16[16,4,6,4,512]{4,3,2,1,0:T(4,128)(2,1)} all-to-all(bf16[16,4,6,4,512]{4,3,2,1,0:T(4,128)(2,1)} %apply.1), channel_id=1, replica_groups=mesh['member'=16,'space'=16] {'member'}, dimensions={0} | all-to-all | bytes 3145728 | tf_op jit(solution)/shard_map/all_to_all | solution.py:263
  130.4 5.4 %join.1 = bf16[4,6,4,8192]{3,2,1,0:T(4,128)(2,1)} custom-call(bf16[16,4,6,4,512]{4,3,2,1,0:T(4,128)(2,1)} %all_to_all.16.x_ref), custom_call_target="tpu_custom_call" | custom-call | tf_op jit(solution)/shard_map/join/pallas_call | solution.py:194
Async XLA Ops:
  11.3 10.4 %collective-permute-start.1 = (f32[8,8,128]{2,1,0:T(8,128)}, f32[8,8,128]{2,1,0:T(8,128)S(1)}, u32[]{:S(2)}, u32[]{:S(2)}) collective-permute-start(f32[8,8,128]{2,1,0:T(8,128)} %observe.1.own_ref), channel_id=1, source_target_pairs={{1,0},{2,1},{3,2},{4,3},{5,4},{6,5},{7,6},{8,7},{9,8},{10,9},{11,1... | collective-permute-start | bytes 98312 | tf_op jit(solution)/shard_map/ppermute | solution.py:257
  19.8 10.2 %collective-permute-start = (f32[8,8,128]{2,1,0:T(8,128)}, f32[8,8,128]{2,1,0:T(8,128)S(1)}, u32[]{:S(2)}, u32[]{:S(2)}) collective-permute-start(f32[8,8,128]{2,1,0:T(8,128)} %observe.1.own_ref), channel_id=1, source_target_pairs={{0,1},{1,2},{2,3},{3,4},{4,5},{5,6},{6,7},{7,8},{8,9},{9,10},{10,1... | collective-permute-start | bytes 98312 | tf_op jit(solution)/shard_map/ppermute | solution.py:256
  21.8 8.3 %copy-start.1 = (f32[8,8,128]{2,1,0:T(8,128)}, f32[8,8,128]{2,1,0:T(8,128)S(1)}, u32[]{:S(2)}) copy-start(f32[8,8,128]{2,1,0:T(8,128)S(1)} %collective-permute-done.1.below_ref) | copy-start | bytes 98308
  30.1 0.6 copy-start.2
  46.7 36.3 %all-to-all-start.1 = ((bf16[16,4,6,4,512]{4,3,2,1,0:T(4,128)(2,1)}), bf16[16,4,6,4,512]{4,3,2,1,0:T(4,128)(2,1)S(1)}, u32[]{:S(2)}, u32[]{:S(2)}) async-start(bf16[16,4,6,4,512]{4,3,2,1,0:T(4,128)(2,1)} %split.1), calls=%async_computation.1 | async-start | bytes 3145728 | tf_op jit(solution)/shard_map/all_to_all | solution.py:253
  83.0 1.1 copy-start

commit v3 on v2

--- a/solution.py
+++ b/solution.py
@@ -13,16 +13,39 @@
 EXACT = lax.Precision.HIGHEST
 
 
+LANES = 128
+
+
 def split_kernel(x_ref, out_ref):
-    share, _, _, _, width = out_ref.shape
-    for h in range(share):
-        out_ref[h] = x_ref[:, :, :, h * width : (h + 1) * width]
+    own, kinds, levels, width = x_ref.shape
+    blocks = width // LANES
+    per = blocks // out_ref.shape[0]
+
+    def body(f, carry):
+        for c in range(blocks):
+            for m in range(own):
+                out_ref[c // per, (f * per + c % per) * own + m] = x_ref[
+                    m, f, :, c * LANES : (c + 1) * LANES
+                ]
+        return carry
+
+    lax.fori_loop(0, kinds, body, 0)
 
 
 def join_kernel(x_ref, out_ref):
-    share, _, _, _, width = x_ref.shape
-    for h in range(share):
-        out_ref[:, :, :, h * width : (h + 1) * width] = x_ref[h]
+    own, kinds, levels, width = out_ref.shape
+    blocks = width // LANES
+    per = blocks // x_ref.shape[0]
+
+    def body(f, carry):
+        for c in range(blocks):
+            for m in range(own):
+                out_ref[m, f, :, c * LANES : (c + 1) * LANES] = x_ref[
+                    c // per, (f * per + c % per) * own + m
+                ]
+        return carry
+
+    lax.fori_loop(0, kinds, body, 0)
 
 
 def observe_kernel(x_ref, value_ref, precision_ref, cell_ref, count_ref, out_ref):
@@ -50,29 +73,36 @@
     out_ref[0, own + 3 : own + 4, :] = col_place
 
 
-def near_kernel(above_ref, own_ref, below_ref, out_ref):
-    parts, _, own, _ = out_ref.shape
+def near_kernel(first, above_ref, own_ref, below_ref, _, out_ref, held, sem):
+    parts, _, own, slots = held.shape
     tiles = own_ref.shape[0]
     share = parts // tiles
     for a, rows_ref in enumerate((above_ref, own_ref, below_ref)):
         for t in range(tiles):
-            rows = rows_ref[t, 0:own, :].astype(out_ref.dtype)
+            rows = rows_ref[t, 0:own, :].astype(held.dtype)
             for b in range(3):
                 for h in range(share):
                     place = t + 1 - b
                     if 0 <= place < tiles:
-                        out_ref[place * share + h, a * 3 + b] = rows
+                        held[place * share + h, a * 3 + b] = rows
+    blank = jnp.zeros((own, slots), held.dtype)
     for h in range(share):
         for a in range(3):
-            blank = jnp.zeros((own, out_ref.shape[-1]), out_ref.dtype)
-            out_ref[h, a * 3] = blank
-            out_ref[(tiles - 1) * share + h, a * 3 + 2] = blank
-
-
-def solve_kernel(levels, where_ref, radius_ref, pred_ref, above_ref, own_ref, below_ref, out_ref):
+            held[h, a * 3] = blank
+            held[(tiles - 1) * share + h, a * 3 + 2] = blank
+    copy = pltpu.make_async_copy(held, out_ref.at[:, pl.ds(first, 9)], sem)
+    copy.start()
+    copy.wait()
+
+
+def analyse_kernel(
+    kinds, where_ref, radius_ref, x_ref, above_ref, own_ref, below_ref, out_ref, mix_ref
+):
     tile = where_ref[0]
     tiles = own_ref.shape[0]
-    sources, _, own, slots = pred_ref.shape
+    sources, _, levels, slots = x_ref.shape
+    own = own_ref.shape[1] - 4
+    first = out_ref.shape[1]
     members = sources * own
     reach = radius_ref[0, tile].astype(jnp.float32)
     centre = 0.5 * TILE_SIDE - 0.5
@@ -93,7 +123,7 @@
             weights.append(jnp.where(inside, active, 0.0) * (taper * taper))
             values.append(value)
             ensemble.append(
-                pred_ref[:, a * 3 + b].astype(jnp.float32).reshape(members, slots)
+                x_ref[:, first + a * 3 + b].astype(jnp.float32).reshape(members, slots)
             )
     ensemble = jnp.concatenate(ensemble, axis=1)
     values = jnp.concatenate(values, axis=1)
@@ -144,14 +174,23 @@
         lax.broadcasted_iota(jnp.int32, (wide, wide), 0) % levels
         == lax.broadcasted_iota(jnp.int32, (wide, wide), 1) % levels
     )
-    out_ref[...] = jnp.where(same, full, 0.0).astype(out_ref.dtype)
-
-
-def apply_kernel(mix_ref, x_ref, out_ref):
-    sources, own, _, levels, width = x_ref.shape
-    rows = x_ref[...].reshape(sources * own * levels, width)
-    mixed = jnp.dot(mix_ref[...], rows, preferred_element_type=jnp.float32)
-    out_ref[...] = mixed.astype(out_ref.dtype).reshape(out_ref.shape)
+    mix_ref[...] = jnp.where(same, full, 0.0).astype(mix_ref.dtype)
+    per = first // (kinds * own)
+
+    def body(f, carry):
+        places = [pl.ds((f * per + c) * own, own) for c in range(per)]
+        rows = jnp.concatenate(
+            [x_ref[:, place].reshape(wide, LANES) for place in places], axis=1
+        )
+        mixed = jnp.dot(mix_ref[...], rows, preferred_element_type=jnp.float32)
+        mixed = mixed.astype(out_ref.dtype)
+        for c, place in enumerate(places):
+            out_ref[:, place] = mixed[:, c * LANES : (c + 1) * LANES].reshape(
+                sources, own, levels, LANES
+            )
+        return carry
+
+    lax.fori_loop(0, kinds, body, 0)
 
 
 def observe(fields, values, precision, cells, count):
@@ -174,70 +213,60 @@
     )(fields, values, precision, cells, count)
 
 
+VMEM = pl.BlockSpec(memory_space=pltpu.VMEM)
+SMEM = pl.BlockSpec(memory_space=pltpu.SMEM)
+ANY = pl.BlockSpec(memory_space=pl.ANY)
+
+
 def split(fields, parts):
     own, kinds, levels, width = fields.shape
-    part = width // parts
-    share = TILE_CELLS // part
+    blocks = own * kinds * (width // parts // LANES)
     return pl.pallas_call(
         split_kernel,
-        grid=(parts // share,),
-        in_specs=[pl.BlockSpec((own, kinds, levels, TILE_CELLS), lambda t: (0, 0, 0, t))],
-        out_specs=pl.BlockSpec((share, own, kinds, levels, part), lambda t: (t, 0, 0, 0, 0)),
-        out_shape=jax.ShapeDtypeStruct((parts, own, kinds, levels, part), fields.dtype),
+        in_specs=[VMEM],
+        out_specs=VMEM,
+        out_shape=jax.ShapeDtypeStruct((parts, blocks + 9, levels, LANES), fields.dtype),
         name="split",
     )(fields)
 
 
-def join(pieces):
-    parts, own, kinds, levels, part = pieces.shape
-    share = TILE_CELLS // part
+def join(pieces, shape):
     return pl.pallas_call(
         join_kernel,
-        grid=(parts // share,),
-        in_specs=[pl.BlockSpec((share, own, kinds, levels, part), lambda t: (t, 0, 0, 0, 0))],
-        out_specs=pl.BlockSpec((own, kinds, levels, TILE_CELLS), lambda t: (0, 0, 0, t)),
-        out_shape=jax.ShapeDtypeStruct((own, kinds, levels, parts * part), pieces.dtype),
+        in_specs=[VMEM],
+        out_specs=VMEM,
+        out_shape=jax.ShapeDtypeStruct(shape, pieces.dtype),
         name="join",
     )(pieces)
 
 
-def surround(above, own, below, parts, members):
-    tiles, _, slots = own.shape
-    vmem = pl.BlockSpec(memory_space=pltpu.VMEM)
-    return pl.pallas_call(
-        near_kernel,
-        in_specs=[vmem, vmem, vmem],
-        out_specs=vmem,
-        out_shape=jax.ShapeDtypeStruct((parts, 9, members, slots), jnp.bfloat16),
+def surround(above, own, below, pieces):
+    parts, blocks, levels, slots = pieces.shape
+    return pl.pallas_call(
+        functools.partial(near_kernel, blocks - 9),
+        in_specs=[VMEM, VMEM, VMEM, ANY],
+        out_specs=ANY,
+        out_shape=jax.ShapeDtypeStruct(pieces.shape, pieces.dtype),
+        scratch_shapes=[
+            pltpu.VMEM((parts, 9, own.shape[1] - 4, slots), pieces.dtype),
+            pltpu.SemaphoreType.DMA,
+        ],
+        input_output_aliases={3: 0},
         name="surround",
-    )(above, own, below)
-
-
-def solve(tile, radius, pred, above, own, below, levels):
-    members = pred.shape[0] * pred.shape[2]
-    wide = members * levels
-    vmem = pl.BlockSpec(memory_space=pltpu.VMEM)
-    smem = pl.BlockSpec(memory_space=pltpu.SMEM)
-    return pl.pallas_call(
-        functools.partial(solve_kernel, levels),
-        in_specs=[smem, smem, vmem, vmem, vmem, vmem],
-        out_specs=vmem,
-        out_shape=jax.ShapeDtypeStruct((wide, wide), jnp.bfloat16),
-        name="solve",
-    )(tile, radius, pred, above, own, below)
-
-
-def apply_mixing(mix, pieces):
-    parts, own, count, levels, part = pieces.shape
-    block = pl.BlockSpec((parts, own, 1, levels, part), lambda f: (0, 0, f, 0, 0))
-    return pl.pallas_call(
-        apply_kernel,
-        grid=(count,),
-        in_specs=[pl.BlockSpec(mix.shape, lambda f: (0, 0)), block],
-        out_specs=block,
-        out_shape=jax.ShapeDtypeStruct(pieces.shape, pieces.dtype),
-        name="apply",
-    )(mix, pieces)
+    )(above, own, below, pieces)
+
+
+def analyse(tile, radius, pieces, above, own, below, kinds):
+    parts, blocks, levels, lanes = pieces.shape
+    wide = parts * (own.shape[1] - 4) * levels
+    return pl.pallas_call(
+        functools.partial(analyse_kernel, kinds),
+        in_specs=[SMEM, SMEM, VMEM, VMEM, VMEM, VMEM],
+        out_specs=VMEM,
+        out_shape=jax.ShapeDtypeStruct((parts, blocks - 9, levels, lanes), pieces.dtype),
+        scratch_shapes=[pltpu.VMEM((wide, wide), jnp.bfloat16)],
+        name="analyse",
+    )(tile, radius, pieces, above, own, below)
 
 
 def on_device(background, obs_values, obs_precision, obs_cell, obs_count, radius):
@@ -248,20 +277,14 @@
     down = [(i, i + 1) for i in range(rows - 1)]
     up = [(i + 1, i) for i in range(rows - 1)]
     fields = background.transpose(0, 2, 3, 1, 4).reshape(own, kinds, levels, width)
-    pieces = split(fields, parts)
-    pieces, fields = lax.optimization_barrier((pieces, fields))
-    sent = lax.all_to_all(pieces, "member", 0, 0)
-
     here = observe(fields, obs_values[0], obs_precision[0], obs_cell[0], obs_count)
     above = lax.ppermute(here, "space", down)
     below = lax.ppermute(here, "space", up)
-    near = lax.all_to_all(surround(above, here, below, parts, own), "member", 0, 0)
+    pieces = surround(above, here, below, split(fields, parts))
+    sent = lax.all_to_all(pieces, "member", 0, 0)
     tile = (lax.axis_index("member") // share).astype(jnp.int32).reshape(1)
-    mix = solve(tile, radius, near, above, here, below, levels)
-
-    mixed = apply_mixing(mix, sent)
-    back = lax.all_to_all(mixed, "member", 0, 0)
-    out = join(back)
+    mixed = analyse(tile, radius, sent, above, here, below, kinds)
+    out = join(lax.all_to_all(mixed, "member", 0, 0), fields.shape)
     return out.reshape(own, kinds, 1, levels, width).transpose(0, 3, 1, 2, 4)
 
 

time: 137 us -> 128 us (0.934)
  blocking collectives: 55.6 us -> 42.9 us
  waiting for transfers between devices: 35.9 us -> 44.5 us
  Pallas kernels: 28.3 us -> 21.2 us
  starting transfers between devices: 14.1 us -> 16.4 us
    all_to_all x2 -> x1, blocking collectives: 55.6 us -> 42.9 us  [on_device(): out = join(lax.all_to_all(mixed, 'member', 0, 0), fields.shape)]
    all_to_all x1, waiting for transfers between devices: 27.6 us -> 39.3 us  [on_device(): sent = lax.all_to_all(pieces, 'member', 0, 0)]
    pallas_call x5 -> x4, Pallas kernels: 22.4 us -> 15.3 us  [the longest x1 7.48 us: analyse(): pl.pallas_call(functools.partial(analyse_kernel, kinds), in_specs=[SMEM,...]
    ppermute x1, waiting for transfers between devices: 8.3 us -> 5.12 us  [on_device(): above = lax.ppermute(here, 'space', down)]
    all_to_all x1, starting transfers between devices: 3.71 us -> 5.95 us  [on_device(): sent = lax.all_to_all(pieces, 'member', 0, 0)]
  transfers between devices with their start and end apart: 3 -> 3, of which waited for: 2 -> 2; matrix products, arithmetic and copies ran while one was open for 0% -> 0% of each run, Pallas kernels for 4% -> 3%
where the time goes in v3:
time: 128 us; the launch traced here: 127 us
  waiting for transfers between devices  44.5 us (35%)
  blocking collectives  42.9 us (34%)
  Pallas kernels  21.2 us (17%)
  starting transfers between devices  16.4 us (13%)
  local copies, waits for them, and re-layouts  1.83 us (1%)
    all_to_all x1, blocking collectives, on_device(): out = join(lax.all_to_all(mixed, 'member', 0, 0), fields.shape)  42.9 us
    all_to_all x1, waiting for transfers between devices, on_device(): sent = lax.all_to_all(pieces, 'member', 0, 0)  39.3 us
    ppermute x1, starting transfers between devices, on_device(): below = lax.ppermute(here, 'space', up)  8.5 us
    pallas_call x1, Pallas kernels, analyse(): pl.pallas_call(functools.partial(analyse_kernel, kinds), in_specs=[SMEM,...  7.48 us
    all_to_all x1, starting transfers between devices, on_device(): sent = lax.all_to_all(pieces, 'member', 0, 0)  5.95 us
    pallas_call x1, Pallas kernels, observe(): pl.pallas_call(observe_kernel, grid=(tiles,), in_specs=[pl.BlockSpec((own...  5.92 us
    ppermute x1, waiting for transfers between devices, on_device(): above = lax.ppermute(here, 'space', down)  5.12 us
    pallas_call x1, Pallas kernels, split(): pl.pallas_call(split_kernel, in_specs=[VMEM], out_specs=VMEM, out_shape=j...  3.19 us
  transfers between devices with their start and end apart: 3, of which 2 were waited for; matrix products, arithmetic and copies ran while one was open for 0% of the time, Pallas kernels for 3%

profile of v3, /device:TPU:2, one launch (start us, length us, event | category | flops | bytes accessed | tf_op | source)
XLA Modules:
  0.0 126.8 jit_solution(17372713718329074006)
XLA Ops:
  0.0 5.9 %observe.1.own_ref = f32[8,8,128]{2,1,0:T(8,128)} custom-call(bf16[4,6,4,8192]{3,2,1,0:T(4,128)(2,1)} %bitcast.14, f32[8,128]{1,0:T(8,128)} %bitcast.16, f32[8,128]{1,0:T(8,128)} %bitcast.17, s32[8,128]{1,0:T(8,128)} %bitcast.18, s32[1,8]{1,0:T(1,128)} %count_ref.1), custom_call_target="tpu_custom_call" | custom-call | tf_op jit(solution)/shard_map/observe/pallas_call | solution.py:200
  5.9 8.5 %collective-permute-start.1 = (f32[8,8,128]{2,1,0:T(8,128)}, f32[8,8,128]{2,1,0:T(8,128)S(1)}, u32[]{:S(2)}, u32[]{:S(2)}) collective-permute-start(f32[8,8,128]{2,1,0:T(8,128)} %observe.1.own_ref), channel_id=1, source_target_pairs={{1,0},{2,1},{3,2},{4,3},{5,4},{6,5},{7,6},{8,7},{9,8},{10,9},{11,1... | collective-permute-start | bytes 98312 | tf_op jit(solution)/shard_map/ppermute | solution.py:282
  14.4 1.9 %collective-permute-start = (f32[8,8,128]{2,1,0:T(8,128)}, f32[8,8,128]{2,1,0:T(8,128)S(1)}, u32[]{:S(2)}, u32[]{:S(2)}) collective-permute-start(f32[8,8,128]{2,1,0:T(8,128)} %observe.1.own_ref), channel_id=1, source_target_pairs={{0,1},{1,2},{2,3},{3,4},{4,5},{5,6},{6,7},{7,8},{8,9},{9,10},{10,1... | collective-permute-start | bytes 98312 | tf_op jit(solution)/shard_map/ppermute | solution.py:281
  16.3 3.2 %split.1._ = bf16[16,105,4,128]{3,2,1,0:T(4,128)(2,1)} custom-call(bf16[4,6,4,8192]{3,2,1,0:T(4,128)(2,1)} %bitcast.15), custom_call_target="tpu_custom_call" | custom-call | tf_op jit(solution)/shard_map/split/pallas_call | solution.py:224
  19.5 0.0 collective-permute-done.1.below_ref
  19.5 0.0 copy-start.1
  19.5 5.1 %collective-permute-done.above_ref = f32[8,8,128]{2,1,0:T(8,128)S(1)} collective-permute-done((f32[8,8,128]{2,1,0:T(8,128)}, f32[8,8,128]{2,1,0:T(8,128)S(1)}, u32[]{:S(2)}, u32[]{:S(2)}) %collective-permute-start) | collective-permute-done | bytes 32800 | tf_op jit(solution)/shard_map/ppermute | solution.py:281
  24.7 0.0 copy-done.1
  24.7 0.0 copy-start.2
  24.7 0.6 copy-done.2
  25.3 1.5 %surround.1 = bf16[16,105,4,128]{3,2,1,0:T(4,128)(2,1)} custom-call(f32[8,8,128]{2,1,0:T(8,128)} %copy-done.2, f32[8,8,128]{2,1,0:T(8,128)} %observe.1.own_ref, f32[8,8,128]{2,1,0:T(8,128)} %copy-done.1, bf16[16,105,4,128]{3,2,1,0:T(4,128)(2,1)} %split.1._), custom_call_target="tpu_custom_call", output_to_operand_aliasing={{}: (3, {})} | custom-call | tf_op jit(solution)/shard_map/surround/pallas_call | solution.py:245
  26.8 6.0 %all-to-all-start = ((bf16[16,105,4,128]{3,2,1,0:T(4,128)(2,1)}), bf16[16,105,4,128]{3,2,1,0:T(4,128)(2,1)S(1)}, u32[]{:S(2)}, u32[]{:S(2)}) async-start(bf16[16,105,4,128]{3,2,1,0:T(4,128)(2,1)} %surround.1), calls=%async_computation | async-start | bytes 3440640 | tf_op jit(solution)/shard_map/all_to_all | solution.py:284
  32.8 39.3 %all-to-all-done.x_ref = bf16[16,105,4,128]{3,2,1,0:T(4,128)(2,1)S(1)} async-done(((bf16[16,105,4,128]{3,2,1,0:T(4,128)(2,1)}), bf16[16,105,4,128]{3,2,1,0:T(4,128)(2,1)S(1)}, u32[]{:S(2)}, u32[]{:S(2)}) %all-to-all-start) | async-done | bytes 1720352 | tf_op jit(solution)/shard_map/all_to_all | solution.py:284
  72.1 0.0 copy-start
  72.1 1.2 copy-done
  73.3 7.5 %analyse.1 = bf16[16,96,4,128]{3,2,1,0:T(4,128)(2,1)} custom-call(s32[1]{0:T(128)} %bitcast.where_ref, s32[1,8]{1,0:T(1,128)} %radius_ref.1, bf16[16,105,4,128]{3,2,1,0:T(4,128)(2,1)} %copy-done, f32[8,8,128]{2,1,0:T(8,128)} %copy-done.2, f32[8,8,128]{2,1,0:T(8,128)} %observe.1.own_ref, f32[8,8,128]{2,1,0:T(8,128)} %copy-done.1), custom_call_target="tpu_custom_call" | custom-call | tf_op jit(solution)/shard_map/analyse/pallas_call | solution.py:262
  80.8 42.9 %all_to_all.10.x_ref = bf16[16,96,4,128]{3,2,1,0:T(4,128)(2,1)} all-to-all(bf16[16,96,4,128]{3,2,1,0:T(4,128)(2,1)} %analyse.1), channel_id=1, replica_groups=mesh['member'=16,'space'=16] {'member'}, dimensions={0} | all-to-all | bytes 3145728 | tf_op jit(solution)/shard_map/all_to_all | solution.py:287
  123.7 3.1 %join.1 = bf16[4,6,4,8192]{3,2,1,0:T(4,128)(2,1)} custom-call(bf16[16,96,4,128]{3,2,1,0:T(4,128)(2,1)} %all_to_all.10.x_ref), custom_call_target="tpu_custom_call" | custom-call | tf_op jit(solution)/shard_map/join/pallas_call | solution.py:234
Async XLA Ops:
  5.9 13.6 %collective-permute-start.1 = (f32[8,8,128]{2,1,0:T(8,128)}, f32[8,8,128]{2,1,0:T(8,128)S(1)}, u32[]{:S(2)}, u32[]{:S(2)}) collective-permute-start(f32[8,8,128]{2,1,0:T(8,128)} %observe.1.own_ref), channel_id=1, source_target_pairs={{1,0},{2,1},{3,2},{4,3},{5,4},{6,5},{7,6},{8,7},{9,8},{10,9},{11,1... | collective-permute-start | bytes 98312 | tf_op jit(solution)/shard_map/ppermute | solution.py:282
  14.4 10.2 %collective-permute-start = (f32[8,8,128]{2,1,0:T(8,128)}, f32[8,8,128]{2,1,0:T(8,128)S(1)}, u32[]{:S(2)}, u32[]{:S(2)}) collective-permute-start(f32[8,8,128]{2,1,0:T(8,128)} %observe.1.own_ref), channel_id=1, source_target_pairs={{0,1},{1,2},{2,3},{3,4},{4,5},{5,6},{6,7},{7,8},{8,9},{9,10},{10,1... | collective-permute-start | bytes 98312 | tf_op jit(solution)/shard_map/ppermute | solution.py:281
  19.5 5.1 %copy-start.1 = (f32[8,8,128]{2,1,0:T(8,128)}, f32[8,8,128]{2,1,0:T(8,128)S(1)}, u32[]{:S(2)}) copy-start(f32[8,8,128]{2,1,0:T(8,128)S(1)} %collective-permute-done.1.below_ref) | copy-start | bytes 98308
  24.7 0.6 copy-start.2
  26.8 45.3 %all-to-all-start = ((bf16[16,105,4,128]{3,2,1,0:T(4,128)(2,1)}), bf16[16,105,4,128]{3,2,1,0:T(4,128)(2,1)S(1)}, u32[]{:S(2)}, u32[]{:S(2)}) async-start(bf16[16,105,4,128]{3,2,1,0:T(4,128)(2,1)} %surround.1), calls=%async_computation | async-start | bytes 3440640 | tf_op jit(solution)/shard_map/all_to_all | solution.py:284
  72.1 1.2 copy-start

commit v4 on v3

--- a/solution.py
+++ b/solution.py
@@ -14,22 +14,30 @@
 
 
 LANES = 128
-
-
-def split_kernel(x_ref, out_ref):
-    own, kinds, levels, width = x_ref.shape
+VMEM = pl.BlockSpec(memory_space=pltpu.VMEM)
+SMEM = pl.BlockSpec(memory_space=pltpu.SMEM)
+PARAMS = pltpu.CompilerParams(vmem_limit_bytes=16 * 1024 * 1024)
+EARLY = 3
+
+
+def copy_blocks(x_ref, out_ref, begin, end):
+    own, _, _, width = x_ref.shape
     blocks = width // LANES
     per = blocks // out_ref.shape[0]
 
     def body(f, carry):
         for c in range(blocks):
             for m in range(own):
-                out_ref[c // per, (f * per + c % per) * own + m] = x_ref[
+                out_ref[c // per, ((f - begin) * per + c % per) * own + m] = x_ref[
                     m, f, :, c * LANES : (c + 1) * LANES
                 ]
         return carry
 
-    lax.fori_loop(0, kinds, body, 0)
+    lax.fori_loop(begin, end, body, 0)
+
+
+def split_kernel(end, x_ref, out_ref):
+    copy_blocks(x_ref, out_ref, 0, end)
 
 
 def join_kernel(x_ref, out_ref):
@@ -73,36 +81,36 @@
     out_ref[0, own + 3 : own + 4, :] = col_place
 
 
-def near_kernel(first, above_ref, own_ref, below_ref, _, out_ref, held, sem):
-    parts, _, own, slots = held.shape
+def pack_kernel(begin, x_ref, above_ref, own_ref, below_ref, out_ref):
+    copy_blocks(x_ref, out_ref, begin, x_ref.shape[1])
+    parts, blocks, own, slots = out_ref.shape
+    first = blocks - 9
     tiles = own_ref.shape[0]
     share = parts // tiles
     for a, rows_ref in enumerate((above_ref, own_ref, below_ref)):
         for t in range(tiles):
-            rows = rows_ref[t, 0:own, :].astype(held.dtype)
+            rows = rows_ref[t, 0:own, :].astype(out_ref.dtype)
             for b in range(3):
                 for h in range(share):
                     place = t + 1 - b
                     if 0 <= place < tiles:
-                        held[place * share + h, a * 3 + b] = rows
-    blank = jnp.zeros((own, slots), held.dtype)
+                        out_ref[place * share + h, first + a * 3 + b] = rows
+    blank = jnp.zeros((own, slots), out_ref.dtype)
     for h in range(share):
         for a in range(3):
-            held[h, a * 3] = blank
-            held[(tiles - 1) * share + h, a * 3 + 2] = blank
-    copy = pltpu.make_async_copy(held, out_ref.at[:, pl.ds(first, 9)], sem)
-    copy.start()
-    copy.wait()
+            out_ref[h, first + a * 3] = blank
+            out_ref[(tiles - 1) * share + h, first + a * 3 + 2] = blank
 
 
 def analyse_kernel(
-    kinds, where_ref, radius_ref, x_ref, above_ref, own_ref, below_ref, out_ref, mix_ref
+    kinds, where_ref, radius_ref, early_ref, x_ref, above_ref, own_ref, below_ref, out_ref, mix_ref
 ):
     tile = where_ref[0]
     tiles = own_ref.shape[0]
     sources, _, levels, slots = x_ref.shape
     own = own_ref.shape[1] - 4
-    first = out_ref.shape[1]
+    ahead = early_ref.shape[1]
+    first = x_ref.shape[1] - 9
     members = sources * own
     reach = radius_ref[0, tile].astype(jnp.float32)
     centre = 0.5 * TILE_SIDE - 0.5
@@ -175,22 +183,30 @@
         == lax.broadcasted_iota(jnp.int32, (wide, wide), 1) % levels
     )
     mix_ref[...] = jnp.where(same, full, 0.0).astype(mix_ref.dtype)
-    per = first // (kinds * own)
-
-    def body(f, carry):
-        places = [pl.ds((f * per + c) * own, own) for c in range(per)]
-        rows = jnp.concatenate(
-            [x_ref[:, place].reshape(wide, LANES) for place in places], axis=1
-        )
-        mixed = jnp.dot(mix_ref[...], rows, preferred_element_type=jnp.float32)
-        mixed = mixed.astype(out_ref.dtype)
-        for c, place in enumerate(places):
-            out_ref[:, place] = mixed[:, c * LANES : (c + 1) * LANES].reshape(
-                sources, own, levels, LANES
+    per = out_ref.shape[1] // (kinds * own)
+
+    def mix_fields(from_ref, offset):
+        def body(f, carry):
+            begin = f * per * own
+            rows = jnp.concatenate(
+                [
+                    from_ref[:, pl.ds(begin + c * own, own)].reshape(wide, LANES)
+                    for c in range(per)
+                ],
+                axis=1,
             )
-        return carry
-
-    lax.fori_loop(0, kinds, body, 0)
+            mixed = jnp.dot(mix_ref[...], rows, preferred_element_type=jnp.float32)
+            mixed = mixed.astype(out_ref.dtype)
+            for c in range(per):
+                out_ref[:, pl.ds(offset + begin + c * own, own)] = mixed[
+                    :, c * LANES : (c + 1) * LANES
+                ].reshape(sources, own, levels, LANES)
+            return carry
+
+        return body
+
+    lax.fori_loop(0, ahead // (per * own), mix_fields(early_ref, 0), 0)
+    lax.fori_loop(0, first // (per * own), mix_fields(x_ref, ahead), 0)
 
 
 def observe(fields, values, precision, cells, count):
@@ -209,23 +225,20 @@
         ],
         out_specs=pl.BlockSpec((1, own + 4, slots), lambda t: (t, 0, 0)),
         out_shape=jax.ShapeDtypeStruct((tiles, own + 4, slots), jnp.float32),
+        compiler_params=PARAMS,
         name="observe",
     )(fields, values, precision, cells, count)
 
 
-VMEM = pl.BlockSpec(memory_space=pltpu.VMEM)
-SMEM = pl.BlockSpec(memory_space=pltpu.SMEM)
-ANY = pl.BlockSpec(memory_space=pl.ANY)
-
-
-def split(fields, parts):
+def split(fields, parts, end):
     own, kinds, levels, width = fields.shape
-    blocks = own * kinds * (width // parts // LANES)
-    return pl.pallas_call(
-        split_kernel,
+    blocks = own * end * (width // parts // LANES)
+    return pl.pallas_call(
+        functools.partial(split_kernel, end),
         in_specs=[VMEM],
         out_specs=VMEM,
-        out_shape=jax.ShapeDtypeStruct((parts, blocks + 9, levels, LANES), fields.dtype),
+        out_shape=jax.ShapeDtypeStruct((parts, blocks, levels, LANES), fields.dtype),
+        compiler_params=PARAMS,
         name="split",
     )(fields)
 
@@ -236,37 +249,37 @@
         in_specs=[VMEM],
         out_specs=VMEM,
         out_shape=jax.ShapeDtypeStruct(shape, pieces.dtype),
+        compiler_params=PARAMS,
         name="join",
     )(pieces)
 
 
-def surround(above, own, below, pieces):
-    parts, blocks, levels, slots = pieces.shape
-    return pl.pallas_call(
-        functools.partial(near_kernel, blocks - 9),
-        in_specs=[VMEM, VMEM, VMEM, ANY],
-        out_specs=ANY,
-        out_shape=jax.ShapeDtypeStruct(pieces.shape, pieces.dtype),
-        scratch_shapes=[
-            pltpu.VMEM((parts, 9, own.shape[1] - 4, slots), pieces.dtype),
-            pltpu.SemaphoreType.DMA,
-        ],
-        input_output_aliases={3: 0},
-        name="surround",
-    )(above, own, below, pieces)
-
-
-def analyse(tile, radius, pieces, above, own, below, kinds):
-    parts, blocks, levels, lanes = pieces.shape
-    wide = parts * (own.shape[1] - 4) * levels
+def pack(fields, parts, begin, above, here, below):
+    own, kinds, levels, width = fields.shape
+    blocks = own * (kinds - begin) * (width // parts // LANES) + 9
+    return pl.pallas_call(
+        functools.partial(pack_kernel, begin),
+        in_specs=[VMEM] * 4,
+        out_specs=VMEM,
+        out_shape=jax.ShapeDtypeStruct((parts, blocks, levels, LANES), fields.dtype),
+        compiler_params=PARAMS,
+        name="pack",
+    )(fields, above, here, below)
+
+
+def analyse(tile, radius, early, late, above, here, below, kinds):
+    parts, blocks, levels, lanes = early.shape
+    wide = parts * (here.shape[1] - 4) * levels
+    blocks += late.shape[1] - 9
     return pl.pallas_call(
         functools.partial(analyse_kernel, kinds),
-        in_specs=[SMEM, SMEM, VMEM, VMEM, VMEM, VMEM],
+        in_specs=[SMEM, SMEM] + [VMEM] * 5,
         out_specs=VMEM,
-        out_shape=jax.ShapeDtypeStruct((parts, blocks - 9, levels, lanes), pieces.dtype),
+        out_shape=jax.ShapeDtypeStruct((parts, blocks, levels, lanes), early.dtype),
         scratch_shapes=[pltpu.VMEM((wide, wide), jnp.bfloat16)],
+        compiler_params=PARAMS,
         name="analyse",
-    )(tile, radius, pieces, above, own, below)
+    )(tile, radius, early, late, above, here, below)
 
 
 def on_device(background, obs_values, obs_precision, obs_cell, obs_count, radius):
@@ -277,13 +290,16 @@
     down = [(i, i + 1) for i in range(rows - 1)]
     up = [(i + 1, i) for i in range(rows - 1)]
     fields = background.transpose(0, 2, 3, 1, 4).reshape(own, kinds, levels, width)
+    early = split(fields, parts, EARLY)
+    early, fields = lax.optimization_barrier((early, fields))
+    early = lax.all_to_all(early, "member", 0, 0)
     here = observe(fields, obs_values[0], obs_precision[0], obs_cell[0], obs_count)
     above = lax.ppermute(here, "space", down)
     below = lax.ppermute(here, "space", up)
-    pieces = surround(above, here, below, split(fields, parts))
-    sent = lax.all_to_all(pieces, "member", 0, 0)
+    late = pack(fields, parts, EARLY, above, here, below)
+    late = lax.all_to_all(late, "member", 0, 0)
     tile = (lax.axis_index("member") // share).astype(jnp.int32).reshape(1)
-    mixed = analyse(tile, radius, sent, above, here, below, kinds)
+    mixed = analyse(tile, radius, early, late, above, here, below, kinds)
     out = join(lax.all_to_all(mixed, "member", 0, 0), fields.shape)
     return out.reshape(own, kinds, 1, levels, width).transpose(0, 3, 1, 2, 4)
 

time: 128 us -> 114 us (0.89)
  Pallas kernels: 21.2 us -> 12.1 us
  waiting for transfers between devices: 44.5 us -> 38.1 us
  starting transfers between devices: 16.4 us -> 19.8 us
    all_to_all x1 -> x2, waiting for transfers between devices: 39.3 us -> 29.6 us  [the longest x1 25.9 us: on_device(): late = lax.all_to_all(late, 'member', 0, 0)]
    all_to_all x1 -> x2, starting transfers between devices: 5.95 us -> 12.4 us  [the longest x1 8.64 us: on_device(): early = lax.all_to_all(early, 'member', 0, 0)]
    ppermute x1, waiting for transfers between devices: 0.01 us -> 3.38 us  [on_device(): below = lax.ppermute(here, 'space', up)]
    pallas_call x1, Pallas kernels: 5.92 us -> 2.57 us  [observe(): pl.pallas_call(observe_kernel, grid=(tiles,), in_specs=[pl.BlockSpec((own...]
    ppermute x1, starting transfers between devices: 8.5 us -> 5.53 us  [on_device(): below = lax.ppermute(here, 'space', up)]
    pallas_call x2, Pallas kernels: 4.7 us -> 2.41 us  [the longest x1 1.24 us: pack(): pl.pallas_call(functools.partial(pack_kernel, begin), in_specs=[VMEM] * 4...]
    pallas_call x1, Pallas kernels: 7.48 us -> 5.39 us  [analyse(): pl.pallas_call(functools.partial(analyse_kernel, kinds), in_specs=[SMEM,...]
    pallas_call x1, Pallas kernels: 3.12 us -> 1.71 us  [join(): pl.pallas_call(join_kernel, in_specs=[VMEM], out_specs=VMEM, out_shape=ja...]
  transfers between devices with their start and end apart: 3 -> 4, of which waited for: 2 -> 4; matrix products, arithmetic and copies ran while one was open for 0% -> 0% of each run, Pallas kernels for 3% -> 3%
where the time goes in v4:
time: 114 us
  blocking collectives  42.3 us (37%)
  waiting for transfers between devices  38.1 us (33%)
  starting transfers between devices  19.8 us (17%)
  Pallas kernels  12.1 us (11%)
  local copies, waits for them, and re-layouts  1.43 us (1%)
    all_to_all x1, blocking collectives, on_device(): out = join(lax.all_to_all(mixed, 'member', 0, 0), fields.shape)  42.3 us
    all_to_all x1, waiting for transfers between devices, on_device(): late = lax.all_to_all(late, 'member', 0, 0)  25.9 us
    all_to_all x1, starting transfers between devices, on_device(): early = lax.all_to_all(early, 'member', 0, 0)  8.64 us
    ppermute x1, starting transfers between devices, on_device(): below = lax.ppermute(here, 'space', up)  5.53 us
    pallas_call x1, Pallas kernels, analyse(): pl.pallas_call(functools.partial(analyse_kernel, kinds), in_specs=[SMEM,...  5.39 us
    ppermute x1, waiting for transfers between devices, on_device(): above = lax.ppermute(here, 'space', down)  5.12 us
    all_to_all x1, starting transfers between devices, on_device(): late = lax.all_to_all(late, 'member', 0, 0)  3.76 us
    all_to_all x1, waiting for transfers between devices, on_device(): early = lax.all_to_all(early, 'member', 0, 0)  3.73 us
  transfers between devices with their start and end apart: 4, of which 4 were waited for; matrix products, arithmetic and copies ran while one was open for 0% of the time, Pallas kernels for 3%

profile of v4, /device:TPU:2, one launch (start us, length us, event | category | flops | bytes accessed | tf_op | source)
XLA Modules:
  0.0 113.9 jit_solution(6105465759378892661)
XLA Ops:
  0.0 0.0 copy-start
  0.0 1.4 %copy-done = bf16[4,4,6,1,8192]{4,1,3,2,0:T(4,128)(2,1)S(1)} copy-done((bf16[4,4,6,1,8192]{4,1,3,2,0:T(4,128)(2,1)S(1)}, bf16[4,4,6,1,8192]{4,1,3,2,0:T(4,128)(2,1)}, u32[]{:S(2)}) %copy-start) | copy-done | bytes 1572888
  1.4 0.0 copy-start.1
  1.4 0.0 copy-start.2
  1.4 0.0 copy-start.3
  1.4 0.0 copy-start.4
  1.4 0.0 copy-start.5
  1.4 1.2 %split.1 = bf16[16,48,4,128]{3,2,1,0:T(4,128)(2,1)} custom-call(bf16[4,6,4,8192]{3,2,1,0:T(4,128)(2,1)S(1)} %bitcast.14), custom_call_target="tpu_custom_call" | custom-call | tf_op jit(solution)/shard_map/split/pallas_call | solution.py:236
  2.6 8.6 %all-to-all-start = ((bf16[16,48,4,128]{3,2,1,0:T(4,128)(2,1)}), bf16[16,48,4,128]{3,2,1,0:T(4,128)(2,1)S(1)}, u32[]{:S(2)}, u32[]{:S(2)}) async-start(bf16[16,48,4,128]{3,2,1,0:T(4,128)(2,1)} %split.1), calls=%async_computation | async-start | bytes 1572864 | tf_op jit(solution)/shard_map/all_to_all | solution.py:295
  11.2 0.0 copy-done.1
  11.3 0.0 copy-done.2
  11.3 0.0 copy-done.3
  11.3 0.0 copy-done.4
  11.3 0.0 copy-done.5
  11.3 2.6 %observe.1.own_ref = f32[8,8,128]{2,1,0:T(8,128)S(1)} custom-call(bf16[4,6,4,8192]{3,2,1,0:T(4,128)(2,1)S(1)} %bitcast.15, f32[8,128]{1,0:T(8,128)S(1)} %bitcast.17, f32[8,128]{1,0:T(8,128)S(1)} %bitcast.18, s32[8,128]{1,0:T(8,128)S(1)} %bitcast.19, s32[1,8]{1,0:T(1,128)S(1)} %copy-done.5), custom_call_target="tpu_custom_call" | custom-call | tf_op jit(solution)/shard_map/observe/pallas_call | solution.py:216
  13.9 5.5 %collective-permute-start.1 = (f32[8,8,128]{2,1,0:T(8,128)S(1)}, f32[8,8,128]{2,1,0:T(8,128)S(1)}, u32[]{:S(2)}, u32[]{:S(2)}) collective-permute-start(f32[8,8,128]{2,1,0:T(8,128)S(1)} %observe.1.own_ref), channel_id=1, source_target_pairs={{1,0},{2,1},{3,2},{4,3},{5,4},{6,5},{7,6},{8,7},{9,8},{10,9},{11,1... | collective-permute-start | bytes 98312 | tf_op jit(solution)/shard_map/ppermute | solution.py:298
  19.4 1.9 %collective-permute-start = (f32[8,8,128]{2,1,0:T(8,128)S(1)}, f32[8,8,128]{2,1,0:T(8,128)S(1)}, u32[]{:S(2)}, u32[]{:S(2)}) collective-permute-start(f32[8,8,128]{2,1,0:T(8,128)S(1)} %observe.1.own_ref), channel_id=1, source_target_pairs={{0,1},{1,2},{2,3},{3,4},{4,5},{5,6},{6,7},{7,8},{8,9},{9,10},{10,1... | collective-permute-start | bytes 98312 | tf_op jit(solution)/shard_map/ppermute | solution.py:297
  21.3 3.4 %collective-permute-done.1.below_ref = f32[8,8,128]{2,1,0:T(8,128)S(1)} collective-permute-done((f32[8,8,128]{2,1,0:T(8,128)S(1)}, f32[8,8,128]{2,1,0:T(8,128)S(1)}, u32[]{:S(2)}, u32[]{:S(2)}) %collective-permute-start.1) | collective-permute-done | bytes 32800 | tf_op jit(solution)/shard_map/ppermute | solution.py:298
  24.7 5.1 %collective-permute-done.above_ref = f32[8,8,128]{2,1,0:T(8,128)S(1)} collective-permute-done((f32[8,8,128]{2,1,0:T(8,128)S(1)}, f32[8,8,128]{2,1,0:T(8,128)S(1)}, u32[]{:S(2)}, u32[]{:S(2)}) %collective-permute-start) | collective-permute-done | bytes 32800 | tf_op jit(solution)/shard_map/ppermute | solution.py:297
  29.8 1.2 %pack.1 = bf16[16,57,4,128]{3,2,1,0:T(4,128)(2,1)} custom-call(bf16[4,6,4,8192]{3,2,1,0:T(4,128)(2,1)S(1)} %bitcast.16, f32[8,8,128]{2,1,0:T(8,128)S(1)} %collective-permute-done.above_ref, f32[8,8,128]{2,1,0:T(8,128)S(1)} %observe.1.own_ref, f32[8,8,128]{2,1,0:T(8,128)S(1)} %collective-permute-done.1.below_ref), custom_call_target="tpu_custom_call" | custom-call | tf_op jit(solution)/shard_map/pack/pallas_call | solution.py:260
  31.1 0.0 copy-start.6
  31.1 3.7 %all-to-all-done.early_ref = bf16[16,48,4,128]{3,2,1,0:T(4,128)(2,1)S(1)} async-done(((bf16[16,48,4,128]{3,2,1,0:T(4,128)(2,1)}), bf16[16,48,4,128]{3,2,1,0:T(4,128)(2,1)S(1)}, u32[]{:S(2)}, u32[]{:S(2)}) %all-to-all-start) | async-done | bytes 786464 | tf_op jit(solution)/shard_map/all_to_all | solution.py:295
  34.8 3.8 %all-to-all-start.1 = ((bf16[16,57,4,128]{3,2,1,0:T(4,128)(2,1)}), bf16[16,57,4,128]{3,2,1,0:T(4,128)(2,1)S(1)}, u32[]{:S(2)}, u32[]{:S(2)}) async-start(bf16[16,57,4,128]{3,2,1,0:T(4,128)(2,1)} %pack.1), calls=%async_computation.1 | async-start | bytes 1867776 | tf_op jit(solution)/shard_map/all_to_all | solution.py:300
  38.6 25.9 %all-to-all-done.1.x_ref = bf16[16,57,4,128]{3,2,1,0:T(4,128)(2,1)S(1)} async-done(((bf16[16,57,4,128]{3,2,1,0:T(4,128)(2,1)}), bf16[16,57,4,128]{3,2,1,0:T(4,128)(2,1)S(1)}, u32[]{:S(2)}, u32[]{:S(2)}) %all-to-all-start.1) | async-done | bytes 933920 | tf_op jit(solution)/shard_map/all_to_all | solution.py:300
  64.5 0.0 copy-done.6
  64.5 5.4 %analyse.1 = bf16[16,96,4,128]{3,2,1,0:T(4,128)(2,1)S(1)} custom-call(s32[1]{0:T(128)} %bitcast.where_ref, s32[1,8]{1,0:T(1,128)S(1)} %copy-done.6, bf16[16,48,4,128]{3,2,1,0:T(4,128)(2,1)S(1)} %all-to-all-done.early_ref, bf16[16,57,4,128]{3,2,1,0:T(4,128)(2,1)S(1)} %all-to-all-done.1.x_ref, f32[8,8,128]{2,1,0:T(8,128)S(1)} %collective-permute-done.above_ref, ...), custom_call_target="tpu_custom_call" | custom-call | tf_op jit(solution)/shard_map/analyse/pallas_call | solution.py:274
  69.9 42.3 %all_to_all.15.x_ref = bf16[16,96,4,128]{3,2,1,0:T(4,128)(2,1)S(1)} all-to-all(bf16[16,96,4,128]{3,2,1,0:T(4,128)(2,1)S(1)} %analyse.1), channel_id=1, replica_groups=mesh['member'=16,'space'=16] {'member'}, dimensions={0} | all-to-all | bytes 3145728 | tf_op jit(solution)/shard_map/all_to_all | solution.py:303
  112.2 1.7 %join.1 = bf16[4,6,4,8192]{3,2,1,0:T(4,128)(2,1)} custom-call(bf16[16,96,4,128]{3,2,1,0:T(4,128)(2,1)S(1)} %all_to_all.15.x_ref), custom_call_target="tpu_custom_call" | custom-call | tf_op jit(solution)/shard_map/join/pallas_call | solution.py:247
Async XLA Ops:
  0.0 1.4 %copy-start = (bf16[4,4,6,1,8192]{4,1,3,2,0:T(4,128)(2,1)S(1)}, bf16[4,4,6,1,8192]{4,1,3,2,0:T(4,128)(2,1)}, u32[]{:S(2)}) copy-start(bf16[4,4,6,1,8192]{4,1,3,2,0:T(4,128)(2,1)} %param.6) | copy-start | bytes 4718596
  1.4 9.8 %copy-start.1 = (bf16[4,4,6,1,8192]{4,1,3,2,0:T(4,128)(2,1)S(1)}, bf16[4,4,6,1,8192]{4,1,3,2,0:T(4,128)(2,1)}, u32[]{:S(2)}) copy-start(bf16[4,4,6,1,8192]{4,1,3,2,0:T(4,128)(2,1)} %param.6) | copy-start | bytes 4718596
  1.4 9.8 %copy-start.2 = (f32[1,8,128]{2,1,0:T(8,128)S(1)}, f32[1,8,128]{2,1,0:T(8,128)}, u32[]{:S(2)}) copy-start(f32[1,8,128]{2,1,0:T(8,128)} %param.7) | copy-start | bytes 12292
  1.4 9.9 %copy-start.3 = (f32[1,8,128]{2,1,0:T(8,128)S(1)}, f32[1,8,128]{2,1,0:T(8,128)}, u32[]{:S(2)}) copy-start(f32[1,8,128]{2,1,0:T(8,128)} %param.8) | copy-start | bytes 12292
  1.4 9.9 %copy-start.4 = (s32[1,8,128]{2,1,0:T(8,128)S(1)}, s32[1,8,128]{2,1,0:T(8,128)}, u32[]{:S(2)}) copy-start(s32[1,8,128]{2,1,0:T(8,128)} %param.9) | copy-start | bytes 12292
  1.4 9.9 %copy-start.5 = (s32[1,8]{1,0:T(1,128)S(1)}, s32[1,8]{1,0:T(1,128)}, u32[]{:S(2)}) copy-start(s32[1,8]{1,0:T(1,128)} %count_ref.1) | copy-start | bytes 100
  2.6 32.2 %all-to-all-start = ((bf16[16,48,4,128]{3,2,1,0:T(4,128)(2,1)}), bf16[16,48,4,128]{3,2,1,0:T(4,128)(2,1)S(1)}, u32[]{:S(2)}, u32[]{:S(2)}) async-start(bf16[16,48,4,128]{3,2,1,0:T(4,128)(2,1)} %split.1), calls=%async_computation | async-start | bytes 1572864 | tf_op jit(solution)/shard_map/all_to_all | solution.py:295
  13.9 10.8 %collective-permute-start.1 = (f32[8,8,128]{2,1,0:T(8,128)S(1)}, f32[8,8,128]{2,1,0:T(8,128)S(1)}, u32[]{:S(2)}, u32[]{:S(2)}) collective-permute-start(f32[8,8,128]{2,1,0:T(8,128)S(1)} %observe.1.own_ref), channel_id=1, source_target_pairs={{1,0},{2,1},{3,2},{4,3},{5,4},{6,5},{7,6},{8,7},{9,8},{10,9},{11,1... | collective-permute-start | bytes 98312 | tf_op jit(solution)/shard_map/ppermute | solution.py:298
  19.4 10.4 %collective-permute-start = (f32[8,8,128]{2,1,0:T(8,128)S(1)}, f32[8,8,128]{2,1,0:T(8,128)S(1)}, u32[]{:S(2)}, u32[]{:S(2)}) collective-permute-start(f32[8,8,128]{2,1,0:T(8,128)S(1)} %observe.1.own_ref), channel_id=1, source_target_pairs={{0,1},{1,2},{2,3},{3,4},{4,5},{5,6},{6,7},{7,8},{8,9},{9,10},{10,1... | collective-permute-start | bytes 98312 | tf_op jit(solution)/shard_map/ppermute | solution.py:297
  31.1 33.4 %copy-start.6 = (s32[1,8]{1,0:T(1,128)S(1)}, s32[1,8]{1,0:T(1,128)}, u32[]{:S(2)}) copy-start(s32[1,8]{1,0:T(1,128)} %radius_ref.1) | copy-start | bytes 100
  34.8 29.7 %all-to-all-start.1 = ((bf16[16,57,4,128]{3,2,1,0:T(4,128)(2,1)}), bf16[16,57,4,128]{3,2,1,0:T(4,128)(2,1)S(1)}, u32[]{:S(2)}, u32[]{:S(2)}) async-start(bf16[16,57,4,128]{3,2,1,0:T(4,128)(2,1)} %pack.1), calls=%async_computation.1 | async-start | bytes 1867776 | tf_op jit(solution)/shard_map/all_to_all | solution.py:300

commit v5 on v4

--- a/solution.py
+++ b/solution.py
@@ -10,50 +10,63 @@
 TILE_SIDE = 32
 TILE_CELLS = 1024
 SWEEPS = 6
-EXACT = lax.Precision.HIGHEST
 
 
 LANES = 128
 VMEM = pl.BlockSpec(memory_space=pltpu.VMEM)
 SMEM = pl.BlockSpec(memory_space=pltpu.SMEM)
+HBM = pl.BlockSpec(memory_space=pltpu.HBM)
 PARAMS = pltpu.CompilerParams(vmem_limit_bytes=16 * 1024 * 1024)
 EARLY = 3
 
 
-def copy_blocks(x_ref, out_ref, begin, end):
-    own, _, _, width = x_ref.shape
+def split_kernel(x_ref, out_ref, held, made, in_sems, out_sems):
+    kinds, own = held.shape[:2]
+    width = held.shape[3]
     blocks = width // LANES
-    per = blocks // out_ref.shape[0]
-
-    def body(f, carry):
+    parts, step = made.shape[1:3]
+    per = blocks // parts
+    loads = [
+        pltpu.make_async_copy(x_ref.at[:, f], held.at[f], in_sems.at[f]) for f in range(kinds)
+    ]
+    stores = [
+        pltpu.make_async_copy(
+            made.at[f], out_ref.at[:, pl.ds(f * step, step)], out_sems.at[f]
+        )
+        for f in range(kinds)
+    ]
+    for load in loads:
+        load.start()
+    for f in range(kinds):
+        loads[f].wait()
         for c in range(blocks):
             for m in range(own):
-                out_ref[c // per, ((f - begin) * per + c % per) * own + m] = x_ref[
-                    m, f, :, c * LANES : (c + 1) * LANES
+                made[f, c // per, c % per * own + m] = held[
+                    f, m, :, c * LANES : (c + 1) * LANES
                 ]
-        return carry
-
-    lax.fori_loop(begin, end, body, 0)
-
-
-def split_kernel(end, x_ref, out_ref):
-    copy_blocks(x_ref, out_ref, 0, end)
-
-
-def join_kernel(x_ref, out_ref):
-    own, kinds, levels, width = out_ref.shape
+        stores[f].start()
+    for store in stores:
+        store.wait()
+
+
+def join_kernel(x_ref, out_ref, made, out_sems):
+    kinds, own = made.shape[:2]
+    width = made.shape[3]
     blocks = width // LANES
     per = blocks // x_ref.shape[0]
-
-    def body(f, carry):
+    stores = [
+        pltpu.make_async_copy(made.at[f], out_ref.at[:, f], out_sems.at[f])
+        for f in range(kinds)
+    ]
+    for f in range(kinds):
         for c in range(blocks):
             for m in range(own):
-                out_ref[m, f, :, c * LANES : (c + 1) * LANES] = x_ref[
+                made[f, m, :, c * LANES : (c + 1) * LANES] = x_ref[
                     c // per, (f * per + c % per) * own + m
                 ]
-        return carry
-
-    lax.fori_loop(0, kinds, body, 0)
+        stores[f].start()
+    for store in stores:
+        store.wait()
 
 
 def observe_kernel(x_ref, value_ref, precision_ref, cell_ref, count_ref, out_ref):
@@ -82,8 +95,19 @@
 
 
 def pack_kernel(begin, x_ref, above_ref, own_ref, below_ref, out_ref):
-    copy_blocks(x_ref, out_ref, begin, x_ref.shape[1])
     parts, blocks, own, slots = out_ref.shape
+    lane_blocks = x_ref.shape[3] // LANES
+    per = lane_blocks // parts
+
+    def copy_field(f, carry):
+        for c in range(lane_blocks):
+            for m in range(own):
+                out_ref[c // per, ((f - begin) * per + c % per) * own + m] = x_ref[
+                    m, f, :, c * LANES : (c + 1) * LANES
+                ]
+        return carry
+
+    lax.fori_loop(begin, x_ref.shape[1], copy_field, 0)
     first = blocks - 9
     tiles = own_ref.shape[0]
     share = parts // tiles
@@ -100,6 +124,30 @@
         for a in range(3):
             out_ref[h, first + a * 3] = blank
             out_ref[(tiles - 1) * share + h, first + a * 3 + 2] = blank
+
+
+def two_terms(array):
+    high = array.astype(jnp.bfloat16)
+    return high, (array - high.astype(jnp.float32)).astype(jnp.bfloat16)
+
+
+def gram(left, right):
+    def product(a, b):
+        return lax.dot_general(
+            a, b, (((1,), (1,)), ((), ())), preferred_element_type=jnp.float32
+        )
+
+    return (
+        product(left[0], right[0]) + product(left[0], right[1]) + product(left[1], right[0])
+    )
+
+
+def doubled_product(left, right):
+    return jnp.dot(
+        jnp.concatenate(left, axis=1),
+        jnp.concatenate(right + right, axis=0),
+        preferred_element_type=jnp.float32,
+    )
 
 
 def analyse_kernel(
@@ -143,27 +191,28 @@
     extended = jnp.concatenate(
         [anomaly, jnp.broadcast_to(innovation, (8, innovation.shape[1]))], axis=0
     )
-    product = lax.dot_general(
-        extended, scaled, (((1,), (1,)), ((), ())), precision=EXACT,
-        preferred_element_type=jnp.float32,
-    )
+    product = gram(two_terms(extended), two_terms(scaled))
     forcing = product[members : members + 1]
-    row_id = lax.broadcasted_iota(jnp.int32, (members, members), 0)
-    col_id = lax.broadcasted_iota(jnp.int32, (members, members), 1)
-    identity = (row_id == col_id).astype(jnp.float32)
-    system = (members - 1.0) * identity + product[:members]
-    scale = jnp.sum(
+    row_id = lax.broadcasted_iota(jnp.int32, (members, 2 * members), 0)
+    col_id = lax.broadcasted_iota(jnp.int32, (members, 2 * members), 1)
+    identity = (row_id == col_id % members).astype(jnp.float32)
+    system = (members - 1.0) * identity + jnp.concatenate([product[:members]] * 2, axis=1)
+    scale = 0.5 * jnp.sum(
         jnp.sum(system * identity, axis=1, keepdims=True), axis=0, keepdims=True
     )
     root_part = system / scale
-    inverse = identity
-    mul = functools.partial(jnp.dot, precision=EXACT, preferred_element_type=jnp.float32)
-    for sweep in range(SWEEPS):
-        factor = 1.5 * identity - 0.5 * (root_part if sweep == 0 else mul(inverse, root_part))
-        if sweep < SWEEPS - 1:
-            root_part = mul(root_part, factor)
-        inverse = factor if sweep == 0 else mul(factor, inverse)
-    inv_sqrt = inverse / jnp.sqrt(scale)
+    factor = 1.5 * identity - 0.5 * root_part
+    inverse = factor
+    for sweep in range(1, SWEEPS):
+        factor_terms = two_terms(factor)
+        if sweep > 1:
+            inverse = doubled_product(factor_terms, two_terms(inverse))
+        root_part = doubled_product(two_terms(root_part), factor_terms)
+        factor = 1.5 * identity - 0.5 * doubled_product(
+            two_terms(inverse), two_terms(root_part)
+        )
+    inverse = doubled_product(two_terms(factor), two_terms(inverse))
+    inv_sqrt = inverse[:, :members] / jnp.sqrt(scale)
     half = jnp.sum(inv_sqrt * forcing, axis=1, keepdims=True)
     mean_weight = jnp.sum(inv_sqrt * half, axis=0, keepdims=True)
     total = jnp.sqrt(jnp.float32(members - 1)) * inv_sqrt + mean_weight
@@ -232,23 +281,33 @@
 
 def split(fields, parts, end):
     own, kinds, levels, width = fields.shape
-    blocks = own * end * (width // parts // LANES)
-    return pl.pallas_call(
-        functools.partial(split_kernel, end),
-        in_specs=[VMEM],
-        out_specs=VMEM,
-        out_shape=jax.ShapeDtypeStruct((parts, blocks, levels, LANES), fields.dtype),
-        compiler_params=PARAMS,
+    step = own * (width // parts // LANES)
+    return pl.pallas_call(
+        split_kernel,
+        in_specs=[HBM],
+        out_specs=HBM,
+        out_shape=jax.ShapeDtypeStruct((parts, end * step, levels, LANES), fields.dtype),
+        scratch_shapes=[
+            pltpu.VMEM((end, own, levels, width), fields.dtype),
+            pltpu.VMEM((end, parts, step, levels, LANES), fields.dtype),
+            pltpu.SemaphoreType.DMA((end,)),
+            pltpu.SemaphoreType.DMA((end,)),
+        ],
         name="split",
     )(fields)
 
 
 def join(pieces, shape):
+    own, kinds, levels, width = shape
     return pl.pallas_call(
         join_kernel,
         in_specs=[VMEM],
-        out_specs=VMEM,
+        out_specs=HBM,
         out_shape=jax.ShapeDtypeStruct(shape, pieces.dtype),
+        scratch_shapes=[
+            pltpu.VMEM((kinds, own, levels, width), pieces.dtype),
+            pltpu.SemaphoreType.DMA((kinds,)),
+        ],
         compiler_params=PARAMS,
         name="join",
     )(pieces)

time: 114 us -> 113 us (level)
  local copies, waits for them, and re-layouts: 1.43 us -> 0.02 us
    unnamed x14 -> x12, local copies, waits for them, and re-layouts: 1.43 us -> 0.02 us
where the time goes in v5:
time: 113 us; the launch traced here: 112 us
  blocking collectives  42.3 us (37%)
  waiting for transfers between devices  38.1 us (34%)
  starting transfers between devices  19.9 us (18%)
  Pallas kernels  12 us (11%)
    all_to_all x1, blocking collectives, on_device(): out = join(lax.all_to_all(mixed, 'member', 0, 0), fields.shape)  42.3 us
    all_to_all x1, waiting for transfers between devices, on_device(): late = lax.all_to_all(late, 'member', 0, 0)  25.9 us
    all_to_all x1, starting transfers between devices, on_device(): early = lax.all_to_all(early, 'member', 0, 0)  8.65 us
    ppermute x1, starting transfers between devices, on_device(): below = lax.ppermute(here, 'space', up)  5.53 us
    ppermute x1, waiting for transfers between devices, on_device(): above = lax.ppermute(here, 'space', down)  5.12 us
    pallas_call x1, Pallas kernels, analyse(): pl.pallas_call(functools.partial(analyse_kernel, kinds), in_specs=[SMEM,...  4.76 us
    all_to_all x1, starting transfers between devices, on_device(): late = lax.all_to_all(late, 'member', 0, 0)  3.76 us
    all_to_all x1, waiting for transfers between devices, on_device(): early = lax.all_to_all(early, 'member', 0, 0)  3.73 us
  transfers between devices with their start and end apart: 4, of which 4 were waited for; matrix products, arithmetic and copies ran while one was open for 0% of the time, Pallas kernels for 3%

profile of v5, /device:TPU:2, one launch (start us, length us, event | category | flops | bytes accessed | tf_op | source)
XLA Modules:
  0.0 112.4 jit_solution(15707618713601903223)
XLA Ops:
  0.0 0.0 copy-start
  0.0 0.0 copy-start.1
  0.0 0.0 copy-start.2
  0.0 0.0 copy-start.3
  0.0 0.0 copy-start.4
  0.0 2.1 %split.1 = bf16[16,48,4,128]{3,2,1,0:T(4,128)(2,1)} custom-call(bf16[4,6,4,8192]{3,2,1,0:T(4,128)(2,1)} %bitcast.14), custom_call_target="tpu_custom_call" | custom-call | tf_op jit(solution)/shard_map/split/pallas_call | solution.py:285
  2.2 8.6 %all-to-all-start = ((bf16[16,48,4,128]{3,2,1,0:T(4,128)(2,1)}), bf16[16,48,4,128]{3,2,1,0:T(4,128)(2,1)S(1)}, u32[]{:S(2)}, u32[]{:S(2)}) async-start(bf16[16,48,4,128]{3,2,1,0:T(4,128)(2,1)} %split.1), calls=%async_computation | async-start | bytes 1572864 | tf_op jit(solution)/shard_map/all_to_all | solution.py:354
  10.8 0.0 copy-done
  10.8 0.0 copy-done.1
  10.8 0.0 copy-done.2
  10.9 0.0 copy-done.3
  10.9 0.0 copy-done.4
  10.9 2.6 %observe.1.own_ref = f32[8,8,128]{2,1,0:T(8,128)S(1)} custom-call(bf16[4,6,4,8192]{3,2,1,0:T(4,128)(2,1)S(1)} %bitcast.15, f32[8,128]{1,0:T(8,128)S(1)} %bitcast.17, f32[8,128]{1,0:T(8,128)S(1)} %bitcast.18, s32[8,128]{1,0:T(8,128)S(1)} %bitcast.19, s32[1,8]{1,0:T(1,128)S(1)} %copy-done.4), custom_call_target="tpu_custom_call" | custom-call | tf_op jit(solution)/shard_map/observe/pallas_call | solution.py:265
  13.4 5.5 %collective-permute-start.1 = (f32[8,8,128]{2,1,0:T(8,128)S(1)}, f32[8,8,128]{2,1,0:T(8,128)S(1)}, u32[]{:S(2)}, u32[]{:S(2)}) collective-permute-start(f32[8,8,128]{2,1,0:T(8,128)S(1)} %observe.1.own_ref), channel_id=1, source_target_pairs={{1,0},{2,1},{3,2},{4,3},{5,4},{6,5},{7,6},{8,7},{9,8},{10,9},{11,1... | collective-permute-start | bytes 98312 | tf_op jit(solution)/shard_map/ppermute | solution.py:357
  19.0 1.9 %collective-permute-start = (f32[8,8,128]{2,1,0:T(8,128)S(1)}, f32[8,8,128]{2,1,0:T(8,128)S(1)}, u32[]{:S(2)}, u32[]{:S(2)}) collective-permute-start(f32[8,8,128]{2,1,0:T(8,128)S(1)} %observe.1.own_ref), channel_id=1, source_target_pairs={{0,1},{1,2},{2,3},{3,4},{4,5},{5,6},{6,7},{7,8},{8,9},{9,10},{10,1... | collective-permute-start | bytes 98312 | tf_op jit(solution)/shard_map/ppermute | solution.py:356
  20.9 3.4 %collective-permute-done.1.below_ref = f32[8,8,128]{2,1,0:T(8,128)S(1)} collective-permute-done((f32[8,8,128]{2,1,0:T(8,128)S(1)}, f32[8,8,128]{2,1,0:T(8,128)S(1)}, u32[]{:S(2)}, u32[]{:S(2)}) %collective-permute-start.1) | collective-permute-done | bytes 32800 | tf_op jit(solution)/shard_map/ppermute | solution.py:357
  24.3 5.1 %collective-permute-done.above_ref = f32[8,8,128]{2,1,0:T(8,128)S(1)} collective-permute-done((f32[8,8,128]{2,1,0:T(8,128)S(1)}, f32[8,8,128]{2,1,0:T(8,128)S(1)}, u32[]{:S(2)}, u32[]{:S(2)}) %collective-permute-start) | collective-permute-done | bytes 32800 | tf_op jit(solution)/shard_map/ppermute | solution.py:356
  29.4 1.2 %pack.1 = bf16[16,57,4,128]{3,2,1,0:T(4,128)(2,1)} custom-call(bf16[4,6,4,8192]{3,2,1,0:T(4,128)(2,1)S(1)} %bitcast.16, f32[8,8,128]{2,1,0:T(8,128)S(1)} %collective-permute-done.above_ref, f32[8,8,128]{2,1,0:T(8,128)S(1)} %observe.1.own_ref, f32[8,8,128]{2,1,0:T(8,128)S(1)} %collective-permute-done.1.below_ref), custom_call_target="tpu_custom_call" | custom-call | tf_op jit(solution)/shard_map/pack/pallas_call | solution.py:319
  30.7 0.0 copy-start.5
  30.7 3.7 %all-to-all-done.early_ref = bf16[16,48,4,128]{3,2,1,0:T(4,128)(2,1)S(1)} async-done(((bf16[16,48,4,128]{3,2,1,0:T(4,128)(2,1)}), bf16[16,48,4,128]{3,2,1,0:T(4,128)(2,1)S(1)}, u32[]{:S(2)}, u32[]{:S(2)}) %all-to-all-start) | async-done | bytes 786464 | tf_op jit(solution)/shard_map/all_to_all | solution.py:354
  34.4 3.8 %all-to-all-start.1 = ((bf16[16,57,4,128]{3,2,1,0:T(4,128)(2,1)}), bf16[16,57,4,128]{3,2,1,0:T(4,128)(2,1)S(1)}, u32[]{:S(2)}, u32[]{:S(2)}) async-start(bf16[16,57,4,128]{3,2,1,0:T(4,128)(2,1)} %pack.1), calls=%async_computation.1 | async-start | bytes 1867776 | tf_op jit(solution)/shard_map/all_to_all | solution.py:359
  38.2 25.9 %all-to-all-done.1.x_ref = bf16[16,57,4,128]{3,2,1,0:T(4,128)(2,1)S(1)} async-done(((bf16[16,57,4,128]{3,2,1,0:T(4,128)(2,1)}), bf16[16,57,4,128]{3,2,1,0:T(4,128)(2,1)S(1)}, u32[]{:S(2)}, u32[]{:S(2)}) %all-to-all-start.1) | async-done | bytes 933920 | tf_op jit(solution)/shard_map/all_to_all | solution.py:359
  64.1 0.0 copy-done.5
  64.1 4.8 %analyse.1 = bf16[16,96,4,128]{3,2,1,0:T(4,128)(2,1)S(1)} custom-call(s32[1]{0:T(128)} %bitcast.where_ref, s32[1,8]{1,0:T(1,128)S(1)} %copy-done.5, bf16[16,48,4,128]{3,2,1,0:T(4,128)(2,1)S(1)} %all-to-all-done.early_ref, bf16[16,57,4,128]{3,2,1,0:T(4,128)(2,1)S(1)} %all-to-all-done.1.x_ref, f32[8,8,128]{2,1,0:T(8,128)S(1)} %collective-permute-done.above_ref, ...), custom_call_target="tpu_custom_call" | custom-call | tf_op jit(solution)/shard_map/analyse/pallas_call | solution.py:333
  68.9 42.3 %all_to_all.15.x_ref = bf16[16,96,4,128]{3,2,1,0:T(4,128)(2,1)S(1)} all-to-all(bf16[16,96,4,128]{3,2,1,0:T(4,128)(2,1)S(1)} %analyse.1), channel_id=1, replica_groups=mesh['member'=16,'space'=16] {'member'}, dimensions={0} | all-to-all | bytes 3145728 | tf_op jit(solution)/shard_map/all_to_all | solution.py:362
  111.1 1.3 %join.1 = bf16[4,6,4,8192]{3,2,1,0:T(4,128)(2,1)} custom-call(bf16[16,96,4,128]{3,2,1,0:T(4,128)(2,1)S(1)} %all_to_all.15.x_ref), custom_call_target="tpu_custom_call" | custom-call | tf_op jit(solution)/shard_map/join/pallas_call | solution.py:302
Async XLA Ops:
  0.0 10.8 %copy-start = (bf16[4,4,6,1,8192]{4,1,3,2,0:T(4,128)(2,1)S(1)}, bf16[4,4,6,1,8192]{4,1,3,2,0:T(4,128)(2,1)}, u32[]{:S(2)}) copy-start(bf16[4,4,6,1,8192]{4,1,3,2,0:T(4,128)(2,1)} %param.6) | copy-start | bytes 4718596
  0.0 10.8 %copy-start.1 = (f32[1,8,128]{2,1,0:T(8,128)S(1)}, f32[1,8,128]{2,1,0:T(8,128)}, u32[]{:S(2)}) copy-start(f32[1,8,128]{2,1,0:T(8,128)} %param.7) | copy-start | bytes 12292
  0.0 10.8 %copy-start.2 = (f32[1,8,128]{2,1,0:T(8,128)S(1)}, f32[1,8,128]{2,1,0:T(8,128)}, u32[]{:S(2)}) copy-start(f32[1,8,128]{2,1,0:T(8,128)} %param.8) | copy-start | bytes 12292
  0.0 10.8 %copy-start.3 = (s32[1,8,128]{2,1,0:T(8,128)S(1)}, s32[1,8,128]{2,1,0:T(8,128)}, u32[]{:S(2)}) copy-start(s32[1,8,128]{2,1,0:T(8,128)} %param.9) | copy-start | bytes 12292
  0.0 10.8 %copy-start.4 = (s32[1,8]{1,0:T(1,128)S(1)}, s32[1,8]{1,0:T(1,128)}, u32[]{:S(2)}) copy-start(s32[1,8]{1,0:T(1,128)} %count_ref.1) | copy-start | bytes 100
  2.2 32.2 %all-to-all-start = ((bf16[16,48,4,128]{3,2,1,0:T(4,128)(2,1)}), bf16[16,48,4,128]{3,2,1,0:T(4,128)(2,1)S(1)}, u32[]{:S(2)}, u32[]{:S(2)}) async-start(bf16[16,48,4,128]{3,2,1,0:T(4,128)(2,1)} %split.1), calls=%async_computation | async-start | bytes 1572864 | tf_op jit(solution)/shard_map/all_to_all | solution.py:354
  13.4 10.8 %collective-permute-start.1 = (f32[8,8,128]{2,1,0:T(8,128)S(1)}, f32[8,8,128]{2,1,0:T(8,128)S(1)}, u32[]{:S(2)}, u32[]{:S(2)}) collective-permute-start(f32[8,8,128]{2,1,0:T(8,128)S(1)} %observe.1.own_ref), channel_id=1, source_target_pairs={{1,0},{2,1},{3,2},{4,3},{5,4},{6,5},{7,6},{8,7},{9,8},{10,9},{11,1... | collective-permute-start | bytes 98312 | tf_op jit(solution)/shard_map/ppermute | solution.py:357
  19.0 10.4 %collective-permute-start = (f32[8,8,128]{2,1,0:T(8,128)S(1)}, f32[8,8,128]{2,1,0:T(8,128)S(1)}, u32[]{:S(2)}, u32[]{:S(2)}) collective-permute-start(f32[8,8,128]{2,1,0:T(8,128)S(1)} %observe.1.own_ref), channel_id=1, source_target_pairs={{0,1},{1,2},{2,3},{3,4},{4,5},{5,6},{6,7},{7,8},{8,9},{9,10},{10,1... | collective-permute-start | bytes 98312 | tf_op jit(solution)/shard_map/ppermute | solution.py:356
  30.7 33.4 %copy-start.5 = (s32[1,8]{1,0:T(1,128)S(1)}, s32[1,8]{1,0:T(1,128)}, u32[]{:S(2)}) copy-start(s32[1,8]{1,0:T(1,128)} %radius_ref.1) | copy-start | bytes 100
  34.4 29.7 %all-to-all-start.1 = ((bf16[16,57,4,128]{3,2,1,0:T(4,128)(2,1)}), bf16[16,57,4,128]{3,2,1,0:T(4,128)(2,1)S(1)}, u32[]{:S(2)}, u32[]{:S(2)}) async-start(bf16[16,57,4,128]{3,2,1,0:T(4,128)(2,1)} %pack.1), calls=%async_computation.1 | async-start | bytes 1867776 | tf_op jit(solution)/shard_map/all_to_all | solution.py:359

commit v6 on v5

--- a/solution.py
+++ b/solution.py
@@ -17,10 +17,15 @@
 SMEM = pl.BlockSpec(memory_space=pltpu.SMEM)
 HBM = pl.BlockSpec(memory_space=pltpu.HBM)
 PARAMS = pltpu.CompilerParams(vmem_limit_bytes=16 * 1024 * 1024)
-EARLY = 3
-
-
-def split_kernel(x_ref, out_ref, held, made, in_sems, out_sems):
+EARLY = 4
+SIDE = 4
+
+
+def turned(core, index):
+    return jnp.where(core == 0, index % SIDE * SIDE + index // SIDE, index)
+
+
+def split_kernel(core_ref, x_ref, out_ref, held, made, in_sems, out_sems):
     kinds, own = held.shape[:2]
     width = held.shape[3]
     blocks = width // LANES
@@ -37,11 +42,12 @@
     ]
     for load in loads:
         load.start()
+    places = [turned(1 - core_ref[0], d) for d in range(parts)]
     for f in range(kinds):
         loads[f].wait()
         for c in range(blocks):
             for m in range(own):
-                made[f, c // per, c % per * own + m] = held[
+                made[f, places[c // per], c % per * own + m] = held[
                     f, m, :, c * LANES : (c + 1) * LANES
                 ]
         stores[f].start()
@@ -94,7 +100,14 @@
     out_ref[0, own + 3 : own + 4, :] = col_place
 
 
-def pack_kernel(begin, x_ref, above_ref, own_ref, below_ref, out_ref):
+def pack_kernel(
+    begin, core_ref, x_ref, inner_ref, own_ref, outer_ref, out_ref, above_ref, below_ref
+):
+    odd = core_ref[0] == 1
+    places = [turned(1 - core_ref[0], d) for d in range(out_ref.shape[0])]
+    inner, outer = inner_ref[...], outer_ref[...]
+    above_ref[...] = jnp.where(odd, inner, outer)
+    below_ref[...] = jnp.where(odd, outer, inner)
     parts, blocks, own, slots = out_ref.shape
     lane_blocks = x_ref.shape[3] // LANES
     per = lane_blocks // parts
@@ -102,7 +115,7 @@
     def copy_field(f, carry):
         for c in range(lane_blocks):
             for m in range(own):
-                out_ref[c // per, ((f - begin) * per + c % per) * own + m] = x_ref[
+                out_ref[places[c // per], ((f - begin) * per + c % per) * own + m] = x_ref[
                     m, f, :, c * LANES : (c + 1) * LANES
                 ]
         return carry
@@ -118,12 +131,12 @@
                 for h in range(share):
                     place = t + 1 - b
                     if 0 <= place < tiles:
-                        out_ref[place * share + h, first + a * 3 + b] = rows
+                        out_ref[places[place * share + h], first + a * 3 + b] = rows
     blank = jnp.zeros((own, slots), out_ref.dtype)
     for h in range(share):
         for a in range(3):
-            out_ref[h, first + a * 3] = blank
-            out_ref[(tiles - 1) * share + h, first + a * 3 + 2] = blank
+            out_ref[places[h], first + a * 3] = blank
+            out_ref[places[(tiles - 1) * share + h], first + a * 3 + 2] = blank
 
 
 def two_terms(array):
@@ -151,13 +164,12 @@
 
 
 def analyse_kernel(
-    kinds, where_ref, radius_ref, early_ref, x_ref, above_ref, own_ref, below_ref, out_ref, mix_ref
+    kinds, tile_ref, core_ref, radius_ref, x_ref, above_ref, own_ref, below_ref, out_ref, mix_ref
 ):
-    tile = where_ref[0]
+    tile = tile_ref[0]
     tiles = own_ref.shape[0]
     sources, _, levels, slots = x_ref.shape
     own = own_ref.shape[1] - 4
-    ahead = early_ref.shape[1]
     first = x_ref.shape[1] - 9
     members = sources * own
     reach = radius_ref[0, tile].astype(jnp.float32)
@@ -223,7 +235,14 @@
         lax.broadcasted_iota(jnp.int32, (wide, members), 0) // levels
         == lax.broadcasted_iota(jnp.int32, (wide, members), 1)
     ).astype(jnp.bfloat16)
-    tall = jnp.dot(spread, mixing, preferred_element_type=jnp.float32).astype(jnp.bfloat16)
+    device = lax.broadcasted_iota(jnp.int32, (wide, members), 0) // (own * levels)
+    row_member = turned(core_ref[0], device) * own + (
+        lax.broadcasted_iota(jnp.int32, (wide, members), 0) // levels % own
+    )
+    chosen = (
+        row_member == lax.broadcasted_iota(jnp.int32, (wide, members), 1)
+    ).astype(jnp.bfloat16)
+    tall = jnp.dot(chosen, mixing, preferred_element_type=jnp.float32).astype(jnp.bfloat16)
     full = lax.dot_general(
         tall, spread, (((1,), (1,)), ((), ())), preferred_element_type=jnp.float32
     )
@@ -234,28 +253,21 @@
     mix_ref[...] = jnp.where(same, full, 0.0).astype(mix_ref.dtype)
     per = out_ref.shape[1] // (kinds * own)
 
-    def mix_fields(from_ref, offset):
-        def body(f, carry):
-            begin = f * per * own
-            rows = jnp.concatenate(
-                [
-                    from_ref[:, pl.ds(begin + c * own, own)].reshape(wide, LANES)
-                    for c in range(per)
-                ],
-                axis=1,
-            )
-            mixed = jnp.dot(mix_ref[...], rows, preferred_element_type=jnp.float32)
-            mixed = mixed.astype(out_ref.dtype)
-            for c in range(per):
-                out_ref[:, pl.ds(offset + begin + c * own, own)] = mixed[
-                    :, c * LANES : (c + 1) * LANES
-                ].reshape(sources, own, levels, LANES)
-            return carry
-
-        return body
-
-    lax.fori_loop(0, ahead // (per * own), mix_fields(early_ref, 0), 0)
-    lax.fori_loop(0, first // (per * own), mix_fields(x_ref, ahead), 0)
+    def body(f, carry):
+        begin = f * per * own
+        rows = jnp.concatenate(
+            [x_ref[:, pl.ds(begin + c * own, own)].reshape(wide, LANES) for c in range(per)],
+            axis=1,
+        )
+        mixed = jnp.dot(mix_ref[...], rows, preferred_element_type=jnp.float32)
+        mixed = mixed.astype(out_ref.dtype)
+        for c in range(per):
+            out_ref[:, pl.ds(begin + c * own, own)] = mixed[
+                :, c * LANES : (c + 1) * LANES
+            ].reshape(sources, own, levels, LANES)
+        return carry
+
+    lax.fori_loop(0, kinds, body, 0)
 
 
 def observe(fields, values, precision, cells, count):
@@ -279,12 +291,12 @@
     )(fields, values, precision, cells, count)
 
 
-def split(fields, parts, end):
+def split(core, fields, parts, end):
     own, kinds, levels, width = fields.shape
     step = own * (width // parts // LANES)
     return pl.pallas_call(
         split_kernel,
-        in_specs=[HBM],
+        in_specs=[SMEM, HBM],
         out_specs=HBM,
         out_shape=jax.ShapeDtypeStruct((parts, end * step, levels, LANES), fields.dtype),
         scratch_shapes=[
@@ -294,7 +306,7 @@
             pltpu.SemaphoreType.DMA((end,)),
         ],
         name="split",
-    )(fields)
+    )(core, fields)
 
 
 def join(pieces, shape):
@@ -313,32 +325,49 @@
     )(pieces)
 
 
-def pack(fields, parts, begin, above, here, below):
+def pack(core, fields, parts, begin, inner, here, outer):
     own, kinds, levels, width = fields.shape
     blocks = own * (kinds - begin) * (width // parts // LANES) + 9
+    small = jax.ShapeDtypeStruct(here.shape, here.dtype)
     return pl.pallas_call(
         functools.partial(pack_kernel, begin),
-        in_specs=[VMEM] * 4,
-        out_specs=VMEM,
-        out_shape=jax.ShapeDtypeStruct((parts, blocks, levels, LANES), fields.dtype),
+        in_specs=[SMEM] + [VMEM] * 4,
+        out_specs=[VMEM] * 3,
+        out_shape=[
+            jax.ShapeDtypeStruct((parts, blocks, levels, LANES), fields.dtype),
+            small,
+            small,
+        ],
         compiler_params=PARAMS,
         name="pack",
-    )(fields, above, here, below)
-
-
-def analyse(tile, radius, early, late, above, here, below, kinds):
-    parts, blocks, levels, lanes = early.shape
+    )(core, fields, inner, here, outer)
+
+
+def analyse(tile, core, radius, pieces, above, here, below, kinds):
+    parts, blocks, levels, lanes = pieces.shape
     wide = parts * (here.shape[1] - 4) * levels
-    blocks += late.shape[1] - 9
     return pl.pallas_call(
         functools.partial(analyse_kernel, kinds),
-        in_specs=[SMEM, SMEM] + [VMEM] * 5,
+        in_specs=[SMEM] * 3 + [VMEM] * 4,
         out_specs=VMEM,
-        out_shape=jax.ShapeDtypeStruct((parts, blocks, levels, lanes), early.dtype),
+        out_shape=jax.ShapeDtypeStruct((parts, blocks - 9, levels, lanes), pieces.dtype),
         scratch_shapes=[pltpu.VMEM((wide, wide), jnp.bfloat16)],
         compiler_params=PARAMS,
         name="analyse",
-    )(tile, radius, early, late, above, here, below)
+    )(tile, core, radius, pieces, above, here, below)
+
+
+def hop_groups(rows):
+    def group(row, fixed, along_y):
+        members = [
+            i * SIDE + fixed if along_y else fixed * SIDE + i for i in range(SIDE)
+        ]
+        return [member * rows + row for member in members]
+
+    return [
+        [group(r, i, r % 2 == hop) for r in range(rows) for i in range(SIDE)]
+        for hop in range(2)
+    ]
 
 
 def on_device(background, obs_values, obs_precision, obs_cell, obs_count, radius):
@@ -346,19 +375,29 @@
     parts = lax.axis_size("member")
     rows = lax.axis_size("space")
     share = parts * TILE_CELLS // width
-    down = [(i, i + 1) for i in range(rows - 1)]
-    up = [(i + 1, i) for i in range(rows - 1)]
+    pairs = [(i, i + 1) for i in range(rows - 1)]
+    swap = [pairs[0::2], pairs[1::2]]
+    swap = [one + [(j, i) for i, j in one] for one in swap]
     fields = background.transpose(0, 2, 3, 1, 4).reshape(own, kinds, levels, width)
-    early = split(fields, parts, EARLY)
+    both = ("member", "space")
+    groups = hop_groups(rows)
+    core = (lax.axis_index("space") % 2).astype(jnp.int32).reshape(1)
+    early = split(core, fields, parts, EARLY)
     early, fields = lax.optimization_barrier((early, fields))
-    early = lax.all_to_all(early, "member", 0, 0)
+    early = early.reshape((SIDE, SIDE) + early.shape[1:])
+    early = lax.all_to_all(early, both, 0, 0, axis_index_groups=groups[0])
     here = observe(fields, obs_values[0], obs_precision[0], obs_cell[0], obs_count)
-    above = lax.ppermute(here, "space", down)
-    below = lax.ppermute(here, "space", up)
-    late = pack(fields, parts, EARLY, above, here, below)
-    late = lax.all_to_all(late, "member", 0, 0)
+    inner = lax.ppermute(here, "space", swap[0])
+    outer = lax.ppermute(here, "space", swap[1])
+    late, above, below = pack(core, fields, parts, EARLY, inner, here, outer)
+    late = late.reshape((SIDE, SIDE) + late.shape[1:])
+    late, early = lax.optimization_barrier((late, early))
+    late = lax.all_to_all(late, both, 0, 0, axis_index_groups=groups[0])
+    pieces = jnp.concatenate([early, late], axis=2).swapaxes(0, 1)
+    pieces = lax.all_to_all(pieces, both, 0, 0, axis_index_groups=groups[1])
+    pieces = pieces.reshape((parts,) + pieces.shape[2:])
     tile = (lax.axis_index("member") // share).astype(jnp.int32).reshape(1)
-    mixed = analyse(tile, radius, early, late, above, here, below, kinds)
+    mixed = analyse(tile, core, radius, pieces, above, here, below, kinds)
     out = join(lax.all_to_all(mixed, "member", 0, 0), fields.shape)
     return out.reshape(own, kinds, 1, levels, width).transpose(0, 3, 1, 2, 4)
 

time: 113 us -> 107 us (0.947)
  waiting for transfers between devices: 38.1 us -> 27.5 us
  blocking collectives: 42.3 us -> 45.5 us
  local copies, waits for them, and re-layouts: 0.02 us -> 1.83 us
    all_to_all x0 -> x1, blocking collectives: none -> 13.1 us  [on_device(): late = lax.all_to_all(late, both, 0, 0, axis_index_groups=groups[0])]
    all_to_all x1, blocking collectives: 42.3 us -> 32.4 us  [on_device(): out = join(lax.all_to_all(mixed, 'member', 0, 0), fields.shape)]
    all_to_all x2, waiting for transfers between devices: 29.6 us -> 23.1 us  [the longest x1 23.1 us: on_device(): pieces = lax.all_to_all(pieces, both, 0, 0, axis_index_groups=groups[1])]
    ppermute x2, waiting for transfers between devices: 8.5 us -> 4.42 us  [the longest x1 4.42 us: on_device(): outer = lax.ppermute(here, 'space', swap[1])]
    all_to_all x2, starting transfers between devices: 12.4 us -> 9.8 us  [the longest x1 5.32 us: on_device(): pieces = lax.all_to_all(pieces, both, 0, 0, axis_index_groups=groups[1])]
    ppermute x2, starting transfers between devices: 7.45 us -> 9.3 us  [the longest x1 7.59 us: on_device(): outer = lax.ppermute(here, 'space', swap[1])]
    transpose x0 -> x1, local copies, waits for them, and re-layouts: none -> 1.8 us  [on_device(): pieces = jnp.concatenate([early, late], axis=2).swapaxes(0, 1)]
  transfers between devices with their start and end apart: 4 -> 4, of which waited for: 4 -> 2; matrix products, arithmetic and copies ran while one was open for 0% -> 0% of each run, Pallas kernels for 3% -> 3%
where the time goes in v6:
time: 107 us; the launch traced here: 106 us
  blocking collectives  45.5 us (43%)
  waiting for transfers between devices  27.5 us (26%)
  starting transfers between devices  19.1 us (18%)
  Pallas kernels  11.1 us (10%)
  local copies, waits for them, and re-layouts  1.83 us (2%)
  other arithmetic  1.11 us (1%)
    all_to_all x1, blocking collectives, on_device(): out = join(lax.all_to_all(mixed, 'member', 0, 0), fields.shape)  32.4 us
    all_to_all x1, waiting for transfers between devices, on_device(): pieces = lax.all_to_all(pieces, both, 0, 0, axis_index_groups=groups[1])  23.1 us
    all_to_all x1, blocking collectives, on_device(): late = lax.all_to_all(late, both, 0, 0, axis_index_groups=groups[0])  13.1 us
    ppermute x1, starting transfers between devices, on_device(): outer = lax.ppermute(here, 'space', swap[1])  7.59 us
    all_to_all x1, starting transfers between devices, on_device(): pieces = lax.all_to_all(pieces, both, 0, 0, axis_index_groups=groups[1])  5.32 us
    pallas_call x1, Pallas kernels, analyse(): pl.pallas_call(functools.partial(analyse_kernel, kinds), in_specs=[SMEM]...  4.76 us
    all_to_all x1, starting transfers between devices, on_device(): early = lax.all_to_all(early, both, 0, 0, axis_index_groups=groups[0])  4.48 us
    ppermute x1, waiting for transfers between devices, on_device(): outer = lax.ppermute(here, 'space', swap[1])  4.42 us
  transfers between devices with their start and end apart: 4, of which 2 were waited for; matrix products, arithmetic and copies ran while one was open for 0% of the time, Pallas kernels for 3%

profile of v6, /device:TPU:2, one launch (start us, length us, event | category | flops | bytes accessed | tf_op | source)
XLA Modules:
  0.0 106.3 jit_solution(10836904164535397051)
XLA Ops:
  0.0 0.0 copy-start
  0.0 0.0 copy-start.1
  0.0 0.0 copy-start.2
  0.0 0.0 copy-start.3
  0.0 0.0 copy-start.4
  0.0 2.2 %split.1 = bf16[16,64,4,128]{3,2,1,0:T(4,128)(2,1)} custom-call(s32[1]{0:T(128)} %bitcast.1.core_ref, bf16[4,6,4,8192]{3,2,1,0:T(4,128)(2,1)} %bitcast.20), custom_call_target="tpu_custom_call" | custom-call | tf_op jit(solution)/shard_map/split/pallas_call | solution.py:297
  2.2 4.5 %all-to-all-start = ((bf16[4,4,64,4,128]{4,3,2,1,0:T(4,128)(2,1)}), bf16[4,4,64,4,128]{4,3,2,1,0:T(4,128)(2,1)S(1)}, u32[]{:S(2)}, u32[]{:S(2)}) async-start(bf16[4,4,64,4,128]{4,3,2,1,0:T(4,128)(2,1)} %bitcast.28), calls=%async_computation | async-start | bytes 2097152 | tf_op jit(solution)/shard_map/all_to_all | solution.py:388
  6.7 0.0 copy-done
  6.7 0.0 copy-done.1
  6.7 0.0 copy-done.2
  6.7 0.0 copy-done.3
  6.7 0.0 copy-done.4
  6.8 2.6 %observe.1.own_ref = f32[8,8,128]{2,1,0:T(8,128)S(1)} custom-call(bf16[4,6,4,8192]{3,2,1,0:T(4,128)(2,1)S(1)} %bitcast.21, f32[8,128]{1,0:T(8,128)S(1)} %bitcast.25, f32[8,128]{1,0:T(8,128)S(1)} %bitcast.26, s32[8,128]{1,0:T(8,128)S(1)} %bitcast.27, s32[1,8]{1,0:T(1,128)S(1)} %copy-done.4), custom_call_target="tpu_custom_call" | custom-call | tf_op jit(solution)/shard_map/observe/pallas_call | solution.py:277
  9.3 7.6 %collective-permute-start.1 = (f32[8,8,128]{2,1,0:T(8,128)S(1)}, f32[8,8,128]{2,1,0:T(8,128)S(1)}, u32[]{:S(2)}, u32[]{:S(2)}) collective-permute-start(f32[8,8,128]{2,1,0:T(8,128)S(1)} %observe.1.own_ref), channel_id=1, source_target_pairs={{1,2},{3,4},{5,6},{7,8},{9,10},{11,12},{13,14},{2,1},{4,3},{6,5},{... | collective-permute-start | bytes 98312 | tf_op jit(solution)/shard_map/ppermute | solution.py:391
  16.9 1.7 %collective-permute-start = (f32[8,8,128]{2,1,0:T(8,128)S(1)}, f32[8,8,128]{2,1,0:T(8,128)S(1)}, u32[]{:S(2)}, u32[]{:S(2)}) collective-permute-start(f32[8,8,128]{2,1,0:T(8,128)S(1)} %observe.1.own_ref), channel_id=1, source_target_pairs={{0,1},{2,3},{4,5},{6,7},{8,9},{10,11},{12,13},{14,15},{1,0},{3,2},... | collective-permute-start | bytes 98312 | tf_op jit(solution)/shard_map/ppermute | solution.py:390
  18.6 4.4 %collective-permute-done.1.outer_ref = f32[8,8,128]{2,1,0:T(8,128)S(1)} collective-permute-done((f32[8,8,128]{2,1,0:T(8,128)S(1)}, f32[8,8,128]{2,1,0:T(8,128)S(1)}, u32[]{:S(2)}, u32[]{:S(2)}) %collective-permute-start.1) | collective-permute-done | bytes 32800 | tf_op jit(solution)/shard_map/ppermute | solution.py:391
  23.0 0.0 collective-permute-done.inner_ref
  23.0 0.3 pack.1
  23.3 0.0 all-to-all-done
  23.3 13.1 %all_to_all.20 = bf16[4,4,41,4,128]{4,3,2,1,0:T(4,128)(2,1)S(1)} all-to-all(bf16[4,4,41,4,128]{4,3,2,1,0:T(4,128)(2,1)S(1)} %bitcast.24), channel_id=1, replica_groups={{0,64,128,192},{16,80,144,208},{32,96,160,224},{48,112,176,240},{1,17,3..., dimensions={0} | all-to-all | bytes 1343488 | tf_op jit(solution)/shard_map/all_to_all | solution.py:395
  36.5 1.1 %maximum_bitcast_fusion = bf16[4,4,105,4,128]{4,3,2,0,1:T(4,128)(2,1)S(1)} fusion(bf16[4,4,41,4,128]{4,3,2,1,0:T(4,128)(2,1)S(1)} %all_to_all.20, bf16[4,4,64,4,128]{4,3,2,1,0:T(4,128)(2,1)S(1)} %all-to-all-done), kind=kLoop, calls=%fused_computation | loop fusion | flops 860160 | bytes 3440640 | tf_op jit(solution)/shard_map/transpose | solution.py:396
  37.6 1.8 %copy.15 = bf16[4,4,105,4,128]{4,3,2,1,0:T(4,128)(2,1)} copy(bf16[4,4,105,4,128]{4,3,2,0,1:T(4,128)(2,1)S(1)} %maximum_bitcast_fusion) | data formatting | bytes 3440640 | tf_op jit(solution)/shard_map/transpose | solution.py:396
  39.4 0.0 copy-start.5
  39.4 5.3 %all-to-all-start.2 = ((bf16[4,4,105,4,128]{4,3,2,1,0:T(4,128)(2,1)}), bf16[4,4,105,4,128]{4,3,2,1,0:T(4,128)(2,1)S(1)}, u32[]{:S(2)}, u32[]{:S(2)}) async-start(bf16[4,4,105,4,128]{4,3,2,1,0:T(4,128)(2,1)} %copy.15), calls=%async_computation.2 | async-start | bytes 3440640 | tf_op jit(solution)/shard_map/all_to_all | solution.py:397
  44.7 23.1 %all-to-all-done.2 = bf16[4,4,105,4,128]{4,3,2,1,0:T(4,128)(2,1)S(1)} async-done(((bf16[4,4,105,4,128]{4,3,2,1,0:T(4,128)(2,1)}), bf16[4,4,105,4,128]{4,3,2,1,0:T(4,128)(2,1)S(1)}, u32[]{:S(2)}, u32[]{:S(2)}) %all-to-all-start.2) | async-done | bytes 1720352 | tf_op jit(solution)/shard_map/all_to_all | solution.py:397
  67.8 0.0 copy-done.5
  67.8 4.8 %analyse.1 = bf16[16,96,4,128]{3,2,1,0:T(4,128)(2,1)S(1)} custom-call(s32[1]{0:T(128)} %bitcast.tile_ref, s32[1]{0:T(128)} %bitcast.1.core_ref, s32[1,8]{1,0:T(1,128)S(1)} %copy-done.5, bf16[16,105,4,128]{3,2,1,0:T(4,128)(2,1)S(1)} %bitcast.23, f32[8,8,128]{2,1,0:T(8,128)S(1)} %get-tuple-element.17.above_ref, f32[8,8,128]{2,1,0:T(8,128)S(1)} %observe.1.own_ref, ...), custom_call_target="tpu_custom_call" | custom-call | tf_op jit(solution)/shard_map/analyse/pallas_call | solution.py:349
  72.6 32.4 %all_to_all.21.x_ref = bf16[16,96,4,128]{3,2,1,0:T(4,128)(2,1)S(1)} all-to-all(bf16[16,96,4,128]{3,2,1,0:T(4,128)(2,1)S(1)} %analyse.1), channel_id=1, replica_groups=mesh['member'=16,'space'=16] {'member'}, dimensions={0} | all-to-all | bytes 3145728 | tf_op jit(solution)/shard_map/all_to_all | solution.py:401
  105.0 1.3 %join.1 = bf16[4,6,4,8192]{3,2,1,0:T(4,128)(2,1)} custom-call(bf16[16,96,4,128]{3,2,1,0:T(4,128)(2,1)S(1)} %all_to_all.21.x_ref), custom_call_target="tpu_custom_call" | custom-call | tf_op jit(solution)/shard_map/join/pallas_call | solution.py:314
Async XLA Ops:
  0.0 6.7 %copy-start = (bf16[4,4,6,1,8192]{4,1,3,2,0:T(4,128)(2,1)S(1)}, bf16[4,4,6,1,8192]{4,1,3,2,0:T(4,128)(2,1)}, u32[]{:S(2)}) copy-start(bf16[4,4,6,1,8192]{4,1,3,2,0:T(4,128)(2,1)} %param.6) | copy-start | bytes 4718596
  0.0 6.7 %copy-start.1 = (f32[1,8,128]{2,1,0:T(8,128)S(1)}, f32[1,8,128]{2,1,0:T(8,128)}, u32[]{:S(2)}) copy-start(f32[1,8,128]{2,1,0:T(8,128)} %param.7) | copy-start | bytes 12292
  0.0 6.7 %copy-start.2 = (f32[1,8,128]{2,1,0:T(8,128)S(1)}, f32[1,8,128]{2,1,0:T(8,128)}, u32[]{:S(2)}) copy-start(f32[1,8,128]{2,1,0:T(8,128)} %param.8) | copy-start | bytes 12292
  0.0 6.7 %copy-start.3 = (s32[1,8,128]{2,1,0:T(8,128)S(1)}, s32[1,8,128]{2,1,0:T(8,128)}, u32[]{:S(2)}) copy-start(s32[1,8,128]{2,1,0:T(8,128)} %param.9) | copy-start | bytes 12292
  0.0 6.7 %copy-start.4 = (s32[1,8]{1,0:T(1,128)S(1)}, s32[1,8]{1,0:T(1,128)}, u32[]{:S(2)}) copy-start(s32[1,8]{1,0:T(1,128)} %count_ref.1) | copy-start | bytes 100
  2.2 21.1 %all-to-all-start = ((bf16[4,4,64,4,128]{4,3,2,1,0:T(4,128)(2,1)}), bf16[4,4,64,4,128]{4,3,2,1,0:T(4,128)(2,1)S(1)}, u32[]{:S(2)}, u32[]{:S(2)}) async-start(bf16[4,4,64,4,128]{4,3,2,1,0:T(4,128)(2,1)} %bitcast.28), calls=%async_computation | async-start | bytes 2097152 | tf_op jit(solution)/shard_map/all_to_all | solution.py:388
  9.3 13.7 %collective-permute-start.1 = (f32[8,8,128]{2,1,0:T(8,128)S(1)}, f32[8,8,128]{2,1,0:T(8,128)S(1)}, u32[]{:S(2)}, u32[]{:S(2)}) collective-permute-start(f32[8,8,128]{2,1,0:T(8,128)S(1)} %observe.1.own_ref), channel_id=1, source_target_pairs={{1,2},{3,4},{5,6},{7,8},{9,10},{11,12},{13,14},{2,1},{4,3},{6,5},{... | collective-permute-start | bytes 98312 | tf_op jit(solution)/shard_map/ppermute | solution.py:391
  16.9 6.1 %collective-permute-start = (f32[8,8,128]{2,1,0:T(8,128)S(1)}, f32[8,8,128]{2,1,0:T(8,128)S(1)}, u32[]{:S(2)}, u32[]{:S(2)}) collective-permute-start(f32[8,8,128]{2,1,0:T(8,128)S(1)} %observe.1.own_ref), channel_id=1, source_target_pairs={{0,1},{2,3},{4,5},{6,7},{8,9},{10,11},{12,13},{14,15},{1,0},{3,2},... | collective-permute-start | bytes 98312 | tf_op jit(solution)/shard_map/ppermute | solution.py:390
  39.4 28.4 %copy-start.5 = (s32[1,8]{1,0:T(1,128)S(1)}, s32[1,8]{1,0:T(1,128)}, u32[]{:S(2)}) copy-start(s32[1,8]{1,0:T(1,128)} %radius_ref.1) | copy-start | bytes 100
  39.4 28.4 %all-to-all-start.2 = ((bf16[4,4,105,4,128]{4,3,2,1,0:T(4,128)(2,1)}), bf16[4,4,105,4,128]{4,3,2,1,0:T(4,128)(2,1)S(1)}, u32[]{:S(2)}, u32[]{:S(2)}) async-start(bf16[4,4,105,4,128]{4,3,2,1,0:T(4,128)(2,1)} %copy.15), calls=%async_computation.2 | async-start | bytes 3440640 | tf_op jit(solution)/shard_map/all_to_all | solution.py:397

commit v7 on v6

--- a/solution.py
+++ b/solution.py
@@ -16,6 +16,7 @@
 VMEM = pl.BlockSpec(memory_space=pltpu.VMEM)
 SMEM = pl.BlockSpec(memory_space=pltpu.SMEM)
 HBM = pl.BlockSpec(memory_space=pltpu.HBM)
+ANY = pl.BlockSpec(memory_space=pl.ANY)
 PARAMS = pltpu.CompilerParams(vmem_limit_bytes=16 * 1024 * 1024)
 EARLY = 4
 SIDE = 4
@@ -357,6 +358,40 @@
     )(tile, core, radius, pieces, above, here, below)
 
 
+def merge_kernel(early_ref, late_ref, out_ref, sems):
+    ahead, rest = early_ref.shape[2], late_ref.shape[2]
+    copies = []
+    for i in range(SIDE):
+        for j in range(SIDE):
+            copies.append(
+                pltpu.make_async_copy(
+                    early_ref.at[i, j], out_ref.at[j, i, pl.ds(0, ahead)], sems.at[0, i, j]
+                )
+            )
+            copies.append(
+                pltpu.make_async_copy(
+                    late_ref.at[i, j], out_ref.at[j, i, pl.ds(ahead, rest)], sems.at[1, i, j]
+                )
+            )
+    for copy in copies:
+        copy.start()
+    for copy in copies:
+        copy.wait()
+
+
+def merge(early, late):
+    shape = early.shape[:2] + (early.shape[2] + late.shape[2],) + early.shape[3:]
+    return pl.pallas_call(
+        merge_kernel,
+        in_specs=[ANY, ANY],
+        out_specs=ANY,
+        out_shape=jax.ShapeDtypeStruct(shape, early.dtype),
+        scratch_shapes=[pltpu.SemaphoreType.DMA((2, SIDE, SIDE))],
+        compiler_params=PARAMS,
+        name="merge",
+    )(early, late)
+
+
 def hop_groups(rows):
     def group(row, fixed, along_y):
         members = [
@@ -393,7 +428,7 @@
     late = late.reshape((SIDE, SIDE) + late.shape[1:])
     late, early = lax.optimization_barrier((late, early))
     late = lax.all_to_all(late, both, 0, 0, axis_index_groups=groups[0])
-    pieces = jnp.concatenate([early, late], axis=2).swapaxes(0, 1)
+    pieces = merge(early, late)
     pieces = lax.all_to_all(pieces, both, 0, 0, axis_index_groups=groups[1])
     pieces = pieces.reshape((parts,) + pieces.shape[2:])
     tile = (lax.axis_index("member") // share).astype(jnp.int32).reshape(1)

time: 107 us -> 105 us (0.981)
  local copies, waits for them, and re-layouts: 1.83 us -> 0.04 us
  Pallas kernels: 11.1 us -> 12.5 us
  other arithmetic: 1.11 us -> 0 us
    transpose x1 -> x0, local copies, waits for them, and re-layouts: 1.8 us -> none  [on_device(): pieces = jnp.concatenate([early, late], axis=2).swapaxes(0, 1)]
    pallas_call x0 -> x1, Pallas kernels: none -> 1.53 us  [merge(): pl.pallas_call(merge_kernel, in_specs=[ANY, ANY], out_specs=ANY, out_shap...]
    transpose x1 -> x0, other arithmetic: 1.11 us -> none  [on_device(): pieces = jnp.concatenate([early, late], axis=2).swapaxes(0, 1)]
where the time goes in v7:
time: 105 us
  blocking collectives  45.5 us (43%)
  waiting for transfers between devices  27.5 us (26%)
  starting transfers between devices  19.1 us (18%)
  Pallas kernels  12.5 us (12%)
    all_to_all x1, blocking collectives, on_device(): out = join(lax.all_to_all(mixed, 'member', 0, 0), fields.shape)  32.4 us
    all_to_all x1, waiting for transfers between devices, on_device(): pieces = lax.all_to_all(pieces, both, 0, 0, axis_index_groups=groups[1])  23.1 us
    all_to_all x1, blocking collectives, on_device(): late = lax.all_to_all(late, both, 0, 0, axis_index_groups=groups[0])  13.1 us
    ppermute x1, starting transfers between devices, on_device(): outer = lax.ppermute(here, 'space', swap[1])  7.58 us
    all_to_all x1, starting transfers between devices, on_device(): pieces = lax.all_to_all(pieces, both, 0, 0, axis_index_groups=groups[1])  5.2 us
    pallas_call x1, Pallas kernels, analyse(): pl.pallas_call(functools.partial(analyse_kernel, kinds), in_specs=[SMEM]...  4.76 us
    all_to_all x1, starting transfers between devices, on_device(): early = lax.all_to_all(early, both, 0, 0, axis_index_groups=groups[0])  4.61 us
    ppermute x1, waiting for transfers between devices, on_device(): outer = lax.ppermute(here, 'space', swap[1])  4.41 us
  transfers between devices with their start and end apart: 4, of which 2 were waited for; matrix products, arithmetic and copies ran while one was open for 0% of the time, Pallas kernels for 3%

profile of v7, /device:TPU:2, one launch (start us, length us, event | category | flops | bytes accessed | tf_op | source)
XLA Modules:
  0.0 104.8 jit_solution(14728636213945808516)
XLA Ops:
  0.0 2.1 %split.1 = bf16[16,64,4,128]{3,2,1,0:T(4,128)(2,1)} custom-call(s32[1]{0:T(128)} %bitcast.1.core_ref, bf16[4,6,4,8192]{3,2,1,0:T(4,128)(2,1)} %bitcast.18), custom_call_target="tpu_custom_call" | custom-call | tf_op jit(solution)/shard_map/split/pallas_call | solution.py:298
  2.1 0.0 copy-start
  2.1 0.0 copy-start.1
  2.1 0.0 copy-start.2
  2.1 0.0 copy-start.3
  2.1 0.0 copy-start.4
  2.2 4.6 %all-to-all-start = ((bf16[4,4,64,4,128]{4,3,2,1,0:T(4,128)(2,1)}), bf16[4,4,64,4,128]{4,3,2,1,0:T(4,128)(2,1)S(1)}, u32[]{:S(2)}, u32[]{:S(2)}) async-start(bf16[4,4,64,4,128]{4,3,2,1,0:T(4,128)(2,1)} %bitcast.26), calls=%async_computation | async-start | bytes 2097152 | tf_op jit(solution)/shard_map/all_to_all | solution.py:423
  6.8 0.0 copy-done
  6.8 0.0 copy-done.1
  6.8 0.0 copy-done.2
  6.8 0.0 copy-done.3
  6.8 0.0 copy-done.4
  6.8 2.6 %observe.1.own_ref = f32[8,8,128]{2,1,0:T(8,128)S(1)} custom-call(bf16[4,6,4,8192]{3,2,1,0:T(4,128)(2,1)S(1)} %bitcast.19, f32[8,128]{1,0:T(8,128)S(1)} %bitcast.23, f32[8,128]{1,0:T(8,128)S(1)} %bitcast.24, s32[8,128]{1,0:T(8,128)S(1)} %bitcast.25, s32[1,8]{1,0:T(1,128)S(1)} %copy-done.4), custom_call_target="tpu_custom_call" | custom-call | tf_op jit(solution)/shard_map/observe/pallas_call | solution.py:278
  9.4 7.6 %collective-permute-start.1 = (f32[8,8,128]{2,1,0:T(8,128)S(1)}, f32[8,8,128]{2,1,0:T(8,128)S(1)}, u32[]{:S(2)}, u32[]{:S(2)}) collective-permute-start(f32[8,8,128]{2,1,0:T(8,128)S(1)} %observe.1.own_ref), channel_id=1, source_target_pairs={{1,2},{3,4},{5,6},{7,8},{9,10},{11,12},{13,14},{2,1},{4,3},{6,5},{... | collective-permute-start | bytes 98312 | tf_op jit(solution)/shard_map/ppermute | solution.py:426
  17.0 1.7 %collective-permute-start = (f32[8,8,128]{2,1,0:T(8,128)S(1)}, f32[8,8,128]{2,1,0:T(8,128)S(1)}, u32[]{:S(2)}, u32[]{:S(2)}) collective-permute-start(f32[8,8,128]{2,1,0:T(8,128)S(1)} %observe.1.own_ref), channel_id=1, source_target_pairs={{0,1},{2,3},{4,5},{6,7},{8,9},{10,11},{12,13},{14,15},{1,0},{3,2},... | collective-permute-start | bytes 98312 | tf_op jit(solution)/shard_map/ppermute | solution.py:425
  18.7 4.4 %collective-permute-done.1.outer_ref = f32[8,8,128]{2,1,0:T(8,128)S(1)} collective-permute-done((f32[8,8,128]{2,1,0:T(8,128)S(1)}, f32[8,8,128]{2,1,0:T(8,128)S(1)}, u32[]{:S(2)}, u32[]{:S(2)}) %collective-permute-start.1) | collective-permute-done | bytes 32800 | tf_op jit(solution)/shard_map/ppermute | solution.py:426
  23.1 0.0 collective-permute-done.inner_ref
  23.1 0.3 pack.1
  23.4 0.0 all-to-all-done.early_ref
  23.4 13.1 %all_to_all.20.late_ref = bf16[4,4,41,4,128]{4,3,2,1,0:T(4,128)(2,1)S(1)} all-to-all(bf16[4,4,41,4,128]{4,3,2,1,0:T(4,128)(2,1)S(1)} %bitcast.22), channel_id=1, replica_groups={{0,64,128,192},{16,80,144,208},{32,96,160,224},{48,112,176,240},{1,17,3..., dimensions={0} | all-to-all | bytes 1343488 | tf_op jit(solution)/shard_map/all_to_all | solution.py:430
  36.5 1.5 %merge.1 = bf16[4,4,105,4,128]{4,3,2,1,0:T(4,128)(2,1)} custom-call(bf16[4,4,64,4,128]{4,3,2,1,0:T(4,128)(2,1)S(1)} %all-to-all-done.early_ref, bf16[4,4,41,4,128]{4,3,2,1,0:T(4,128)(2,1)S(1)} %all_to_all.20.late_ref), custom_call_target="tpu_custom_call" | custom-call | tf_op jit(solution)/shard_map/merge/pallas_call | solution.py:384
  38.0 0.0 copy-start.5
  38.1 5.2 %all-to-all-start.2 = ((bf16[4,4,105,4,128]{4,3,2,1,0:T(4,128)(2,1)}), bf16[4,4,105,4,128]{4,3,2,1,0:T(4,128)(2,1)S(1)}, u32[]{:S(2)}, u32[]{:S(2)}) async-start(bf16[4,4,105,4,128]{4,3,2,1,0:T(4,128)(2,1)} %merge.1), calls=%async_computation.2 | async-start | bytes 3440640 | tf_op jit(solution)/shard_map/all_to_all | solution.py:432
  43.3 23.1 %all-to-all-done.2 = bf16[4,4,105,4,128]{4,3,2,1,0:T(4,128)(2,1)S(1)} async-done(((bf16[4,4,105,4,128]{4,3,2,1,0:T(4,128)(2,1)}), bf16[4,4,105,4,128]{4,3,2,1,0:T(4,128)(2,1)S(1)}, u32[]{:S(2)}, u32[]{:S(2)}) %all-to-all-start.2) | async-done | bytes 1720352 | tf_op jit(solution)/shard_map/all_to_all | solution.py:432
  66.4 0.0 copy-done.5
  66.4 4.8 %analyse.1 = bf16[16,96,4,128]{3,2,1,0:T(4,128)(2,1)S(1)} custom-call(s32[1]{0:T(128)} %bitcast.tile_ref, s32[1]{0:T(128)} %bitcast.1.core_ref, s32[1,8]{1,0:T(1,128)S(1)} %copy-done.5, bf16[16,105,4,128]{3,2,1,0:T(4,128)(2,1)S(1)} %bitcast.21, f32[8,8,128]{2,1,0:T(8,128)S(1)} %get-tuple-element.17.above_ref, f32[8,8,128]{2,1,0:T(8,128)S(1)} %observe.1.own_ref, ...), custom_call_target="tpu_custom_call" | custom-call | tf_op jit(solution)/shard_map/analyse/pallas_call | solution.py:350
  71.1 32.4 %all_to_all.21.x_ref = bf16[16,96,4,128]{3,2,1,0:T(4,128)(2,1)S(1)} all-to-all(bf16[16,96,4,128]{3,2,1,0:T(4,128)(2,1)S(1)} %analyse.1), channel_id=1, replica_groups=mesh['member'=16,'space'=16] {'member'}, dimensions={0} | all-to-all | bytes 3145728 | tf_op jit(solution)/shard_map/all_to_all | solution.py:436
  103.5 1.3 %join.1 = bf16[4,6,4,8192]{3,2,1,0:T(4,128)(2,1)} custom-call(bf16[16,96,4,128]{3,2,1,0:T(4,128)(2,1)S(1)} %all_to_all.21.x_ref), custom_call_target="tpu_custom_call" | custom-call | tf_op jit(solution)/shard_map/join/pallas_call | solution.py:315
Async XLA Ops:
  2.1 4.7 %copy-start = (bf16[4,4,6,1,8192]{4,1,3,2,0:T(4,128)(2,1)S(1)}, bf16[4,4,6,1,8192]{4,1,3,2,0:T(4,128)(2,1)}, u32[]{:S(2)}) copy-start(bf16[4,4,6,1,8192]{4,1,3,2,0:T(4,128)(2,1)} %param.6) | copy-start | bytes 4718596
  2.1 4.7 %copy-start.1 = (f32[1,8,128]{2,1,0:T(8,128)S(1)}, f32[1,8,128]{2,1,0:T(8,128)}, u32[]{:S(2)}) copy-start(f32[1,8,128]{2,1,0:T(8,128)} %param.7) | copy-start | bytes 12292
  2.1 4.7 %copy-start.2 = (f32[1,8,128]{2,1,0:T(8,128)S(1)}, f32[1,8,128]{2,1,0:T(8,128)}, u32[]{:S(2)}) copy-start(f32[1,8,128]{2,1,0:T(8,128)} %param.8) | copy-start | bytes 12292
  2.1 4.6 %copy-start.3 = (s32[1,8,128]{2,1,0:T(8,128)S(1)}, s32[1,8,128]{2,1,0:T(8,128)}, u32[]{:S(2)}) copy-start(s32[1,8,128]{2,1,0:T(8,128)} %param.9) | copy-start | bytes 12292
  2.1 4.6 %copy-start.4 = (s32[1,8]{1,0:T(1,128)S(1)}, s32[1,8]{1,0:T(1,128)}, u32[]{:S(2)}) copy-start(s32[1,8]{1,0:T(1,128)} %count_ref.1) | copy-start | bytes 100
  2.2 21.2 %all-to-all-start = ((bf16[4,4,64,4,128]{4,3,2,1,0:T(4,128)(2,1)}), bf16[4,4,64,4,128]{4,3,2,1,0:T(4,128)(2,1)S(1)}, u32[]{:S(2)}, u32[]{:S(2)}) async-start(bf16[4,4,64,4,128]{4,3,2,1,0:T(4,128)(2,1)} %bitcast.26), calls=%async_computation | async-start | bytes 2097152 | tf_op jit(solution)/shard_map/all_to_all | solution.py:423
  9.4 13.7 %collective-permute-start.1 = (f32[8,8,128]{2,1,0:T(8,128)S(1)}, f32[8,8,128]{2,1,0:T(8,128)S(1)}, u32[]{:S(2)}, u32[]{:S(2)}) collective-permute-start(f32[8,8,128]{2,1,0:T(8,128)S(1)} %observe.1.own_ref), channel_id=1, source_target_pairs={{1,2},{3,4},{5,6},{7,8},{9,10},{11,12},{13,14},{2,1},{4,3},{6,5},{... | collective-permute-start | bytes 98312 | tf_op jit(solution)/shard_map/ppermute | solution.py:426
  17.0 6.1 %collective-permute-start = (f32[8,8,128]{2,1,0:T(8,128)S(1)}, f32[8,8,128]{2,1,0:T(8,128)S(1)}, u32[]{:S(2)}, u32[]{:S(2)}) collective-permute-start(f32[8,8,128]{2,1,0:T(8,128)S(1)} %observe.1.own_ref), channel_id=1, source_target_pairs={{0,1},{2,3},{4,5},{6,7},{8,9},{10,11},{12,13},{14,15},{1,0},{3,2},... | collective-permute-start | bytes 98312 | tf_op jit(solution)/shard_map/ppermute | solution.py:425
  38.0 28.3 %copy-start.5 = (s32[1,8]{1,0:T(1,128)S(1)}, s32[1,8]{1,0:T(1,128)}, u32[]{:S(2)}) copy-start(s32[1,8]{1,0:T(1,128)} %radius_ref.1) | copy-start | bytes 100
  38.1 28.3 %all-to-all-start.2 = ((bf16[4,4,105,4,128]{4,3,2,1,0:T(4,128)(2,1)}), bf16[4,4,105,4,128]{4,3,2,1,0:T(4,128)(2,1)S(1)}, u32[]{:S(2)}, u32[]{:S(2)}) async-start(bf16[4,4,105,4,128]{4,3,2,1,0:T(4,128)(2,1)} %merge.1), calls=%async_computation.2 | async-start | bytes 3440640 | tf_op jit(solution)/shard_map/all_to_all | solution.py:432

commit v8 on v7

--- a/solution.py
+++ b/solution.py
@@ -18,7 +18,7 @@
 HBM = pl.BlockSpec(memory_space=pltpu.HBM)
 ANY = pl.BlockSpec(memory_space=pl.ANY)
 PARAMS = pltpu.CompilerParams(vmem_limit_bytes=16 * 1024 * 1024)
-EARLY = 4
+EARLY = 3
 SIDE = 4
 
 
@@ -77,28 +77,32 @@
 
 
 def observe_kernel(x_ref, value_ref, precision_ref, cell_ref, count_ref, out_ref):
-    own, fields, levels, cells = x_ref.shape
-    slots = out_ref.shape[-1]
-    tile = pl.program_id(0)
-    cell = cell_ref[pl.ds(tile, 1), :]
+    own, kinds, levels, width = x_ref.shape
+    tiles, slots = cell_ref.shape
+    cells = width // tiles
+    cell = cell_ref[...]
     in_tile = cell % cells
     level_field = cell // cells
-    wanted = (level_field % fields) * levels + level_field // fields
-    onehot = lax.broadcasted_iota(jnp.int32, (cells, slots), 0) == in_tile
-    rows = x_ref[...].reshape(own * fields * levels, cells)
-    found = jnp.dot(rows, onehot.astype(rows.dtype), preferred_element_type=jnp.float32)
-    found = found.reshape(own, fields * levels, slots)
-    match = lax.broadcasted_iota(jnp.int32, (fields * levels, slots), 0) == wanted
-    picked = jnp.sum(jnp.where(match[None], found, 0.0), axis=1)
-    used = lax.broadcasted_iota(jnp.int32, (1, slots), 1) < count_ref[0, tile]
-    active = jnp.where(used, precision_ref[pl.ds(tile, 1), :], 0.0)
+    wanted = (level_field % kinds) * levels + level_field // kinds
     row_place = (in_tile // TILE_SIDE).astype(jnp.float32)
     col_place = (in_tile % TILE_SIDE).astype(jnp.float32)
-    out_ref[0, 0:own, :] = picked
-    out_ref[0, own : own + 1, :] = value_ref[pl.ds(tile, 1), :]
-    out_ref[0, own + 1 : own + 2, :] = active
-    out_ref[0, own + 2 : own + 3, :] = row_place
-    out_ref[0, own + 3 : own + 4, :] = col_place
+    place_id = lax.broadcasted_iota(jnp.int32, (cells, slots), 0)
+    field_id = lax.broadcasted_iota(jnp.int32, (kinds * levels, slots), 0)
+    slot_id = lax.broadcasted_iota(jnp.int32, (1, slots), 1)
+    for tile in range(tiles):
+        at = slice(tile, tile + 1)
+        onehot = (place_id == in_tile[at]).astype(x_ref.dtype)
+        rows = x_ref[:, :, :, tile * cells : (tile + 1) * cells].reshape(-1, cells)
+        found = jnp.dot(rows, onehot, preferred_element_type=jnp.float32)
+        found = found.reshape(own, kinds * levels, slots)
+        match = field_id == wanted[at]
+        out_ref[tile, 0:own, :] = jnp.sum(jnp.where(match[None], found, 0.0), axis=1)
+        out_ref[tile, own : own + 1, :] = value_ref[at, :]
+        out_ref[tile, own + 1 : own + 2, :] = jnp.where(
+            slot_id < count_ref[0, tile], precision_ref[at, :], 0.0
+        )
+        out_ref[tile, own + 2 : own + 3, :] = row_place[at]
+        out_ref[tile, own + 3 : own + 4, :] = col_place[at]
 
 
 def pack_kernel(
@@ -272,20 +276,12 @@
 
 
 def observe(fields, values, precision, cells, count):
-    own, kinds, levels, width = fields.shape
+    own = fields.shape[0]
     tiles, slots = cells.shape
-    whole = pl.BlockSpec((tiles, slots), lambda t: (0, 0))
     return pl.pallas_call(
         observe_kernel,
-        grid=(tiles,),
-        in_specs=[
-            pl.BlockSpec((own, kinds, levels, TILE_CELLS), lambda t: (0, 0, 0, t)),
-            whole,
-            whole,
-            whole,
-            pl.BlockSpec(memory_space=pltpu.SMEM),
-        ],
-        out_specs=pl.BlockSpec((1, own + 4, slots), lambda t: (t, 0, 0)),
+        in_specs=[VMEM] * 4 + [SMEM],
+        out_specs=VMEM,
         out_shape=jax.ShapeDtypeStruct((tiles, own + 4, slots), jnp.float32),
         compiler_params=PARAMS,
         name="observe",

time: 105 us -> 105 us (level)
  blocking collectives: 45.5 us -> 47.6 us
  Pallas kernels: 12.5 us -> 11.4 us
    all_to_all x1, blocking collectives: 13.1 us -> 14.5 us  [on_device(): late = lax.all_to_all(late, both, 0, 0, axis_index_groups=groups[0])]
    pallas_call x1, Pallas kernels: 2.57 us -> 1.32 us  [observe(): pl.pallas_call(observe_kernel, in_specs=[VMEM] * 4 + [SMEM], out_specs=VM...]
  transfers between devices with their start and end apart: 4 -> 4, of which waited for: 2 -> 2; matrix products, arithmetic and copies ran while one was open for 0% -> 0% of each run, Pallas kernels for 3% -> 2%
where the time goes in v8:
time: 105 us; the launch traced here: 104 us
  blocking collectives  47.6 us (45%)
  waiting for transfers between devices  26.6 us (25%)
  starting transfers between devices  18.6 us (18%)
  Pallas kernels  11.4 us (11%)
    all_to_all x1, blocking collectives, on_device(): out = join(lax.all_to_all(mixed, 'member', 0, 0), fields.shape)  33.1 us
    all_to_all x1, waiting for transfers between devices, on_device(): pieces = lax.all_to_all(pieces, both, 0, 0, axis_index_groups=groups[1])  23.1 us
    all_to_all x1, blocking collectives, on_device(): late = lax.all_to_all(late, both, 0, 0, axis_index_groups=groups[0])  14.5 us
    ppermute x1, starting transfers between devices, on_device(): outer = lax.ppermute(here, 'space', swap[1])  7.57 us
    all_to_all x1, starting transfers between devices, on_device(): pieces = lax.all_to_all(pieces, both, 0, 0, axis_index_groups=groups[1])  4.85 us
    pallas_call x1, Pallas kernels, analyse(): pl.pallas_call(functools.partial(analyse_kernel, kinds), in_specs=[SMEM]...  4.76 us
    all_to_all x1, starting transfers between devices, on_device(): early = lax.all_to_all(early, both, 0, 0, axis_index_groups=groups[0])  4.48 us
    ppermute x1, waiting for transfers between devices, on_device(): outer = lax.ppermute(here, 'space', swap[1])  3.53 us
  transfers between devices with their start and end apart: 4, of which 2 were waited for; matrix products, arithmetic and copies ran while one was open for 0% of the time, Pallas kernels for 2%

profile of v8, /device:TPU:2, one launch (start us, length us, event | category | flops | bytes accessed | tf_op | source)
XLA Modules:
  0.0 104.4 jit_solution(5554482856686751854)
XLA Ops:
  0.0 0.0 copy-start
  0.0 0.0 copy-start.1
  0.0 0.0 copy-start.2
  0.0 0.0 copy-start.3
  0.0 0.0 copy-start.4
  0.0 2.1 %split.1 = bf16[16,48,4,128]{3,2,1,0:T(4,128)(2,1)} custom-call(s32[1]{0:T(128)} %bitcast.1.core_ref, bf16[4,6,4,8192]{3,2,1,0:T(4,128)(2,1)} %bitcast.18), custom_call_target="tpu_custom_call" | custom-call | tf_op jit(solution)/shard_map/split/pallas_call | solution.py:294
  2.1 4.5 %all-to-all-start = ((bf16[4,4,48,4,128]{4,3,2,1,0:T(4,128)(2,1)}), bf16[4,4,48,4,128]{4,3,2,1,0:T(4,128)(2,1)S(1)}, u32[]{:S(2)}, u32[]{:S(2)}) async-start(bf16[4,4,48,4,128]{4,3,2,1,0:T(4,128)(2,1)} %bitcast.26), calls=%async_computation | async-start | bytes 1572864 | tf_op jit(solution)/shard_map/all_to_all | solution.py:419
  6.6 0.0 copy-done
  6.6 0.0 copy-done.1
  6.6 0.0 copy-done.2
  6.6 0.0 copy-done.3
  6.6 0.0 copy-done.4
  6.6 1.3 %observe.1.own_ref = f32[8,8,128]{2,1,0:T(8,128)S(1)} custom-call(bf16[4,6,4,8192]{3,2,1,0:T(4,128)(2,1)S(1)} %bitcast.19, f32[8,128]{1,0:T(8,128)S(1)} %bitcast.23, f32[8,128]{1,0:T(8,128)S(1)} %bitcast.24, s32[8,128]{1,0:T(8,128)S(1)} %bitcast.25, s32[1,8]{1,0:T(1,128)S(1)} %copy-done.4), custom_call_target="tpu_custom_call" | custom-call | tf_op jit(solution)/shard_map/observe/pallas_call | solution.py:281
  8.0 7.6 %collective-permute-start.1 = (f32[8,8,128]{2,1,0:T(8,128)S(1)}, f32[8,8,128]{2,1,0:T(8,128)S(1)}, u32[]{:S(2)}, u32[]{:S(2)}) collective-permute-start(f32[8,8,128]{2,1,0:T(8,128)S(1)} %observe.1.own_ref), channel_id=1, source_target_pairs={{1,2},{3,4},{5,6},{7,8},{9,10},{11,12},{13,14},{2,1},{4,3},{6,5},{... | collective-permute-start | bytes 98312 | tf_op jit(solution)/shard_map/ppermute | solution.py:422
  15.5 1.7 %collective-permute-start = (f32[8,8,128]{2,1,0:T(8,128)S(1)}, f32[8,8,128]{2,1,0:T(8,128)S(1)}, u32[]{:S(2)}, u32[]{:S(2)}) collective-permute-start(f32[8,8,128]{2,1,0:T(8,128)S(1)} %observe.1.own_ref), channel_id=1, source_target_pairs={{0,1},{2,3},{4,5},{6,7},{8,9},{10,11},{12,13},{14,15},{1,0},{3,2},... | collective-permute-start | bytes 98312 | tf_op jit(solution)/shard_map/ppermute | solution.py:421
  17.3 3.5 %collective-permute-done.1.outer_ref = f32[8,8,128]{2,1,0:T(8,128)S(1)} collective-permute-done((f32[8,8,128]{2,1,0:T(8,128)S(1)}, f32[8,8,128]{2,1,0:T(8,128)S(1)}, u32[]{:S(2)}, u32[]{:S(2)}) %collective-permute-start.1) | collective-permute-done | bytes 32800 | tf_op jit(solution)/shard_map/ppermute | solution.py:422
  20.8 0.0 collective-permute-done.inner_ref
  20.8 0.4 pack.1
  21.2 0.0 all-to-all-done.early_ref
  21.2 14.5 %all_to_all.20.late_ref = bf16[4,4,57,4,128]{4,3,2,1,0:T(4,128)(2,1)S(1)} all-to-all(bf16[4,4,57,4,128]{4,3,2,1,0:T(4,128)(2,1)S(1)} %bitcast.22), channel_id=1, replica_groups={{0,64,128,192},{16,80,144,208},{32,96,160,224},{48,112,176,240},{1,17,3..., dimensions={0} | all-to-all | bytes 1867776 | tf_op jit(solution)/shard_map/all_to_all | solution.py:426
  35.7 1.5 %merge.1 = bf16[4,4,105,4,128]{4,3,2,1,0:T(4,128)(2,1)} custom-call(bf16[4,4,48,4,128]{4,3,2,1,0:T(4,128)(2,1)S(1)} %all-to-all-done.early_ref, bf16[4,4,57,4,128]{4,3,2,1,0:T(4,128)(2,1)S(1)} %all_to_all.20.late_ref), custom_call_target="tpu_custom_call" | custom-call | tf_op jit(solution)/shard_map/merge/pallas_call | solution.py:380
  37.3 0.0 copy-start.5
  37.3 4.9 %all-to-all-start.2 = ((bf16[4,4,105,4,128]{4,3,2,1,0:T(4,128)(2,1)}), bf16[4,4,105,4,128]{4,3,2,1,0:T(4,128)(2,1)S(1)}, u32[]{:S(2)}, u32[]{:S(2)}) async-start(bf16[4,4,105,4,128]{4,3,2,1,0:T(4,128)(2,1)} %merge.1), calls=%async_computation.2 | async-start | bytes 3440640 | tf_op jit(solution)/shard_map/all_to_all | solution.py:428
  42.1 23.1 %all-to-all-done.2 = bf16[4,4,105,4,128]{4,3,2,1,0:T(4,128)(2,1)S(1)} async-done(((bf16[4,4,105,4,128]{4,3,2,1,0:T(4,128)(2,1)}), bf16[4,4,105,4,128]{4,3,2,1,0:T(4,128)(2,1)S(1)}, u32[]{:S(2)}, u32[]{:S(2)}) %all-to-all-start.2) | async-done | bytes 1720352 | tf_op jit(solution)/shard_map/all_to_all | solution.py:428
  65.2 0.0 copy-done.5
  65.2 4.8 %analyse.1 = bf16[16,96,4,128]{3,2,1,0:T(4,128)(2,1)S(1)} custom-call(s32[1]{0:T(128)} %bitcast.tile_ref, s32[1]{0:T(128)} %bitcast.1.core_ref, s32[1,8]{1,0:T(1,128)S(1)} %copy-done.5, bf16[16,105,4,128]{3,2,1,0:T(4,128)(2,1)S(1)} %bitcast.21, f32[8,8,128]{2,1,0:T(8,128)S(1)} %get-tuple-element.17.above_ref, f32[8,8,128]{2,1,0:T(8,128)S(1)} %observe.1.own_ref, ...), custom_call_target="tpu_custom_call" | custom-call | tf_op jit(solution)/shard_map/analyse/pallas_call | solution.py:346
  70.0 33.1 %all_to_all.21.x_ref = bf16[16,96,4,128]{3,2,1,0:T(4,128)(2,1)S(1)} all-to-all(bf16[16,96,4,128]{3,2,1,0:T(4,128)(2,1)S(1)} %analyse.1), channel_id=1, replica_groups=mesh['member'=16,'space'=16] {'member'}, dimensions={0} | all-to-all | bytes 3145728 | tf_op jit(solution)/shard_map/all_to_all | solution.py:432
  103.1 1.3 %join.1 = bf16[4,6,4,8192]{3,2,1,0:T(4,128)(2,1)} custom-call(bf16[16,96,4,128]{3,2,1,0:T(4,128)(2,1)S(1)} %all_to_all.21.x_ref), custom_call_target="tpu_custom_call" | custom-call | tf_op jit(solution)/shard_map/join/pallas_call | solution.py:311
Async XLA Ops:
  0.0 6.6 %copy-start = (bf16[4,4,6,1,8192]{4,1,3,2,0:T(4,128)(2,1)S(1)}, bf16[4,4,6,1,8192]{4,1,3,2,0:T(4,128)(2,1)}, u32[]{:S(2)}) copy-start(bf16[4,4,6,1,8192]{4,1,3,2,0:T(4,128)(2,1)} %param.6) | copy-start | bytes 4718596
  0.0 6.6 %copy-start.1 = (f32[1,8,128]{2,1,0:T(8,128)S(1)}, f32[1,8,128]{2,1,0:T(8,128)}, u32[]{:S(2)}) copy-start(f32[1,8,128]{2,1,0:T(8,128)} %param.7) | copy-start | bytes 12292
  0.0 6.6 %copy-start.2 = (f32[1,8,128]{2,1,0:T(8,128)S(1)}, f32[1,8,128]{2,1,0:T(8,128)}, u32[]{:S(2)}) copy-start(f32[1,8,128]{2,1,0:T(8,128)} %param.8) | copy-start | bytes 12292
  0.0 6.6 %copy-start.3 = (s32[1,8,128]{2,1,0:T(8,128)S(1)}, s32[1,8,128]{2,1,0:T(8,128)}, u32[]{:S(2)}) copy-start(s32[1,8,128]{2,1,0:T(8,128)} %param.9) | copy-start | bytes 12292
  0.0 6.6 %copy-start.4 = (s32[1,8]{1,0:T(1,128)S(1)}, s32[1,8]{1,0:T(1,128)}, u32[]{:S(2)}) copy-start(s32[1,8]{1,0:T(1,128)} %count_ref.1) | copy-start | bytes 100
  2.1 19.0 %all-to-all-start = ((bf16[4,4,48,4,128]{4,3,2,1,0:T(4,128)(2,1)}), bf16[4,4,48,4,128]{4,3,2,1,0:T(4,128)(2,1)S(1)}, u32[]{:S(2)}, u32[]{:S(2)}) async-start(bf16[4,4,48,4,128]{4,3,2,1,0:T(4,128)(2,1)} %bitcast.26), calls=%async_computation | async-start | bytes 1572864 | tf_op jit(solution)/shard_map/all_to_all | solution.py:419
  8.0 12.8 %collective-permute-start.1 = (f32[8,8,128]{2,1,0:T(8,128)S(1)}, f32[8,8,128]{2,1,0:T(8,128)S(1)}, u32[]{:S(2)}, u32[]{:S(2)}) collective-permute-start(f32[8,8,128]{2,1,0:T(8,128)S(1)} %observe.1.own_ref), channel_id=1, source_target_pairs={{1,2},{3,4},{5,6},{7,8},{9,10},{11,12},{13,14},{2,1},{4,3},{6,5},{... | collective-permute-start | bytes 98312 | tf_op jit(solution)/shard_map/ppermute | solution.py:422
  15.5 5.3 %collective-permute-start = (f32[8,8,128]{2,1,0:T(8,128)S(1)}, f32[8,8,128]{2,1,0:T(8,128)S(1)}, u32[]{:S(2)}, u32[]{:S(2)}) collective-permute-start(f32[8,8,128]{2,1,0:T(8,128)S(1)} %observe.1.own_ref), channel_id=1, source_target_pairs={{0,1},{2,3},{4,5},{6,7},{8,9},{10,11},{12,13},{14,15},{1,0},{3,2},... | collective-permute-start | bytes 98312 | tf_op jit(solution)/shard_map/ppermute | solution.py:421
  37.3 28.0 %copy-start.5 = (s32[1,8]{1,0:T(1,128)S(1)}, s32[1,8]{1,0:T(1,128)}, u32[]{:S(2)}) copy-start(s32[1,8]{1,0:T(1,128)} %radius_ref.1) | copy-start | bytes 100
  37.3 28.0 %all-to-all-start.2 = ((bf16[4,4,105,4,128]{4,3,2,1,0:T(4,128)(2,1)}), bf16[4,4,105,4,128]{4,3,2,1,0:T(4,128)(2,1)S(1)}, u32[]{:S(2)}, u32[]{:S(2)}) async-start(bf16[4,4,105,4,128]{4,3,2,1,0:T(4,128)(2,1)} %merge.1), calls=%async_computation.2 | async-start | bytes 3440640 | tf_op jit(solution)/shard_map/all_to_all | solution.py:428

commit v9 on v8

--- a/solution.py
+++ b/solution.py
@@ -272,7 +272,7 @@
             ].reshape(sources, own, levels, LANES)
         return carry
 
-    lax.fori_loop(0, kinds, body, 0)
+    lax.fori_loop(0, kinds, body, 0, unroll=True)
 
 
 def observe(fields, values, precision, cells, count):
@@ -357,18 +357,17 @@
 def merge_kernel(early_ref, late_ref, out_ref, sems):
     ahead, rest = early_ref.shape[2], late_ref.shape[2]
     copies = []
-    for i in range(SIDE):
-        for j in range(SIDE):
-            copies.append(
-                pltpu.make_async_copy(
-                    early_ref.at[i, j], out_ref.at[j, i, pl.ds(0, ahead)], sems.at[0, i, j]
-                )
+    for j in range(SIDE):
+        copies.append(
+            pltpu.make_async_copy(
+                early_ref.at[:, j], out_ref.at[j, :, pl.ds(0, ahead)], sems.at[0, j]
             )
-            copies.append(
-                pltpu.make_async_copy(
-                    late_ref.at[i, j], out_ref.at[j, i, pl.ds(ahead, rest)], sems.at[1, i, j]
-                )
+        )
+        copies.append(
+            pltpu.make_async_copy(
+                late_ref.at[:, j], out_ref.at[j, :, pl.ds(ahead, rest)], sems.at[1, j]
             )
+        )
     for copy in copies:
         copy.start()
     for copy in copies:
@@ -382,7 +381,7 @@
         in_specs=[ANY, ANY],
         out_specs=ANY,
         out_shape=jax.ShapeDtypeStruct(shape, early.dtype),
-        scratch_shapes=[pltpu.SemaphoreType.DMA((2, SIDE, SIDE))],
+        scratch_shapes=[pltpu.SemaphoreType.DMA((2, SIDE))],
         compiler_params=PARAMS,
         name="merge",
     )(early, late)

time: 105 us -> 104 us (level)
  no operation moved by 1% of the time
where the time goes in v9:
time: 104 us; the launch traced here: 103 us
  blocking collectives  47.6 us (46%)
  waiting for transfers between devices  26.6 us (26%)
  starting transfers between devices  18.6 us (18%)
  Pallas kernels  10.4 us (10%)
    all_to_all x1, blocking collectives, on_device(): out = join(lax.all_to_all(mixed, 'member', 0, 0), fields.shape)  33.1 us
    all_to_all x1, waiting for transfers between devices, on_device(): pieces = lax.all_to_all(pieces, both, 0, 0, axis_index_groups=groups[1])  23.1 us
    all_to_all x1, blocking collectives, on_device(): late = lax.all_to_all(late, both, 0, 0, axis_index_groups=groups[0])  14.5 us
    ppermute x1, starting transfers between devices, on_device(): outer = lax.ppermute(here, 'space', swap[1])  7.57 us
    all_to_all x1, starting transfers between devices, on_device(): pieces = lax.all_to_all(pieces, both, 0, 0, axis_index_groups=groups[1])  4.85 us
    all_to_all x1, starting transfers between devices, on_device(): early = lax.all_to_all(early, both, 0, 0, axis_index_groups=groups[0])  4.48 us
    pallas_call x1, Pallas kernels, analyse(): pl.pallas_call(functools.partial(analyse_kernel, kinds), in_specs=[SMEM]...  4.02 us
    ppermute x1, waiting for transfers between devices, on_device(): outer = lax.ppermute(here, 'space', swap[1])  3.53 us
  transfers between devices with their start and end apart: 4, of which 2 were waited for; matrix products, arithmetic and copies ran while one was open for 0% of the time, Pallas kernels for 2%

profile of v9, /device:TPU:2, one launch (start us, length us, event | category | flops | bytes accessed | tf_op | source)
XLA Modules:
  0.0 103.4 jit_solution(5748056935643959565)
XLA Ops:
  0.0 0.0 copy-start
  0.0 0.0 copy-start.1
  0.0 0.0 copy-start.2
  0.0 0.0 copy-start.3
  0.0 0.0 copy-start.4
  0.0 2.1 %split.1 = bf16[16,48,4,128]{3,2,1,0:T(4,128)(2,1)} custom-call(s32[1]{0:T(128)} %bitcast.1.core_ref, bf16[4,6,4,8192]{3,2,1,0:T(4,128)(2,1)} %bitcast.18), custom_call_target="tpu_custom_call" | custom-call | tf_op jit(solution)/shard_map/split/pallas_call | solution.py:294
  2.1 4.5 %all-to-all-start = ((bf16[4,4,48,4,128]{4,3,2,1,0:T(4,128)(2,1)}), bf16[4,4,48,4,128]{4,3,2,1,0:T(4,128)(2,1)S(1)}, u32[]{:S(2)}, u32[]{:S(2)}) async-start(bf16[4,4,48,4,128]{4,3,2,1,0:T(4,128)(2,1)} %bitcast.26), calls=%async_computation | async-start | bytes 1572864 | tf_op jit(solution)/shard_map/all_to_all | solution.py:418
  6.6 0.0 copy-done
  6.6 0.0 copy-done.1
  6.6 0.0 copy-done.2
  6.6 0.0 copy-done.3
  6.6 0.0 copy-done.4
  6.6 1.3 %observe.1.own_ref = f32[8,8,128]{2,1,0:T(8,128)S(1)} custom-call(bf16[4,6,4,8192]{3,2,1,0:T(4,128)(2,1)S(1)} %bitcast.19, f32[8,128]{1,0:T(8,128)S(1)} %bitcast.23, f32[8,128]{1,0:T(8,128)S(1)} %bitcast.24, s32[8,128]{1,0:T(8,128)S(1)} %bitcast.25, s32[1,8]{1,0:T(1,128)S(1)} %copy-done.4), custom_call_target="tpu_custom_call" | custom-call | tf_op jit(solution)/shard_map/observe/pallas_call | solution.py:281
  8.0 7.6 %collective-permute-start.1 = (f32[8,8,128]{2,1,0:T(8,128)S(1)}, f32[8,8,128]{2,1,0:T(8,128)S(1)}, u32[]{:S(2)}, u32[]{:S(2)}) collective-permute-start(f32[8,8,128]{2,1,0:T(8,128)S(1)} %observe.1.own_ref), channel_id=1, source_target_pairs={{1,2},{3,4},{5,6},{7,8},{9,10},{11,12},{13,14},{2,1},{4,3},{6,5},{... | collective-permute-start | bytes 98312 | tf_op jit(solution)/shard_map/ppermute | solution.py:421
  15.5 1.7 %collective-permute-start = (f32[8,8,128]{2,1,0:T(8,128)S(1)}, f32[8,8,128]{2,1,0:T(8,128)S(1)}, u32[]{:S(2)}, u32[]{:S(2)}) collective-permute-start(f32[8,8,128]{2,1,0:T(8,128)S(1)} %observe.1.own_ref), channel_id=1, source_target_pairs={{0,1},{2,3},{4,5},{6,7},{8,9},{10,11},{12,13},{14,15},{1,0},{3,2},... | collective-permute-start | bytes 98312 | tf_op jit(solution)/shard_map/ppermute | solution.py:420
  17.3 3.5 %collective-permute-done.1.outer_ref = f32[8,8,128]{2,1,0:T(8,128)S(1)} collective-permute-done((f32[8,8,128]{2,1,0:T(8,128)S(1)}, f32[8,8,128]{2,1,0:T(8,128)S(1)}, u32[]{:S(2)}, u32[]{:S(2)}) %collective-permute-start.1) | collective-permute-done | bytes 32800 | tf_op jit(solution)/shard_map/ppermute | solution.py:421
  20.8 0.0 collective-permute-done.inner_ref
  20.8 0.4 pack.1
  21.2 0.0 all-to-all-done.early_ref
  21.2 14.5 %all_to_all.20.late_ref = bf16[4,4,57,4,128]{4,3,2,1,0:T(4,128)(2,1)S(1)} all-to-all(bf16[4,4,57,4,128]{4,3,2,1,0:T(4,128)(2,1)S(1)} %bitcast.22), channel_id=1, replica_groups={{0,64,128,192},{16,80,144,208},{32,96,160,224},{48,112,176,240},{1,17,3..., dimensions={0} | all-to-all | bytes 1867776 | tf_op jit(solution)/shard_map/all_to_all | solution.py:425
  35.7 1.3 %merge.1 = bf16[4,4,105,4,128]{4,3,2,1,0:T(4,128)(2,1)} custom-call(bf16[4,4,48,4,128]{4,3,2,1,0:T(4,128)(2,1)S(1)} %all-to-all-done.early_ref, bf16[4,4,57,4,128]{4,3,2,1,0:T(4,128)(2,1)S(1)} %all_to_all.20.late_ref), custom_call_target="tpu_custom_call" | custom-call | tf_op jit(solution)/shard_map/merge/pallas_call | solution.py:379
  37.0 0.0 copy-start.5
  37.0 4.9 %all-to-all-start.2 = ((bf16[4,4,105,4,128]{4,3,2,1,0:T(4,128)(2,1)}), bf16[4,4,105,4,128]{4,3,2,1,0:T(4,128)(2,1)S(1)}, u32[]{:S(2)}, u32[]{:S(2)}) async-start(bf16[4,4,105,4,128]{4,3,2,1,0:T(4,128)(2,1)} %merge.1), calls=%async_computation.2 | async-start | bytes 3440640 | tf_op jit(solution)/shard_map/all_to_all | solution.py:427
  41.9 23.1 %all-to-all-done.2 = bf16[4,4,105,4,128]{4,3,2,1,0:T(4,128)(2,1)S(1)} async-done(((bf16[4,4,105,4,128]{4,3,2,1,0:T(4,128)(2,1)}), bf16[4,4,105,4,128]{4,3,2,1,0:T(4,128)(2,1)S(1)}, u32[]{:S(2)}, u32[]{:S(2)}) %all-to-all-start.2) | async-done | bytes 1720352 | tf_op jit(solution)/shard_map/all_to_all | solution.py:427
  65.0 0.0 copy-done.5
  65.0 4.0 %analyse.1 = bf16[16,96,4,128]{3,2,1,0:T(4,128)(2,1)S(1)} custom-call(s32[1]{0:T(128)} %bitcast.tile_ref, s32[1]{0:T(128)} %bitcast.1.core_ref, s32[1,8]{1,0:T(1,128)S(1)} %copy-done.5, bf16[16,105,4,128]{3,2,1,0:T(4,128)(2,1)S(1)} %bitcast.21, f32[8,8,128]{2,1,0:T(8,128)S(1)} %get-tuple-element.17.above_ref, f32[8,8,128]{2,1,0:T(8,128)S(1)} %observe.1.own_ref, ...), custom_call_target="tpu_custom_call" | custom-call | tf_op jit(solution)/shard_map/analyse/pallas_call | solution.py:346
  69.0 33.1 %all_to_all.21.x_ref = bf16[16,96,4,128]{3,2,1,0:T(4,128)(2,1)S(1)} all-to-all(bf16[16,96,4,128]{3,2,1,0:T(4,128)(2,1)S(1)} %analyse.1), channel_id=1, replica_groups=mesh['member'=16,'space'=16] {'member'}, dimensions={0} | all-to-all | bytes 3145728 | tf_op jit(solution)/shard_map/all_to_all | solution.py:431
  102.1 1.3 %join.1 = bf16[4,6,4,8192]{3,2,1,0:T(4,128)(2,1)} custom-call(bf16[16,96,4,128]{3,2,1,0:T(4,128)(2,1)S(1)} %all_to_all.21.x_ref), custom_call_target="tpu_custom_call" | custom-call | tf_op jit(solution)/shard_map/join/pallas_call | solution.py:311
Async XLA Ops:
  0.0 6.6 %copy-start = (bf16[4,4,6,1,8192]{4,1,3,2,0:T(4,128)(2,1)S(1)}, bf16[4,4,6,1,8192]{4,1,3,2,0:T(4,128)(2,1)}, u32[]{:S(2)}) copy-start(bf16[4,4,6,1,8192]{4,1,3,2,0:T(4,128)(2,1)} %param.6) | copy-start | bytes 4718596
  0.0 6.6 %copy-start.1 = (f32[1,8,128]{2,1,0:T(8,128)S(1)}, f32[1,8,128]{2,1,0:T(8,128)}, u32[]{:S(2)}) copy-start(f32[1,8,128]{2,1,0:T(8,128)} %param.7) | copy-start | bytes 12292
  0.0 6.6 %copy-start.2 = (f32[1,8,128]{2,1,0:T(8,128)S(1)}, f32[1,8,128]{2,1,0:T(8,128)}, u32[]{:S(2)}) copy-start(f32[1,8,128]{2,1,0:T(8,128)} %param.8) | copy-start | bytes 12292
  0.0 6.6 %copy-start.3 = (s32[1,8,128]{2,1,0:T(8,128)S(1)}, s32[1,8,128]{2,1,0:T(8,128)}, u32[]{:S(2)}) copy-start(s32[1,8,128]{2,1,0:T(8,128)} %param.9) | copy-start | bytes 12292
  0.0 6.6 %copy-start.4 = (s32[1,8]{1,0:T(1,128)S(1)}, s32[1,8]{1,0:T(1,128)}, u32[]{:S(2)}) copy-start(s32[1,8]{1,0:T(1,128)} %count_ref.1) | copy-start | bytes 100
  2.1 19.0 %all-to-all-start = ((bf16[4,4,48,4,128]{4,3,2,1,0:T(4,128)(2,1)}), bf16[4,4,48,4,128]{4,3,2,1,0:T(4,128)(2,1)S(1)}, u32[]{:S(2)}, u32[]{:S(2)}) async-start(bf16[4,4,48,4,128]{4,3,2,1,0:T(4,128)(2,1)} %bitcast.26), calls=%async_computation | async-start | bytes 1572864 | tf_op jit(solution)/shard_map/all_to_all | solution.py:418
  8.0 12.8 %collective-permute-start.1 = (f32[8,8,128]{2,1,0:T(8,128)S(1)}, f32[8,8,128]{2,1,0:T(8,128)S(1)}, u32[]{:S(2)}, u32[]{:S(2)}) collective-permute-start(f32[8,8,128]{2,1,0:T(8,128)S(1)} %observe.1.own_ref), channel_id=1, source_target_pairs={{1,2},{3,4},{5,6},{7,8},{9,10},{11,12},{13,14},{2,1},{4,3},{6,5},{... | collective-permute-start | bytes 98312 | tf_op jit(solution)/shard_map/ppermute | solution.py:421
  15.5 5.3 %collective-permute-start = (f32[8,8,128]{2,1,0:T(8,128)S(1)}, f32[8,8,128]{2,1,0:T(8,128)S(1)}, u32[]{:S(2)}, u32[]{:S(2)}) collective-permute-start(f32[8,8,128]{2,1,0:T(8,128)S(1)} %observe.1.own_ref), channel_id=1, source_target_pairs={{0,1},{2,3},{4,5},{6,7},{8,9},{10,11},{12,13},{14,15},{1,0},{3,2},... | collective-permute-start | bytes 98312 | tf_op jit(solution)/shard_map/ppermute | solution.py:420
  37.0 28.0 %copy-start.5 = (s32[1,8]{1,0:T(1,128)S(1)}, s32[1,8]{1,0:T(1,128)}, u32[]{:S(2)}) copy-start(s32[1,8]{1,0:T(1,128)} %radius_ref.1) | copy-start | bytes 100
  37.0 28.0 %all-to-all-start.2 = ((bf16[4,4,105,4,128]{4,3,2,1,0:T(4,128)(2,1)}), bf16[4,4,105,4,128]{4,3,2,1,0:T(4,128)(2,1)S(1)}, u32[]{:S(2)}, u32[]{:S(2)}) async-start(bf16[4,4,105,4,128]{4,3,2,1,0:T(4,128)(2,1)} %merge.1), calls=%async_computation.2 | async-start | bytes 3440640 | tf_op jit(solution)/shard_map/all_to_all | solution.py:427

commit v10 on v9

--- a/solution.py
+++ b/solution.py
@@ -106,8 +106,20 @@
 
 
 def pack_kernel(
-    begin, core_ref, x_ref, inner_ref, own_ref, outer_ref, out_ref, above_ref, below_ref
+    begin,
+    core_ref,
+    tile_ref,
+    radius_ref,
+    x_ref,
+    inner_ref,
+    own_ref,
+    outer_ref,
+    out_ref,
+    above_ref,
+    below_ref,
+    reach_ref,
 ):
+    reach_ref[...] = jnp.full(reach_ref.shape, radius_ref[0, tile_ref[0]], jnp.float32)
     odd = core_ref[0] == 1
     places = [turned(1 - core_ref[0], d) for d in range(out_ref.shape[0])]
     inner, outer = inner_ref[...], outer_ref[...]
@@ -125,7 +137,7 @@
                 ]
         return carry
 
-    lax.fori_loop(begin, x_ref.shape[1], copy_field, 0)
+    lax.fori_loop(begin, x_ref.shape[1], copy_field, 0, unroll=True)
     first = blocks - 9
     tiles = own_ref.shape[0]
     share = parts // tiles
@@ -155,9 +167,9 @@
             a, b, (((1,), (1,)), ((), ())), preferred_element_type=jnp.float32
         )
 
-    return (
-        product(left[0], right[0]) + product(left[0], right[1]) + product(left[1], right[0])
-    )
+    count = left[0].shape[0]
+    both = product(jnp.concatenate(left, axis=0), right[0])
+    return both[:count] + both[count:] + product(left[0], right[1])
 
 
 def doubled_product(left, right):
@@ -169,7 +181,7 @@
 
 
 def analyse_kernel(
-    kinds, tile_ref, core_ref, radius_ref, x_ref, above_ref, own_ref, below_ref, out_ref, mix_ref
+    kinds, tile_ref, core_ref, reach_ref, x_ref, above_ref, own_ref, below_ref, out_ref, mix_ref
 ):
     tile = tile_ref[0]
     tiles = own_ref.shape[0]
@@ -177,7 +189,7 @@
     own = own_ref.shape[1] - 4
     first = x_ref.shape[1] - 9
     members = sources * own
-    reach = radius_ref[0, tile].astype(jnp.float32)
+    reach = reach_ref[0:1, :]
     centre = 0.5 * TILE_SIDE - 0.5
     ensemble, values, weights = [], [], []
     for a, rows_ref in enumerate((above_ref, own_ref, below_ref)):
@@ -322,36 +334,37 @@
     )(pieces)
 
 
-def pack(core, fields, parts, begin, inner, here, outer):
+def pack(core, tile, radius, fields, parts, begin, inner, here, outer):
     own, kinds, levels, width = fields.shape
     blocks = own * (kinds - begin) * (width // parts // LANES) + 9
     small = jax.ShapeDtypeStruct(here.shape, here.dtype)
     return pl.pallas_call(
         functools.partial(pack_kernel, begin),
-        in_specs=[SMEM] + [VMEM] * 4,
-        out_specs=[VMEM] * 3,
+        in_specs=[SMEM] * 3 + [VMEM] * 4,
+        out_specs=[VMEM] * 4,
         out_shape=[
             jax.ShapeDtypeStruct((parts, blocks, levels, LANES), fields.dtype),
             small,
             small,
+            jax.ShapeDtypeStruct((8, LANES), jnp.float32),
         ],
         compiler_params=PARAMS,
         name="pack",
-    )(core, fields, inner, here, outer)
-
-
-def analyse(tile, core, radius, pieces, above, here, below, kinds):
+    )(core, tile, radius, fields, inner, here, outer)
+
+
+def analyse(tile, core, reach, pieces, above, here, below, kinds):
     parts, blocks, levels, lanes = pieces.shape
     wide = parts * (here.shape[1] - 4) * levels
     return pl.pallas_call(
         functools.partial(analyse_kernel, kinds),
-        in_specs=[SMEM] * 3 + [VMEM] * 4,
+        in_specs=[SMEM] * 2 + [VMEM] * 5,
         out_specs=VMEM,
         out_shape=jax.ShapeDtypeStruct((parts, blocks - 9, levels, lanes), pieces.dtype),
         scratch_shapes=[pltpu.VMEM((wide, wide), jnp.bfloat16)],
         compiler_params=PARAMS,
         name="analyse",
-    )(tile, core, radius, pieces, above, here, below)
+    )(tile, core, reach, pieces, above, here, below)
 
 
 def merge_kernel(early_ref, late_ref, out_ref, sems):
@@ -412,6 +425,7 @@
     both = ("member", "space")
     groups = hop_groups(rows)
     core = (lax.axis_index("space") % 2).astype(jnp.int32).reshape(1)
+    tile = (lax.axis_index("member") // share).astype(jnp.int32).reshape(1)
     early = split(core, fields, parts, EARLY)
     early, fields = lax.optimization_barrier((early, fields))
     early = early.reshape((SIDE, SIDE) + early.shape[1:])
@@ -419,15 +433,14 @@
     here = observe(fields, obs_values[0], obs_precision[0], obs_cell[0], obs_count)
     inner = lax.ppermute(here, "space", swap[0])
     outer = lax.ppermute(here, "space", swap[1])
-    late, above, below = pack(core, fields, parts, EARLY, inner, here, outer)
+    late, above, below, reach = pack(core, tile, radius, fields, parts, EARLY, inner, here, outer)
     late = late.reshape((SIDE, SIDE) + late.shape[1:])
     late, early = lax.optimization_barrier((late, early))
     late = lax.all_to_all(late, both, 0, 0, axis_index_groups=groups[0])
     pieces = merge(early, late)
     pieces = lax.all_to_all(pieces, both, 0, 0, axis_index_groups=groups[1])
     pieces = pieces.reshape((parts,) + pieces.shape[2:])
-    tile = (lax.axis_index("member") // share).astype(jnp.int32).reshape(1)
-    mixed = analyse(tile, core, radius, pieces, above, here, below, kinds)
+    mixed = analyse(tile, core, reach, pieces, above, here, below, kinds)
     out = join(lax.all_to_all(mixed, "member", 0, 0), fields.shape)
     return out.reshape(own, kinds, 1, levels, width).transpose(0, 3, 1, 2, 4)
 

time: 104 us -> 103 us (level)
  blocking collectives: 47.6 us -> 75.6 us
  waiting for transfers between devices: 26.6 us -> 3.53 us
  starting transfers between devices: 18.6 us -> 13.8 us
    all_to_all x0 -> x1, blocking collectives: none -> 27.7 us  [on_device(): pieces = lax.all_to_all(pieces, both, 0, 0, axis_index_groups=groups[1])]
    all_to_all x1 -> x0, waiting for transfers between devices: 23.1 us -> none  [on_device(): pieces = lax.all_to_all(pieces, both, 0, 0, axis_index_groups=groups[1])]
    all_to_all x1 -> x0, starting transfers between devices: 4.85 us -> none  [on_device(): pieces = lax.all_to_all(pieces, both, 0, 0, axis_index_groups=groups[1])]
  transfers between devices with their start and end apart: 4 -> 3, of which waited for: 2 -> 1; matrix products, arithmetic and copies ran while one was open for 0% -> 0% of each run, Pallas kernels for 2% -> 2%
where the time goes in v10:
time: 103 us
  blocking collectives  75.6 us (73%)
  starting transfers between devices  13.8 us (13%)
  Pallas kernels  9.6 us (9%)
  waiting for transfers between devices  3.53 us (3%)
    all_to_all x1, blocking collectives, on_device(): out = join(lax.all_to_all(mixed, 'member', 0, 0), fields.shape)  33.3 us
    all_to_all x1, blocking collectives, on_device(): pieces = lax.all_to_all(pieces, both, 0, 0, axis_index_groups=groups[1])  27.7 us
    all_to_all x1, blocking collectives, on_device(): late = lax.all_to_all(late, both, 0, 0, axis_index_groups=groups[0])  14.5 us
    ppermute x1, starting transfers between devices, on_device(): outer = lax.ppermute(here, 'space', swap[1])  7.57 us
    all_to_all x1, starting transfers between devices, on_device(): early = lax.all_to_all(early, both, 0, 0, axis_index_groups=groups[0])  4.48 us
    ppermute x1, waiting for transfers between devices, on_device(): outer = lax.ppermute(here, 'space', swap[1])  3.53 us
    pallas_call x1, Pallas kernels, analyse(): pl.pallas_call(functools.partial(analyse_kernel, kinds), in_specs=[SMEM]...  3.37 us
    pallas_call x1, Pallas kernels, split(): pl.pallas_call(split_kernel, in_specs=[SMEM, HBM], out_specs=HBM, out_sha...  2.1 us
  transfers between devices with their start and end apart: 3, of which 1 were waited for; matrix products, arithmetic and copies ran while one was open for 0% of the time, Pallas kernels for 2%

profile of v10, /device:TPU:2, one launch (start us, length us, event | category | flops | bytes accessed | tf_op | source)
XLA Modules:
  0.0 102.7 jit_solution(10788091869927322768)
XLA Ops:
  0.0 0.0 copy-start
  0.0 0.0 copy-start.1
  0.0 0.0 copy-start.2
  0.0 0.0 copy-start.3
  0.0 0.0 copy-start.4
  0.0 2.1 %split.1 = bf16[16,48,4,128]{3,2,1,0:T(4,128)(2,1)} custom-call(s32[1]{0:T(128)} %bitcast.1.core_ref, bf16[4,6,4,8192]{3,2,1,0:T(4,128)(2,1)} %bitcast.18), custom_call_target="tpu_custom_call" | custom-call | tf_op jit(solution)/shard_map/split/pallas_call | solution.py:306
  2.1 0.0 copy-start.5
  2.1 4.5 %all-to-all-start = ((bf16[4,4,48,4,128]{4,3,2,1,0:T(4,128)(2,1)}), bf16[4,4,48,4,128]{4,3,2,1,0:T(4,128)(2,1)S(1)}, u32[]{:S(2)}, u32[]{:S(2)}) async-start(bf16[4,4,48,4,128]{4,3,2,1,0:T(4,128)(2,1)} %bitcast.26), calls=%async_computation | async-start | bytes 1572864 | tf_op jit(solution)/shard_map/all_to_all | solution.py:432
  6.6 0.0 copy-done
  6.6 0.0 copy-done.1
  6.6 0.0 copy-done.2
  6.6 0.0 copy-done.3
  6.6 0.0 copy-done.4
  6.7 1.3 %observe.1.own_ref = f32[8,8,128]{2,1,0:T(8,128)S(1)} custom-call(bf16[4,6,4,8192]{3,2,1,0:T(4,128)(2,1)S(1)} %bitcast.19, f32[8,128]{1,0:T(8,128)S(1)} %bitcast.23, f32[8,128]{1,0:T(8,128)S(1)} %bitcast.24, s32[8,128]{1,0:T(8,128)S(1)} %bitcast.25, s32[1,8]{1,0:T(1,128)S(1)} %copy-done.4), custom_call_target="tpu_custom_call" | custom-call | tf_op jit(solution)/shard_map/observe/pallas_call | solution.py:293
  8.0 7.6 %collective-permute-start.1 = (f32[8,8,128]{2,1,0:T(8,128)S(1)}, f32[8,8,128]{2,1,0:T(8,128)S(1)}, u32[]{:S(2)}, u32[]{:S(2)}) collective-permute-start(f32[8,8,128]{2,1,0:T(8,128)S(1)} %observe.1.own_ref), channel_id=1, source_target_pairs={{1,2},{3,4},{5,6},{7,8},{9,10},{11,12},{13,14},{2,1},{4,3},{6,5},{... | collective-permute-start | bytes 98312 | tf_op jit(solution)/shard_map/ppermute | solution.py:435
  15.6 1.7 %collective-permute-start = (f32[8,8,128]{2,1,0:T(8,128)S(1)}, f32[8,8,128]{2,1,0:T(8,128)S(1)}, u32[]{:S(2)}, u32[]{:S(2)}) collective-permute-start(f32[8,8,128]{2,1,0:T(8,128)S(1)} %observe.1.own_ref), channel_id=1, source_target_pairs={{0,1},{2,3},{4,5},{6,7},{8,9},{10,11},{12,13},{14,15},{1,0},{3,2},... | collective-permute-start | bytes 98312 | tf_op jit(solution)/shard_map/ppermute | solution.py:434
  17.3 3.5 %collective-permute-done.1.outer_ref = f32[8,8,128]{2,1,0:T(8,128)S(1)} collective-permute-done((f32[8,8,128]{2,1,0:T(8,128)S(1)}, f32[8,8,128]{2,1,0:T(8,128)S(1)}, u32[]{:S(2)}, u32[]{:S(2)}) %collective-permute-start.1) | collective-permute-done | bytes 32800 | tf_op jit(solution)/shard_map/ppermute | solution.py:435
  20.8 0.0 collective-permute-done.inner_ref
  20.8 0.0 copy-done.5
  20.8 0.9 pack.1
  21.7 0.0 all-to-all-done.early_ref
  21.7 14.5 %all_to_all.20.late_ref = bf16[4,4,57,4,128]{4,3,2,1,0:T(4,128)(2,1)S(1)} all-to-all(bf16[4,4,57,4,128]{4,3,2,1,0:T(4,128)(2,1)S(1)} %bitcast.22), channel_id=1, replica_groups={{0,64,128,192},{16,80,144,208},{32,96,160,224},{48,112,176,240},{1,17,3..., dimensions={0} | all-to-all | bytes 1867776 | tf_op jit(solution)/shard_map/all_to_all | solution.py:439
  36.3 0.6 merge.1
  36.9 27.7 %all_to_all.21 = bf16[4,4,105,4,128]{4,3,2,1,0:T(4,128)(2,1)S(1)} all-to-all(bf16[4,4,105,4,128]{4,3,2,1,0:T(4,128)(2,1)S(1)} %merge.1), channel_id=1, replica_groups={{0,16,32,48},{64,80,96,112},{128,144,160,176},{192,208,224,240},{1,65,1..., dimensions={0} | all-to-all | bytes 3440640 | tf_op jit(solution)/shard_map/all_to_all | solution.py:441
  64.7 3.4 %analyse.1 = bf16[16,96,4,128]{3,2,1,0:T(4,128)(2,1)S(1)} custom-call(s32[1]{0:T(128)} %bitcast.tile_ref, s32[1]{0:T(128)} %bitcast.1.core_ref, f32[8,128]{1,0:T(8,128)S(1)} %get-tuple-element.14.reach_ref, bf16[16,105,4,128]{3,2,1,0:T(4,128)(2,1)S(1)} %bitcast.21, f32[8,8,128]{2,1,0:T(8,128)S(1)} %get-tuple-element.19.above_ref, ...), custom_call_target="tpu_custom_call" | custom-call | tf_op jit(solution)/shard_map/analyse/pallas_call | solution.py:359
  68.0 33.3 %all_to_all.22.x_ref = bf16[16,96,4,128]{3,2,1,0:T(4,128)(2,1)S(1)} all-to-all(bf16[16,96,4,128]{3,2,1,0:T(4,128)(2,1)S(1)} %analyse.1), channel_id=1, replica_groups=mesh['member'=16,'space'=16] {'member'}, dimensions={0} | all-to-all | bytes 3145728 | tf_op jit(solution)/shard_map/all_to_all | solution.py:444
  101.4 1.3 %join.1 = bf16[4,6,4,8192]{3,2,1,0:T(4,128)(2,1)} custom-call(bf16[16,96,4,128]{3,2,1,0:T(4,128)(2,1)S(1)} %all_to_all.22.x_ref), custom_call_target="tpu_custom_call" | custom-call | tf_op jit(solution)/shard_map/join/pallas_call | solution.py:323
Async XLA Ops:
  0.0 6.6 %copy-start = (bf16[4,4,6,1,8192]{4,1,3,2,0:T(4,128)(2,1)S(1)}, bf16[4,4,6,1,8192]{4,1,3,2,0:T(4,128)(2,1)}, u32[]{:S(2)}) copy-start(bf16[4,4,6,1,8192]{4,1,3,2,0:T(4,128)(2,1)} %param.6) | copy-start | bytes 4718596
  0.0 6.6 %copy-start.1 = (f32[1,8,128]{2,1,0:T(8,128)S(1)}, f32[1,8,128]{2,1,0:T(8,128)}, u32[]{:S(2)}) copy-start(f32[1,8,128]{2,1,0:T(8,128)} %param.7) | copy-start | bytes 12292
  0.0 6.6 %copy-start.2 = (f32[1,8,128]{2,1,0:T(8,128)S(1)}, f32[1,8,128]{2,1,0:T(8,128)}, u32[]{:S(2)}) copy-start(f32[1,8,128]{2,1,0:T(8,128)} %param.8) | copy-start | bytes 12292
  0.0 6.6 %copy-start.3 = (s32[1,8,128]{2,1,0:T(8,128)S(1)}, s32[1,8,128]{2,1,0:T(8,128)}, u32[]{:S(2)}) copy-start(s32[1,8,128]{2,1,0:T(8,128)} %param.9) | copy-start | bytes 12292
  0.0 6.6 %copy-start.4 = (s32[1,8]{1,0:T(1,128)S(1)}, s32[1,8]{1,0:T(1,128)}, u32[]{:S(2)}) copy-start(s32[1,8]{1,0:T(1,128)} %count_ref.1) | copy-start | bytes 100
  2.1 18.7 %copy-start.5 = (s32[1,8]{1,0:T(1,128)S(1)}, s32[1,8]{1,0:T(1,128)}, u32[]{:S(2)}) copy-start(s32[1,8]{1,0:T(1,128)} %radius_ref.1) | copy-start | bytes 100
  2.1 19.6 %all-to-all-start = ((bf16[4,4,48,4,128]{4,3,2,1,0:T(4,128)(2,1)}), bf16[4,4,48,4,128]{4,3,2,1,0:T(4,128)(2,1)S(1)}, u32[]{:S(2)}, u32[]{:S(2)}) async-start(bf16[4,4,48,4,128]{4,3,2,1,0:T(4,128)(2,1)} %bitcast.26), calls=%async_computation | async-start | bytes 1572864 | tf_op jit(solution)/shard_map/all_to_all | solution.py:432
  8.0 12.8 %collective-permute-start.1 = (f32[8,8,128]{2,1,0:T(8,128)S(1)}, f32[8,8,128]{2,1,0:T(8,128)S(1)}, u32[]{:S(2)}, u32[]{:S(2)}) collective-permute-start(f32[8,8,128]{2,1,0:T(8,128)S(1)} %observe.1.own_ref), channel_id=1, source_target_pairs={{1,2},{3,4},{5,6},{7,8},{9,10},{11,12},{13,14},{2,1},{4,3},{6,5},{... | collective-permute-start | bytes 98312 | tf_op jit(solution)/shard_map/ppermute | solution.py:435
  15.6 5.3 %collective-permute-start = (f32[8,8,128]{2,1,0:T(8,128)S(1)}, f32[8,8,128]{2,1,0:T(8,128)S(1)}, u32[]{:S(2)}, u32[]{:S(2)}) collective-permute-start(f32[8,8,128]{2,1,0:T(8,128)S(1)} %observe.1.own_ref), channel_id=1, source_target_pairs={{0,1},{2,3},{4,5},{6,7},{8,9},{10,11},{12,13},{14,15},{1,0},{3,2},... | collective-permute-start | bytes 98312 | tf_op jit(solution)/shard_map/ppermute | solution.py:434

commit v11 on v10

--- a/solution.py
+++ b/solution.py
@@ -76,7 +76,18 @@
         store.wait()
 
 
-def observe_kernel(x_ref, value_ref, precision_ref, cell_ref, count_ref, out_ref):
+def observe_kernel(
+    x_ref,
+    value_ref,
+    precision_ref,
+    cell_ref,
+    count_ref,
+    tile_ref,
+    radius_ref,
+    out_ref,
+    reach_ref,
+):
+    reach_ref[...] = jnp.full(reach_ref.shape, radius_ref[0, tile_ref[0]], jnp.float32)
     own, kinds, levels, width = x_ref.shape
     tiles, slots = cell_ref.shape
     cells = width // tiles
@@ -108,8 +119,6 @@
 def pack_kernel(
     begin,
     core_ref,
-    tile_ref,
-    radius_ref,
     x_ref,
     inner_ref,
     own_ref,
@@ -117,9 +126,7 @@
     out_ref,
     above_ref,
     below_ref,
-    reach_ref,
 ):
-    reach_ref[...] = jnp.full(reach_ref.shape, radius_ref[0, tile_ref[0]], jnp.float32)
     odd = core_ref[0] == 1
     places = [turned(1 - core_ref[0], d) for d in range(out_ref.shape[0])]
     inner, outer = inner_ref[...], outer_ref[...]
@@ -287,17 +294,20 @@
     lax.fori_loop(0, kinds, body, 0, unroll=True)
 
 
-def observe(fields, values, precision, cells, count):
+def observe(fields, values, precision, cells, count, tile, radius):
     own = fields.shape[0]
     tiles, slots = cells.shape
     return pl.pallas_call(
         observe_kernel,
-        in_specs=[VMEM] * 4 + [SMEM],
-        out_specs=VMEM,
-        out_shape=jax.ShapeDtypeStruct((tiles, own + 4, slots), jnp.float32),
+        in_specs=[VMEM] * 4 + [SMEM] * 3,
+        out_specs=[VMEM] * 2,
+        out_shape=[
+            jax.ShapeDtypeStruct((tiles, own + 4, slots), jnp.float32),
+            jax.ShapeDtypeStruct((8, LANES), jnp.float32),
+        ],
         compiler_params=PARAMS,
         name="observe",
-    )(fields, values, precision, cells, count)
+    )(fields, values, precision, cells, count, tile, radius)
 
 
 def split(core, fields, parts, end):
@@ -334,23 +344,22 @@
     )(pieces)
 
 
-def pack(core, tile, radius, fields, parts, begin, inner, here, outer):
+def pack(core, fields, parts, begin, inner, here, outer):
     own, kinds, levels, width = fields.shape
     blocks = own * (kinds - begin) * (width // parts // LANES) + 9
     small = jax.ShapeDtypeStruct(here.shape, here.dtype)
     return pl.pallas_call(
         functools.partial(pack_kernel, begin),
-        in_specs=[SMEM] * 3 + [VMEM] * 4,
-        out_specs=[VMEM] * 4,
+        in_specs=[SMEM] + [VMEM] * 4,
+        out_specs=[VMEM] * 3,
         out_shape=[
             jax.ShapeDtypeStruct((parts, blocks, levels, LANES), fields.dtype),
             small,
             small,
-            jax.ShapeDtypeStruct((8, LANES), jnp.float32),
         ],
         compiler_params=PARAMS,
         name="pack",
-    )(core, tile, radius, fields, inner, here, outer)
+    )(core, fields, inner, here, outer)
 
 
 def analyse(tile, core, reach, pieces, above, here, below, kinds):
@@ -430,10 +439,12 @@
     early, fields = lax.optimization_barrier((early, fields))
     early = early.reshape((SIDE, SIDE) + early.shape[1:])
     early = lax.all_to_all(early, both, 0, 0, axis_index_groups=groups[0])
-    here = observe(fields, obs_values[0], obs_precision[0], obs_cell[0], obs_count)
+    here, reach = observe(
+        fields, obs_values[0], obs_precision[0], obs_cell[0], obs_count, tile, radius
+    )
     inner = lax.ppermute(here, "space", swap[0])
     outer = lax.ppermute(here, "space", swap[1])
-    late, above, below, reach = pack(core, tile, radius, fields, parts, EARLY, inner, here, outer)
+    late, above, below = pack(core, fields, parts, EARLY, inner, here, outer)
     late = late.reshape((SIDE, SIDE) + late.shape[1:])
     late, early = lax.optimization_barrier((late, early))
     late = lax.all_to_all(late, both, 0, 0, axis_index_groups=groups[0])

time: 103 us -> 102 us (level)
  no operation moved by 1% of the time
where the time goes in v11:
time: 102 us
  blocking collectives  75.7 us (74%)
  starting transfers between devices  13.8 us (14%)
  Pallas kernels  9.07 us (9%)
  waiting for transfers between devices  3.51 us (3%)
    all_to_all x1, blocking collectives, on_device(): out = join(lax.all_to_all(mixed, 'member', 0, 0), fields.shape)  33.4 us
    all_to_all x1, blocking collectives, on_device(): pieces = lax.all_to_all(pieces, both, 0, 0, axis_index_groups=groups[1])  27.7 us
    all_to_all x1, blocking collectives, on_device(): late = lax.all_to_all(late, both, 0, 0, axis_index_groups=groups[0])  14.5 us
    ppermute x1, starting transfers between devices, on_device(): outer = lax.ppermute(here, 'space', swap[1])  7.57 us
    all_to_all x1, starting transfers between devices, on_device(): early = lax.all_to_all(early, both, 0, 0, axis_index_groups=groups[0])  4.48 us
    ppermute x1, waiting for transfers between devices, on_device(): outer = lax.ppermute(here, 'space', swap[1])  3.51 us
    pallas_call x1, Pallas kernels, analyse(): pl.pallas_call(functools.partial(analyse_kernel, kinds), in_specs=[SMEM]...  3.37 us
    pallas_call x1, Pallas kernels, split(): pl.pallas_call(split_kernel, in_specs=[SMEM, HBM], out_specs=HBM, out_sha...  2.09 us
  transfers between devices with their start and end apart: 3, of which 1 were waited for; matrix products, arithmetic and copies ran while one was open for 0% of the time, Pallas kernels for 2%

profile of v11, /device:TPU:2, one launch (start us, length us, event | category | flops | bytes accessed | tf_op | source)
XLA Modules:
  0.0 102.1 jit_solution(18015642133920771725)
XLA Ops:
  0.0 0.0 copy-start
  0.0 0.0 copy-start.1
  0.0 0.0 copy-start.2
  0.0 0.0 copy-start.3
  0.0 0.0 copy-start.4
  0.0 0.0 copy-start.5
  0.0 2.1 %split.1 = bf16[16,48,4,128]{3,2,1,0:T(4,128)(2,1)} custom-call(s32[1]{0:T(128)} %bitcast.1.core_ref, bf16[4,6,4,8192]{3,2,1,0:T(4,128)(2,1)} %bitcast.18), custom_call_target="tpu_custom_call" | custom-call | tf_op jit(solution)/shard_map/split/pallas_call | solution.py:316
  2.1 4.5 %all-to-all-start = ((bf16[4,4,48,4,128]{4,3,2,1,0:T(4,128)(2,1)}), bf16[4,4,48,4,128]{4,3,2,1,0:T(4,128)(2,1)S(1)}, u32[]{:S(2)}, u32[]{:S(2)}) async-start(bf16[4,4,48,4,128]{4,3,2,1,0:T(4,128)(2,1)} %bitcast.26), calls=%async_computation | async-start | bytes 1572864 | tf_op jit(solution)/shard_map/all_to_all | solution.py:441
  6.6 0.0 copy-done
  6.6 0.0 copy-done.1
  6.6 0.0 copy-done.2
  6.6 0.0 copy-done.3
  6.6 0.0 copy-done.4
  6.6 0.0 copy-done.5
  6.7 1.3 %observe.1 = (f32[8,8,128]{2,1,0:T(8,128)S(1)}, f32[8,128]{1,0:T(8,128)S(1)}) custom-call(bf16[4,6,4,8192]{3,2,1,0:T(4,128)(2,1)S(1)} %bitcast.19, f32[8,128]{1,0:T(8,128)S(1)} %bitcast.23, f32[8,128]{1,0:T(8,128)S(1)} %bitcast.24, s32[8,128]{1,0:T(8,128)S(1)} %bitcast.25, s32[1,8]{1,0:T(1,128)S(1)} %copy-done.4, s32[1]{0:T(128)} %bitcast.tile_ref, ...), custom_call_target="tpu_custom_call" | custom-call | tf_op jit(solution)/shard_map/observe/pallas_call | solution.py:300
  8.0 7.6 %collective-permute-start.1 = (f32[8,8,128]{2,1,0:T(8,128)S(1)}, f32[8,8,128]{2,1,0:T(8,128)S(1)}, u32[]{:S(2)}, u32[]{:S(2)}) collective-permute-start(f32[8,8,128]{2,1,0:T(8,128)S(1)} %get-tuple-element.16.own_ref), channel_id=1, source_target_pairs={{1,2},{3,4},{5,6},{7,8},{9,10},{11,12},{13,14},{2,1},{4,3},{6,5},{... | collective-permute-start | bytes 98312 | tf_op jit(solution)/shard_map/ppermute | solution.py:446
  15.6 1.7 %collective-permute-start = (f32[8,8,128]{2,1,0:T(8,128)S(1)}, f32[8,8,128]{2,1,0:T(8,128)S(1)}, u32[]{:S(2)}, u32[]{:S(2)}) collective-permute-start(f32[8,8,128]{2,1,0:T(8,128)S(1)} %get-tuple-element.16.own_ref), channel_id=1, source_target_pairs={{0,1},{2,3},{4,5},{6,7},{8,9},{10,11},{12,13},{14,15},{1,0},{3,2},... | collective-permute-start | bytes 98312 | tf_op jit(solution)/shard_map/ppermute | solution.py:445
  17.3 3.5 %collective-permute-done.1.outer_ref = f32[8,8,128]{2,1,0:T(8,128)S(1)} collective-permute-done((f32[8,8,128]{2,1,0:T(8,128)S(1)}, f32[8,8,128]{2,1,0:T(8,128)S(1)}, u32[]{:S(2)}, u32[]{:S(2)}) %collective-permute-start.1) | collective-permute-done | bytes 32800 | tf_op jit(solution)/shard_map/ppermute | solution.py:446
  20.8 0.0 collective-permute-done.inner_ref
  20.8 0.3 pack.1
  21.2 0.0 all-to-all-done.early_ref
  21.2 14.5 %all_to_all.20.late_ref = bf16[4,4,57,4,128]{4,3,2,1,0:T(4,128)(2,1)S(1)} all-to-all(bf16[4,4,57,4,128]{4,3,2,1,0:T(4,128)(2,1)S(1)} %bitcast.22), channel_id=1, replica_groups={{0,64,128,192},{16,80,144,208},{32,96,160,224},{48,112,176,240},{1,17,3..., dimensions={0} | all-to-all | bytes 1867776 | tf_op jit(solution)/shard_map/all_to_all | solution.py:450
  35.7 0.6 merge.1
  36.4 27.7 %all_to_all.21 = bf16[4,4,105,4,128]{4,3,2,1,0:T(4,128)(2,1)S(1)} all-to-all(bf16[4,4,105,4,128]{4,3,2,1,0:T(4,128)(2,1)S(1)} %merge.1), channel_id=1, replica_groups={{0,16,32,48},{64,80,96,112},{128,144,160,176},{192,208,224,240},{1,65,1..., dimensions={0} | all-to-all | bytes 3440640 | tf_op jit(solution)/shard_map/all_to_all | solution.py:452
  64.1 3.4 %analyse.1 = bf16[16,96,4,128]{3,2,1,0:T(4,128)(2,1)S(1)} custom-call(s32[1]{0:T(128)} %bitcast.tile_ref, s32[1]{0:T(128)} %bitcast.1.core_ref, f32[8,128]{1,0:T(8,128)S(1)} %get-tuple-element.15.reach_ref, bf16[16,105,4,128]{3,2,1,0:T(4,128)(2,1)S(1)} %bitcast.21, f32[8,8,128]{2,1,0:T(8,128)S(1)} %get-tuple-element.21.above_ref, ...), custom_call_target="tpu_custom_call" | custom-call | tf_op jit(solution)/shard_map/analyse/pallas_call | solution.py:368
  67.5 33.4 %all_to_all.22.x_ref = bf16[16,96,4,128]{3,2,1,0:T(4,128)(2,1)S(1)} all-to-all(bf16[16,96,4,128]{3,2,1,0:T(4,128)(2,1)S(1)} %analyse.1), channel_id=1, replica_groups=mesh['member'=16,'space'=16] {'member'}, dimensions={0} | all-to-all | bytes 3145728 | tf_op jit(solution)/shard_map/all_to_all | solution.py:455
  100.8 1.3 %join.1 = bf16[4,6,4,8192]{3,2,1,0:T(4,128)(2,1)} custom-call(bf16[16,96,4,128]{3,2,1,0:T(4,128)(2,1)S(1)} %all_to_all.22.x_ref), custom_call_target="tpu_custom_call" | custom-call | tf_op jit(solution)/shard_map/join/pallas_call | solution.py:333
Async XLA Ops:
  0.0 6.6 %copy-start = (bf16[4,4,6,1,8192]{4,1,3,2,0:T(4,128)(2,1)S(1)}, bf16[4,4,6,1,8192]{4,1,3,2,0:T(4,128)(2,1)}, u32[]{:S(2)}) copy-start(bf16[4,4,6,1,8192]{4,1,3,2,0:T(4,128)(2,1)} %param.6) | copy-start | bytes 4718596
  0.0 6.6 %copy-start.1 = (f32[1,8,128]{2,1,0:T(8,128)S(1)}, f32[1,8,128]{2,1,0:T(8,128)}, u32[]{:S(2)}) copy-start(f32[1,8,128]{2,1,0:T(8,128)} %param.7) | copy-start | bytes 12292
  0.0 6.6 %copy-start.2 = (f32[1,8,128]{2,1,0:T(8,128)S(1)}, f32[1,8,128]{2,1,0:T(8,128)}, u32[]{:S(2)}) copy-start(f32[1,8,128]{2,1,0:T(8,128)} %param.8) | copy-start | bytes 12292
  0.0 6.6 %copy-start.3 = (s32[1,8,128]{2,1,0:T(8,128)S(1)}, s32[1,8,128]{2,1,0:T(8,128)}, u32[]{:S(2)}) copy-start(s32[1,8,128]{2,1,0:T(8,128)} %param.9) | copy-start | bytes 12292
  0.0 6.6 %copy-start.4 = (s32[1,8]{1,0:T(1,128)S(1)}, s32[1,8]{1,0:T(1,128)}, u32[]{:S(2)}) copy-start(s32[1,8]{1,0:T(1,128)} %count_ref.1) | copy-start | bytes 100
  0.0 6.6 %copy-start.5 = (s32[1,8]{1,0:T(1,128)S(1)}, s32[1,8]{1,0:T(1,128)}, u32[]{:S(2)}) copy-start(s32[1,8]{1,0:T(1,128)} %radius_ref.1) | copy-start | bytes 100
  2.1 19.0 %all-to-all-start = ((bf16[4,4,48,4,128]{4,3,2,1,0:T(4,128)(2,1)}), bf16[4,4,48,4,128]{4,3,2,1,0:T(4,128)(2,1)S(1)}, u32[]{:S(2)}, u32[]{:S(2)}) async-start(bf16[4,4,48,4,128]{4,3,2,1,0:T(4,128)(2,1)} %bitcast.26), calls=%async_computation | async-start | bytes 1572864 | tf_op jit(solution)/shard_map/all_to_all | solution.py:441
  8.0 12.8 %collective-permute-start.1 = (f32[8,8,128]{2,1,0:T(8,128)S(1)}, f32[8,8,128]{2,1,0:T(8,128)S(1)}, u32[]{:S(2)}, u32[]{:S(2)}) collective-permute-start(f32[8,8,128]{2,1,0:T(8,128)S(1)} %get-tuple-element.16.own_ref), channel_id=1, source_target_pairs={{1,2},{3,4},{5,6},{7,8},{9,10},{11,12},{13,14},{2,1},{4,3},{6,5},{... | collective-permute-start | bytes 98312 | tf_op jit(solution)/shard_map/ppermute | solution.py:446
  15.6 5.2 %collective-permute-start = (f32[8,8,128]{2,1,0:T(8,128)S(1)}, f32[8,8,128]{2,1,0:T(8,128)S(1)}, u32[]{:S(2)}, u32[]{:S(2)}) collective-permute-start(f32[8,8,128]{2,1,0:T(8,128)S(1)} %get-tuple-element.16.own_ref), channel_id=1, source_target_pairs={{0,1},{2,3},{4,5},{6,7},{8,9},{10,11},{12,13},{14,15},{1,0},{3,2},... | collective-permute-start | bytes 98312 | tf_op jit(solution)/shard_map/ppermute | solution.py:445

commit v12 on v11

--- a/solution.py
+++ b/solution.py
@@ -188,9 +188,9 @@
 
 
 def analyse_kernel(
-    kinds, tile_ref, core_ref, reach_ref, x_ref, above_ref, own_ref, below_ref, out_ref, mix_ref
+    kinds, where_ref, reach_ref, x_ref, above_ref, own_ref, below_ref, out_ref, mix_ref
 ):
-    tile = tile_ref[0]
+    tile, core = where_ref[0] // 2, where_ref[0] % 2
     tiles = own_ref.shape[0]
     sources, _, levels, slots = x_ref.shape
     own = own_ref.shape[1] - 4
@@ -260,7 +260,7 @@
         == lax.broadcasted_iota(jnp.int32, (wide, members), 1)
     ).astype(jnp.bfloat16)
     device = lax.broadcasted_iota(jnp.int32, (wide, members), 0) // (own * levels)
-    row_member = turned(core_ref[0], device) * own + (
+    row_member = turned(core, device) * own + (
         lax.broadcasted_iota(jnp.int32, (wide, members), 0) // levels % own
     )
     chosen = (
@@ -362,18 +362,18 @@
     )(core, fields, inner, here, outer)
 
 
-def analyse(tile, core, reach, pieces, above, here, below, kinds):
+def analyse(where, reach, pieces, above, here, below, kinds):
     parts, blocks, levels, lanes = pieces.shape
     wide = parts * (here.shape[1] - 4) * levels
     return pl.pallas_call(
         functools.partial(analyse_kernel, kinds),
-        in_specs=[SMEM] * 2 + [VMEM] * 5,
+        in_specs=[SMEM] + [VMEM] * 5,
         out_specs=VMEM,
         out_shape=jax.ShapeDtypeStruct((parts, blocks - 9, levels, lanes), pieces.dtype),
         scratch_shapes=[pltpu.VMEM((wide, wide), jnp.bfloat16)],
         compiler_params=PARAMS,
         name="analyse",
-    )(tile, core, reach, pieces, above, here, below)
+    )(where, reach, pieces, above, here, below)
 
 
 def merge_kernel(early_ref, late_ref, out_ref, sems):
@@ -451,7 +451,7 @@
     pieces = merge(early, late)
     pieces = lax.all_to_all(pieces, both, 0, 0, axis_index_groups=groups[1])
     pieces = pieces.reshape((parts,) + pieces.shape[2:])
-    mixed = analyse(tile, core, reach, pieces, above, here, below, kinds)
+    mixed = analyse(tile * 2 + core, reach, pieces, above, here, below, kinds)
     out = join(lax.all_to_all(mixed, "member", 0, 0), fields.shape)
     return out.reshape(own, kinds, 1, levels, width).transpose(0, 3, 1, 2, 4)
 

time: 102 us -> 103 us (level)
  blocking collectives: 75.7 us -> 47.6 us
  waiting for transfers between devices: 3.51 us -> 26.6 us
  starting transfers between devices: 13.8 us -> 18.6 us
    all_to_all x1 -> x0, blocking collectives: 27.7 us -> none  [on_device(): pieces = lax.all_to_all(pieces, both, 0, 0, axis_index_groups=groups[1])]
    all_to_all x0 -> x1, waiting for transfers between devices: none -> 23.1 us  [on_device(): pieces = lax.all_to_all(pieces, both, 0, 0, axis_index_groups=groups[1])]
    all_to_all x0 -> x1, starting transfers between devices: none -> 4.85 us  [on_device(): pieces = lax.all_to_all(pieces, both, 0, 0, axis_index_groups=groups[1])]
  transfers between devices with their start and end apart: 3 -> 4, of which waited for: 1 -> 2; matrix products, arithmetic and copies ran while one was open for 0% -> 0% of each run, Pallas kernels for 2% -> 2%
where the time goes in v12:
time: 103 us
  blocking collectives  47.6 us (46%)
  waiting for transfers between devices  26.6 us (26%)
  starting transfers between devices  18.6 us (18%)
  Pallas kernels  9.73 us (9%)
    all_to_all x1, blocking collectives, on_device(): out = join(lax.all_to_all(mixed, 'member', 0, 0), fields.shape)  33.1 us
    all_to_all x1, waiting for transfers between devices, on_device(): pieces = lax.all_to_all(pieces, both, 0, 0, axis_index_groups=groups[1])  23.1 us
    all_to_all x1, blocking collectives, on_device(): late = lax.all_to_all(late, both, 0, 0, axis_index_groups=groups[0])  14.5 us
    ppermute x1, starting transfers between devices, on_device(): outer = lax.ppermute(here, 'space', swap[1])  7.57 us
    all_to_all x1, starting transfers between devices, on_device(): pieces = lax.all_to_all(pieces, both, 0, 0, axis_index_groups=groups[1])  4.85 us
    all_to_all x1, starting transfers between devices, on_device(): early = lax.all_to_all(early, both, 0, 0, axis_index_groups=groups[0])  4.48 us
    ppermute x1, waiting for transfers between devices, on_device(): outer = lax.ppermute(here, 'space', swap[1])  3.51 us
    pallas_call x1, Pallas kernels, analyse(): pl.pallas_call(functools.partial(analyse_kernel, kinds), in_specs=[SMEM]...  3.36 us
  transfers between devices with their start and end apart: 4, of which 2 were waited for; matrix products, arithmetic and copies ran while one was open for 0% of the time, Pallas kernels for 2%

profile of v12, /device:TPU:2, one launch (start us, length us, event | category | flops | bytes accessed | tf_op | source)
XLA Modules:
  0.0 102.7 jit_solution(7838343187621219403)
XLA Ops:
  0.0 0.0 copy-start
  0.0 0.0 copy-start.1
  0.0 0.0 copy-start.2
  0.0 0.0 copy-start.3
  0.0 0.0 copy-start.4
  0.0 0.0 copy-start.5
  0.0 2.1 %split.1 = bf16[16,48,4,128]{3,2,1,0:T(4,128)(2,1)} custom-call(s32[1]{0:T(128)} %bitcast.1.core_ref, bf16[4,6,4,8192]{3,2,1,0:T(4,128)(2,1)} %bitcast.18), custom_call_target="tpu_custom_call" | custom-call | tf_op jit(solution)/shard_map/split/pallas_call | solution.py:316
  2.1 4.5 %all-to-all-start = ((bf16[4,4,48,4,128]{4,3,2,1,0:T(4,128)(2,1)}), bf16[4,4,48,4,128]{4,3,2,1,0:T(4,128)(2,1)S(1)}, u32[]{:S(2)}, u32[]{:S(2)}) async-start(bf16[4,4,48,4,128]{4,3,2,1,0:T(4,128)(2,1)} %bitcast.26), calls=%async_computation | async-start | bytes 1572864 | tf_op jit(solution)/shard_map/all_to_all | solution.py:441
  6.6 0.0 copy-done
  6.6 0.0 copy-done.1
  6.6 0.0 copy-done.2
  6.6 0.0 copy-done.3
  6.6 0.0 copy-done.4
  6.6 0.0 copy-done.5
  6.7 1.3 %observe.1 = (f32[8,8,128]{2,1,0:T(8,128)S(1)}, f32[8,128]{1,0:T(8,128)S(1)}) custom-call(bf16[4,6,4,8192]{3,2,1,0:T(4,128)(2,1)S(1)} %bitcast.19, f32[8,128]{1,0:T(8,128)S(1)} %bitcast.23, f32[8,128]{1,0:T(8,128)S(1)} %bitcast.24, s32[8,128]{1,0:T(8,128)S(1)} %bitcast.25, s32[1,8]{1,0:T(1,128)S(1)} %copy-done.4, s32[1]{0:T(128)} %bitcast.tile_ref, ...), custom_call_target="tpu_custom_call" | custom-call | tf_op jit(solution)/shard_map/observe/pallas_call | solution.py:300
  8.0 7.6 %collective-permute-start.1 = (f32[8,8,128]{2,1,0:T(8,128)S(1)}, f32[8,8,128]{2,1,0:T(8,128)S(1)}, u32[]{:S(2)}, u32[]{:S(2)}) collective-permute-start(f32[8,8,128]{2,1,0:T(8,128)S(1)} %get-tuple-element.16.own_ref), channel_id=1, source_target_pairs={{1,2},{3,4},{5,6},{7,8},{9,10},{11,12},{13,14},{2,1},{4,3},{6,5},{... | collective-permute-start | bytes 98312 | tf_op jit(solution)/shard_map/ppermute | solution.py:446
  15.6 1.7 %collective-permute-start = (f32[8,8,128]{2,1,0:T(8,128)S(1)}, f32[8,8,128]{2,1,0:T(8,128)S(1)}, u32[]{:S(2)}, u32[]{:S(2)}) collective-permute-start(f32[8,8,128]{2,1,0:T(8,128)S(1)} %get-tuple-element.16.own_ref), channel_id=1, source_target_pairs={{0,1},{2,3},{4,5},{6,7},{8,9},{10,11},{12,13},{14,15},{1,0},{3,2},... | collective-permute-start | bytes 98312 | tf_op jit(solution)/shard_map/ppermute | solution.py:445
  17.3 3.5 %collective-permute-done.1.outer_ref = f32[8,8,128]{2,1,0:T(8,128)S(1)} collective-permute-done((f32[8,8,128]{2,1,0:T(8,128)S(1)}, f32[8,8,128]{2,1,0:T(8,128)S(1)}, u32[]{:S(2)}, u32[]{:S(2)}) %collective-permute-start.1) | collective-permute-done | bytes 32800 | tf_op jit(solution)/shard_map/ppermute | solution.py:446
  20.8 0.0 collective-permute-done.inner_ref
  20.8 0.3 pack.1
  21.2 0.0 all-to-all-done.early_ref
  21.2 14.5 %all_to_all.20.late_ref = bf16[4,4,57,4,128]{4,3,2,1,0:T(4,128)(2,1)S(1)} all-to-all(bf16[4,4,57,4,128]{4,3,2,1,0:T(4,128)(2,1)S(1)} %bitcast.22), channel_id=1, replica_groups={{0,64,128,192},{16,80,144,208},{32,96,160,224},{48,112,176,240},{1,17,3..., dimensions={0} | all-to-all | bytes 1867776 | tf_op jit(solution)/shard_map/all_to_all | solution.py:450
  35.7 1.3 %merge.1 = bf16[4,4,105,4,128]{4,3,2,1,0:T(4,128)(2,1)} custom-call(bf16[4,4,48,4,128]{4,3,2,1,0:T(4,128)(2,1)S(1)} %all-to-all-done.early_ref, bf16[4,4,57,4,128]{4,3,2,1,0:T(4,128)(2,1)S(1)} %all_to_all.20.late_ref), custom_call_target="tpu_custom_call" | custom-call | tf_op jit(solution)/shard_map/merge/pallas_call | solution.py:401
  37.0 4.9 %all-to-all-start.2 = ((bf16[4,4,105,4,128]{4,3,2,1,0:T(4,128)(2,1)}), bf16[4,4,105,4,128]{4,3,2,1,0:T(4,128)(2,1)S(1)}, u32[]{:S(2)}, u32[]{:S(2)}) async-start(bf16[4,4,105,4,128]{4,3,2,1,0:T(4,128)(2,1)} %merge.1), calls=%async_computation.2 | async-start | bytes 3440640 | tf_op jit(solution)/shard_map/all_to_all | solution.py:452
  41.9 23.1 %all-to-all-done.2 = bf16[4,4,105,4,128]{4,3,2,1,0:T(4,128)(2,1)S(1)} async-done(((bf16[4,4,105,4,128]{4,3,2,1,0:T(4,128)(2,1)}), bf16[4,4,105,4,128]{4,3,2,1,0:T(4,128)(2,1)S(1)}, u32[]{:S(2)}, u32[]{:S(2)}) %all-to-all-start.2) | async-done | bytes 1720352 | tf_op jit(solution)/shard_map/all_to_all | solution.py:452
  65.0 3.4 %analyse.1 = bf16[16,96,4,128]{3,2,1,0:T(4,128)(2,1)S(1)} custom-call(s32[1]{0:T(128)S(6)} %add.9.where_ref, f32[8,128]{1,0:T(8,128)S(1)} %get-tuple-element.15.reach_ref, bf16[16,105,4,128]{3,2,1,0:T(4,128)(2,1)S(1)} %bitcast.21, f32[8,8,128]{2,1,0:T(8,128)S(1)} %get-tuple-element.21.above_ref, f32[8,8,128]{2,1,0:T(8,128)S(1)} %get-tuple-element.16.own_ref, ...), custom_call_target="tpu_custom_call" | custom-call | tf_op jit(solution)/shard_map/analyse/pallas_call | solution.py:368
  68.4 33.1 %all_to_all.21.x_ref = bf16[16,96,4,128]{3,2,1,0:T(4,128)(2,1)S(1)} all-to-all(bf16[16,96,4,128]{3,2,1,0:T(4,128)(2,1)S(1)} %analyse.1), channel_id=1, replica_groups=mesh['member'=16,'space'=16] {'member'}, dimensions={0} | all-to-all | bytes 3145728 | tf_op jit(solution)/shard_map/all_to_all | solution.py:455
  101.4 1.3 %join.1 = bf16[4,6,4,8192]{3,2,1,0:T(4,128)(2,1)} custom-call(bf16[16,96,4,128]{3,2,1,0:T(4,128)(2,1)S(1)} %all_to_all.21.x_ref), custom_call_target="tpu_custom_call" | custom-call | tf_op jit(solution)/shard_map/join/pallas_call | solution.py:333
Async XLA Ops:
  0.0 6.6 %copy-start = (bf16[4,4,6,1,8192]{4,1,3,2,0:T(4,128)(2,1)S(1)}, bf16[4,4,6,1,8192]{4,1,3,2,0:T(4,128)(2,1)}, u32[]{:S(2)}) copy-start(bf16[4,4,6,1,8192]{4,1,3,2,0:T(4,128)(2,1)} %param.6) | copy-start | bytes 4718596
  0.0 6.6 %copy-start.1 = (f32[1,8,128]{2,1,0:T(8,128)S(1)}, f32[1,8,128]{2,1,0:T(8,128)}, u32[]{:S(2)}) copy-start(f32[1,8,128]{2,1,0:T(8,128)} %param.7) | copy-start | bytes 12292
  0.0 6.6 %copy-start.2 = (f32[1,8,128]{2,1,0:T(8,128)S(1)}, f32[1,8,128]{2,1,0:T(8,128)}, u32[]{:S(2)}) copy-start(f32[1,8,128]{2,1,0:T(8,128)} %param.8) | copy-start | bytes 12292
  0.0 6.6 %copy-start.3 = (s32[1,8,128]{2,1,0:T(8,128)S(1)}, s32[1,8,128]{2,1,0:T(8,128)}, u32[]{:S(2)}) copy-start(s32[1,8,128]{2,1,0:T(8,128)} %param.9) | copy-start | bytes 12292
  0.0 6.6 %copy-start.4 = (s32[1,8]{1,0:T(1,128)S(1)}, s32[1,8]{1,0:T(1,128)}, u32[]{:S(2)}) copy-start(s32[1,8]{1,0:T(1,128)} %count_ref.1) | copy-start | bytes 100
  0.0 6.6 %copy-start.5 = (s32[1,8]{1,0:T(1,128)S(1)}, s32[1,8]{1,0:T(1,128)}, u32[]{:S(2)}) copy-start(s32[1,8]{1,0:T(1,128)} %radius_ref.1) | copy-start | bytes 100
  2.1 19.0 %all-to-all-start = ((bf16[4,4,48,4,128]{4,3,2,1,0:T(4,128)(2,1)}), bf16[4,4,48,4,128]{4,3,2,1,0:T(4,128)(2,1)S(1)}, u32[]{:S(2)}, u32[]{:S(2)}) async-start(bf16[4,4,48,4,128]{4,3,2,1,0:T(4,128)(2,1)} %bitcast.26), calls=%async_computation | async-start | bytes 1572864 | tf_op jit(solution)/shard_map/all_to_all | solution.py:441
  8.0 12.8 %collective-permute-start.1 = (f32[8,8,128]{2,1,0:T(8,128)S(1)}, f32[8,8,128]{2,1,0:T(8,128)S(1)}, u32[]{:S(2)}, u32[]{:S(2)}) collective-permute-start(f32[8,8,128]{2,1,0:T(8,128)S(1)} %get-tuple-element.16.own_ref), channel_id=1, source_target_pairs={{1,2},{3,4},{5,6},{7,8},{9,10},{11,12},{13,14},{2,1},{4,3},{6,5},{... | collective-permute-start | bytes 98312 | tf_op jit(solution)/shard_map/ppermute | solution.py:446
  15.6 5.2 %collective-permute-start = (f32[8,8,128]{2,1,0:T(8,128)S(1)}, f32[8,8,128]{2,1,0:T(8,128)S(1)}, u32[]{:S(2)}, u32[]{:S(2)}) collective-permute-start(f32[8,8,128]{2,1,0:T(8,128)S(1)} %get-tuple-element.16.own_ref), channel_id=1, source_target_pairs={{0,1},{2,3},{4,5},{6,7},{8,9},{10,11},{12,13},{14,15},{1,0},{3,2},... | collective-permute-start | bytes 98312 | tf_op jit(solution)/shard_map/ppermute | solution.py:445
  37.0 28.0 %all-to-all-start.2 = ((bf16[4,4,105,4,128]{4,3,2,1,0:T(4,128)(2,1)}), bf16[4,4,105,4,128]{4,3,2,1,0:T(4,128)(2,1)S(1)}, u32[]{:S(2)}, u32[]{:S(2)}) async-start(bf16[4,4,105,4,128]{4,3,2,1,0:T(4,128)(2,1)} %merge.1), calls=%async_computation.2 | async-start | bytes 3440640 | tf_op jit(solution)/shard_map/all_to_all | solution.py:452
